TPU v7x, 32 devices: a whole 2x2x4 slice. The times are simulated.
32 devices in a mesh: node: 8 (over y, x, core), local: 4 (over z).
Axes of the slice: x: 2, y: 2, z: 4, core: 2. Of those that a mesh axis runs over, the one named last changes fastest.
Arguments:
- tokens: bfloat16 [512, 4096], P('local', 'node'), may hold values from -6 to 6
- cotangent: bfloat16 [512, 4096], P('local', 'node'), may hold values from -0.25 to 0.25
- gain: bfloat16 [1, 4096], P(None, 'node'), may hold values from 0.099609375 to 1.8984375
- up_q: bfloat16 [4096, 14336], P('local', 'node'), may hold values from -4 to 4
- up_scale: bfloat16 [32, 14336], P('local', 'node'), may hold values from 0.0078125 to 0.0390625
- down_q: bfloat16 [14336, 4096], P('node', 'local'), may hold values from -4 to 4
- down_scale: bfloat16 [14336, 32], P('node', 'local'), may hold values from 0.005004883 to 0.025024414
Outputs:
- states: bfloat16 [512, 4096], P('local', 'node')
- grad_down: bfloat16 [14336, 4096], P('node', 'local')
All inputs are finite; a program needn't handle non-finite values.
Results may differ from a plain program's by a relative error of at most 0.035.
Values may be sent and summed in bfloat16 or wider, within the bound.
No kernel may reach another device: no remote copies, remote signals or barrier semaphores. Data moves between devices by JAX's collectives and lax.ppermute only.
A program may use at most 128 MiB of HBM per device.

v0:
```python
import jax
import jax.numpy as jnp
from jax import lax
from jax.sharding import PartitionSpec as P

LOOPS = 2


epsilon = 1e-05


def dequant_rows(quanta, scales):
    blocks = scales.shape[0]
    widened = quanta.astype(jnp.float32).reshape(blocks, quanta.shape[0] // blocks, quanta.shape[1])
    return (
        (widened * scales.astype(jnp.float32)[:, None, :])
        .reshape(quanta.shape)
        .astype(jnp.bfloat16)
    )


def dequant_cols(quanta, scales):
    blocks = scales.shape[1]
    widened = quanta.astype(jnp.float32).reshape(quanta.shape[0], blocks, quanta.shape[1] // blocks)
    return (
        (widened * scales.astype(jnp.float32)[:, :, None])
        .reshape(quanta.shape)
        .astype(jnp.bfloat16)
    )


def normalize(values, gains):
    widened = values.astype(jnp.float32)
    meansq = jnp.mean(widened * widened, axis=-1, keepdims=True) + epsilon
    factor = lax.rsqrt(meansq)
    return ((widened * factor * gains).astype(jnp.bfloat16), factor)


def norm_backward(values, factor, gains, upstream):
    widened = values.astype(jnp.float32)
    scaled = upstream * gains
    inner = jnp.mean(scaled * widened, axis=-1, keepdims=True)
    return factor * scaled - widened * factor * factor * factor * inner


def silu_slope(pre):
    sigma = jax.nn.sigmoid(pre)
    return sigma * (1.0 + pre * (1.0 - sigma))


def per_device(tokens, cotangent, gain, up_q, up_scale, down_q, down_scale):
    values, gain_row = (
        lax.all_gather(tokens, "node", axis=1, tiled=True),
        lax.all_gather(gain, "node", axis=1, tiled=True),
    )
    gains = gain_row.astype(jnp.float32)
    up_quanta, up_scales = (
        lax.all_gather(up_q, "local", axis=0, tiled=True),
        lax.all_gather(up_scale, "local", axis=0, tiled=True),
    )
    down_quanta, down_scales = (
        lax.all_gather(down_q, "local", axis=1, tiled=True),
        lax.all_gather(down_scale, "local", axis=1, tiled=True),
    )
    up_weight = dequant_rows(up_quanta, up_scales)
    down_weight = dequant_cols(down_quanta, down_scales)
    saved = []
    for loop_index in range(LOOPS):
        normed, factor = normalize(values, gains)
        pre = jnp.dot(normed, up_weight, preferred_element_type=jnp.float32)
        hidden = jax.nn.silu(pre).astype(jnp.bfloat16)
        partial_out = jnp.dot(hidden, down_weight, preferred_element_type=jnp.float32)
        update = lax.psum(partial_out.astype(jnp.bfloat16), "node").astype(jnp.float32)
        saved.append((values, factor, pre, hidden))
        values = (values.astype(jnp.float32) + update).astype(jnp.bfloat16)
    columns_own = tokens.shape[1]
    offset = lax.axis_index("node") * columns_own
    result = lax.dynamic_slice_in_dim(values, offset, columns_own, 1)
    carried = lax.all_gather(cotangent, "node", axis=1, tiled=True)
    activations = []
    gradients = []
    for loop_index in reversed(range(LOOPS)):
        before, factor, pre, hidden = saved[loop_index]
        activations.append(hidden)
        gradients.append(carried)
        if loop_index > 0:
            slope = lax.dot_general(
                carried, down_weight, (((1,), (1,)), ((), ())), preferred_element_type=jnp.float32
            )
            pre_grad = (slope * silu_slope(pre)).astype(jnp.bfloat16)
            normed_part = lax.dot_general(
                pre_grad, up_weight, (((1,), (1,)), ((), ())), preferred_element_type=jnp.float32
            )
            normed_grad = lax.psum(normed_part.astype(jnp.bfloat16), "node").astype(jnp.float32)
            carried = (
                carried.astype(jnp.float32) + norm_backward(before, factor, gains, normed_grad)
            ).astype(jnp.bfloat16)
    acts_all = jnp.concatenate(activations, axis=0)
    grads_all = jnp.concatenate(gradients, axis=0)
    partial_grad = lax.dot_general(
        acts_all, grads_all, (((0,), (0,)), ((), ())), preferred_element_type=jnp.float32
    )
    grad_down = lax.psum_scatter(
        partial_grad.astype(jnp.bfloat16), "local", scatter_dimension=1, tiled=True
    )
    return (result, grad_down)


def solution(mesh):
    in_specs = (
        P("local", "node"),
        P("local", "node"),
        P(None, "node"),
        P("local", "node"),
        P("local", "node"),
        P("node", "local"),
        P("node", "local"),
    )
    out_specs = (P("local", "node"), P("node", "local"))
    return jax.shard_map(
        per_device, mesh=mesh, in_specs=in_specs, out_specs=out_specs, check_vma=False
    )
```

profile of v0, /device:TPU:2, one launch (start us, length us, event | category | flops | bytes accessed | tf_op | source)
XLA Modules:
  0.0 1023.4 jit_solution(14615437093114911210)
XLA Ops:
  7.2 0.0 all-gather.5.cloned.1.call-start
  7.2 0.7 all-gather.5.cloned.1.call-update
  7.9 0.0 all-gather.7.cloned.1.call-start
  7.9 0.7 all-gather.7.cloned.1.call-update
  8.7 0.0 all-gather.9.cloned.1.call-start
  8.7 0.7 all-gather.9.cloned.1.call-update
  9.4 0.0 all-reduce.4.cloned.1.call-start
  9.5 8.9 all_gather.22
  18.4 13.5 %all_gather.24 = bf16[32,1792]{1,0:T(8,128)(2,1)S(1)} all-gather(bf16[8,1792]{1,0:T(8,128)(2,1)S(1)} %copy-done.5), channel_id=1, replica_groups=mesh['node'=8,'local'=4] {'local'}, dimensions={0}, use_global_device_ids=true | all-gather | bytes 143360 | tf_op jit(solution)/shard_map/all_gather | solution.py:59
  32.0 13.4 %all_gather.26 = bf16[1792,32]{0,1:T(8,128)(2,1)S(1)} all-gather(bf16[1792,8]{0,1:T(8,128)(2,1)S(1)} %copy-done.6), channel_id=1, replica_groups=mesh['node'=8,'local'=4] {'local'}, dimensions={1}, use_global_device_ids=true | all-gather | bytes 143360 | tf_op jit(solution)/shard_map/all_gather | solution.py:63
  45.4 0.2 copy.9
  45.6 0.0 all-gather.5.cloned.1.call-done
  45.6 1.7 fusion.4
  47.3 241.5 %all-gather.7.cloned.1.call-done = bf16[4096,1792]{1,0:T(8,128)(2,1)} async-done(((bf16[1024,1792]{1,0:T(8,128)(2,1)}), bf16[4096,1792]{1,0:T(8,128)(2,1)}) %all-gather.7.cloned.1.call-update) | async-done | bytes 14680080 | tf_op jit(solution)/shard_map/all_gather | solution.py:58
  288.8 14.6 %fusion.1 = bf16[4096,1792]{1,0:T(8,128)(2,1)} fusion(bf16[4096,1792]{1,0:T(8,128)(2,1)} %all-gather.7.cloned.1.call-done, f32[32,1792]{1,0:T(8,128)S(1)} %convert_element_type.79), kind=kLoop, calls=%fused_computation.3 | loop fusion | flops 22020096 | bytes 29589504 | tf_op jit(solution)/shard_map/convert_element_type | solution.py:18
  303.4 237.7 %all-gather.9.cloned.1.call-done = bf16[1792,4096]{1,0:T(8,128)(2,1)} async-done(((bf16[1792,1024]{1,0:T(8,128)(2,1)}), bf16[1792,4096]{1,0:T(8,128)(2,1)}) %all-gather.9.cloned.1.call-update) | async-done | bytes 14680080 | tf_op jit(solution)/shard_map/all_gather | solution.py:62
  541.1 14.0 %mul.132 = f32[1792,32,128]{2,1,0:T(8,128)} broadcast(f32[1792,32]{1,0:T(8,128)S(1)} %copy.9), dimensions={0,1} | broadcast | bytes 29589504 | tf_op jit(solution)/shard_map/mul | solution.py:26
  555.1 0.0 copy-done.1
  555.1 26.2 %fusion = bf16[1792,4096]{1,0:T(8,128)(2,1)S(1)} fusion(f32[224,8,32,128]{3,2,1,0:T(8,128)} %bitcast.29, bf16[1792,4096]{1,0:T(8,128)(2,1)S(1)} %copy-done.1), kind=kLoop, calls=%fused_computation.1 | loop fusion | flops 22020096 | bytes 58720256 | tf_op jit(solution)/shard_map/convert_element_type | solution.py:28
  581.3 12.8 %multiply_convert_fusion.3 = bf16[128,1792]{1,0:T(8,128)(2,1)S(1)} fusion(bf16[4096,1792]{1,0:T(8,128)(2,1)} %fusion.1, bf16[128,4096]{1,0:T(8,128)(2,1)S(1)} %copy-done.4, f32[4096]{0:T(1024)S(1)} %bitcast.30, f32[128]{0:T(128)S(1)} %add_rsqrt_fusion.1), kind=kOutput, calls=%fused_computation.41 | convolution fusion | flops 1882292224 | bytes 16204288 | tf_op jit(solution)/shard_map/dot_general | solution.py:70
  594.0 3.1 convolution_convert_fusion.3
  597.2 0.0 all-reduce.4.cloned.1.call-update
  597.2 0.0 all-gather.11.cloned.1.call-start
  597.2 0.5 all-gather.11.cloned.1.call-update
  597.8 0.2 all-reduce.6.cloned.1.call-start
  598.0 53.2 %all-reduce.4.cloned.1.call-done = bf16[128,4096]{1,0:T(8,128)(2,1)} async-done(((bf16[128,4096]{1,0:T(8,128)(2,1)}), bf16[128,4096]{1,0:T(8,128)(2,1)}) %all-reduce.4.cloned.1.call-update) | async-done | bytes 1048592 | tf_op jit(solution)/shard_map/psum | solution.py:73
  651.2 1.8 multiply_reduce_fusion.1
  653.0 0.0 slice-start.1
  653.1 0.0 slice-start.2
  653.1 0.0 slice-start.3
  653.1 7.6 multiply_convert_fusion.2
  660.7 0.0 slice-done
  660.7 0.0 slice-done.1
  660.7 0.1 slice-done.2
  660.8 0.6 slice-done.3
  661.5 3.1 convolution_convert_fusion.2
  664.6 12.0 %all-gather.11.cloned.1.call-done = bf16[128,4096]{1,0:T(8,128)(2,1)} async-done(((bf16[128,512]{1,0:T(8,128)(2,1)}), bf16[128,4096]{1,0:T(8,128)(2,1)}) %all-gather.11.cloned.1.call-update) | async-done | bytes 1048592 | tf_op jit(solution)/shard_map/all_gather | solution.py:79
  676.5 23.3 %convolution_convert_fusion.1 = bf16[128,4096]{1,0:T(8,128)(2,1)} fusion(bf16[4096,1792]{1,0:T(8,128)(2,1)} %fusion.1, bf16[1792,4096]{1,0:T(8,128)(2,1)} %copy-done, bf16[128,4096]{1,0:T(8,128)(2,1)} %all-gather.11.cloned.1.call-done, f32[128,1792]{1,0:T(8,128)S(1)} %get-tuple-element.7), kind=kOutput, calls=%fused_computation.5 | convolution fusion | flops 3760685056 | bytes 32374784 | tf_op jit(solution)/shard_map/dot_general | solution.py:91
  699.9 0.0 all-reduce.6.cloned.1.call-update
  699.9 0.3 reduce-scatter.2.cloned.1.call-start
  700.2 60.4 %all-reduce.6.cloned.1.call-done = (bf16[128,4096]{1,0:T(8,128)(2,1)}, bf16[128,4096]{1,0:T(8,128)(2,1)}) async-done(((bf16[128,4096]{1,0:T(8,128)(2,1)}, bf16[128,4096]{1,0:T(8,128)(2,1)}), (bf16[128,4096]{1,0:T(8,128)(2,1)}, bf16[128,4096]{1,0:T(8,128)(2,1)})) %all-reduce.6.cloned.1.call-update) | async-done | bytes 2097168 | tf_op jit(solution)/shard_map/psum | solution.py:73
  760.6 1.7 multiply_reduce_fusion
  762.3 0.8 add_convert_fusion
  763.2 7.2 convolution_convert_fusion
  770.4 0.0 reduce-scatter.2.cloned.1.call-update
  770.4 0.2 convert_element_type.88
  770.6 1.6 fusion.28
  772.2 244.3 %reduce-scatter.2.cloned.1.call-done = bf16[1792,1024]{1,0:T(8,128)(2,1)} async-done(((bf16[1792,4096]{1,0:T(8,128)(2,1)}), bf16[1792,1024]{1,0:T(8,128)(2,1)}) %reduce-scatter.2.cloned.1.call-update) | async-done | bytes 3670032 | tf_op jit(solution)/shard_map/reduce_scatter | solution.py:103
  (22 shorter events, 0.1 us)
Async XLA Ops:
  7.2 38.4 %all-gather.5.cloned.1.call-start = ((), (), s32[]{:S(2)}) async-start(), calls=%async_computation.1 | async-start | bytes 1179648 | tf_op jit(solution)/shard_map/all_gather | solution.py:53
  7.9 280.9 %all-gather.7.cloned.1.call-start = ((), (), s32[]{:S(2)}) async-start(), calls=%async_computation.2 | async-start | bytes 18350080 | tf_op jit(solution)/shard_map/all_gather | solution.py:58
  8.6 0.8 copy-start.7
  8.7 9.7 copy-start.5
  8.7 23.3 %copy-start.6 = (bf16[1792,8]{0,1:T(8,128)(2,1)S(1)}, bf16[1792,8]{0,1:T(8,128)(2,1)}, u32[]{:S(2)}) copy-start(bf16[1792,8]{0,1:T(8,128)(2,1)} %param.13) | copy-start | bytes 86020
  8.7 532.4 %all-gather.9.cloned.1.call-start = ((), (), s32[]{:S(2)}) async-start(), calls=%async_computation.3 | async-start | bytes 18350080 | tf_op jit(solution)/shard_map/all_gather | solution.py:62
  9.4 641.8 %all-reduce.4.cloned.1.call-start = ((), (), s32[]{:S(2)}) async-start(), calls=%async_computation.4 | async-start | bytes 2097152 | tf_op jit(solution)/shard_map/psum | solution.py:73
  541.1 14.0 %copy-start.1 = (bf16[1792,4096]{1,0:T(8,128)(2,1)S(1)}, bf16[1792,4096]{1,0:T(8,128)(2,1)}, u32[]{:S(2)}) copy-start(bf16[1792,4096]{1,0:T(8,128)(2,1)} %all-gather.9.cloned.1.call-done) | copy-start | bytes 44040196
  555.1 26.2 %copy-start.4 = (bf16[128,4096]{1,0:T(8,128)(2,1)S(1)}, bf16[128,4096]{1,0:T(8,128)(2,1)}, u32[]{:S(2)}) copy-start(bf16[128,4096]{1,0:T(8,128)(2,1)} %all-gather.5.cloned.1.call-done) | copy-start | bytes 3145732
  581.2 12.8 %copy-start = (bf16[1792,4096]{1,0:T(8,128)(2,1)}, bf16[1792,4096]{1,0:T(8,128)(2,1)S(1)}, u32[]{:S(2)}) copy-start(bf16[1792,4096]{1,0:T(8,128)(2,1)S(1)} %fusion) | copy-start | bytes 44040196
  597.2 79.4 %all-gather.11.cloned.1.call-start = ((), (), s32[]{:S(2)}) async-start(), calls=%async_computation.5 | async-start | bytes 1179648 | tf_op jit(solution)/shard_map/all_gather | solution.py:79
  597.8 162.8 %all-reduce.6.cloned.1.call-start = ((), (), s32[]{:S(2)}) async-start(), calls=%async_computation.7 | async-start | bytes 4194304 | tf_op jit(solution)/shard_map/psum | solution.py:73
  651.2 9.5 slice-start
  653.0 7.7 slice-start.1
  653.1 7.8 slice-start.2
  653.1 8.4 slice-start.3
  699.9 62.4 %copy-start.2 = (bf16[128,4096]{1,0:T(8,128)(2,1)S(1)}, bf16[128,4096]{1,0:T(8,128)(2,1)}, u32[]{:S(2)}) copy-start(bf16[128,4096]{1,0:T(8,128)(2,1)} %all-gather.11.cloned.1.call-done) | copy-start | bytes 3145732
  699.9 316.7 %reduce-scatter.2.cloned.1.call-start = ((), (), s32[]{:S(2)}) async-start(), calls=%async_computation.6 | async-start | bytes 18350080 | tf_op jit(solution)/shard_map/reduce_scatter | solution.py:103
  760.6 1.8 copy-start.3
Sparse Core Ops, SparseCore 0:
  9.9 24.7 all-gather.4
  36.3 252.4 all-gather.6
  290.4 250.6 all-gather.8
  597.3 53.8 all-reduce.3
  652.9 23.5 all-gather.10
  700.0 60.4 all-reduce.5
  770.5 245.9 reduce-scatter.1
where the time goes:
time: 1030 us; the launch traced here: 1020 us
  waiting for transfers between devices  852 us (83%)
  matrix products  57.2 us (6%)
  other arithmetic  48.8 us (5%)
  blocking collectives  35.8 us (3%)
  local copies, waits for them, and re-layouts  15 us (1%)
  between operations  14.3 us (1%)
    reduce_scatter x1, waiting for transfers between devices, per_device(): lax.psum_scatter(partial_grad.astype(jnp.bfloat16), 'local', scatter_dime...  244 us
    all_gather x1, waiting for transfers between devices, per_device(): lax.all_gather(up_q, 'local', axis=0, tiled=True)  241 us
    all_gather x1, waiting for transfers between devices, per_device(): lax.all_gather(down_q, 'local', axis=1, tiled=True)  238 us
    psum x2, waiting for transfers between devices, per_device(): lax.psum(partial_out.astype(jnp.bfloat16), 'node').astype(jnp.float32)  114 us
    convert_element_type x1, other arithmetic, dequant_cols(): return (widened * scales.astype(jnp.float32)[:, :, None]).reshape(quanta....  26.2 us
    dot_general x1, matrix products, per_device(): lax.dot_general(pre_grad, up_weight, (((1,), (1,)), ((), ())), preferred_...  23.3 us
  transfers between devices with their start and end apart: 7, of which 6 were waited for; matrix products, arithmetic and copies ran while one was open for 3% of the time, Pallas kernels for 0%

commit v1 on v0

v1 whole, which is shorter than its diff:
```python
import jax
import jax.numpy as jnp
from jax import lax
from jax.sharding import PartitionSpec as P

LOOPS = 2
epsilon = 1e-05
F32 = jnp.float32
BF16 = jnp.bfloat16


def dequant_rows(quanta, scales):
    blocks = scales.shape[0]
    widened = quanta.astype(F32).reshape(blocks, quanta.shape[0] // blocks, quanta.shape[1])
    return (widened * scales.astype(F32)[:, None, :]).reshape(quanta.shape).astype(BF16)


def dequant_cols(quanta, scales):
    blocks = scales.shape[1]
    widened = quanta.astype(F32).reshape(quanta.shape[0], blocks, quanta.shape[1] // blocks)
    return (widened * scales.astype(F32)[:, :, None]).reshape(quanta.shape).astype(BF16)


def dot(left, right, dims):
    return lax.dot_general(left, right, (dims, ((), ())), preferred_element_type=F32)


def body(n_node, n_local, tokens, cotangent, gain, up_q, up_scale, down_q, down_scale):
    rows, cols = tokens.shape
    halves = n_node // n_local
    features = cols * n_node
    total_rows = rows * n_local

    swap = [
        ((halves * c + j) * n_local + l, (halves * l + j) * n_local + c)
        for c in range(n_local)
        for j in range(halves)
        for l in range(n_local)
    ]

    def exchange(block):
        return lax.ppermute(block, ("node", "local"), swap)

    def gather_node(block):
        parts = lax.all_gather(block, "node", axis=0, tiled=False)
        parts = parts.reshape((n_local, halves) + block.shape)
        return parts.transpose(0, 2, 1, 3).reshape(total_rows, halves * cols)

    def scatter_node(partial):
        parts = partial.reshape(n_local, rows, halves, cols).transpose(0, 2, 1, 3)
        parts = parts.reshape(n_node, rows, cols)
        return lax.psum_scatter(parts, "node", scatter_dimension=0, tiled=False)

    def scatter_local(partial):
        return lax.psum_scatter(partial, "local", scatter_dimension=0, tiled=True)

    def gather_local(block):
        return lax.all_gather(block, "local", axis=0, tiled=True)

    local_index = lax.axis_index("local")
    node_index = lax.axis_index("node")

    def factor_of(values):
        widened = values.astype(F32)
        sums = lax.psum(jnp.sum(widened * widened, axis=-1, keepdims=True), "local")
        return lax.rsqrt(sums / features + epsilon)

    def own_local(column):
        return lax.dynamic_slice_in_dim(column, local_index * rows, rows, 0)

    gains_all = lax.all_gather(gain, "node", axis=1, tiled=True).astype(F32)
    gains = lax.dynamic_slice_in_dim(gains_all, local_index * halves * cols, halves * cols, 1)
    gains_home = lax.dynamic_slice_in_dim(gains, (node_index % halves) * cols, cols, 1)

    x_home = exchange(tokens)
    g_home = exchange(cotangent)
    up_weight = dequant_rows(up_q, up_scale)
    down_weight = dequant_cols(down_q, down_scale)

    x = gather_node(x_home)
    hiddens = []
    for loop_index in range(LOOPS):
        factor = factor_of(x)
        scaled = (x.astype(F32) * gains).astype(BF16)
        raw = dot(scaled, up_weight, ((1,), (0,))).astype(BF16)
        raw = scatter_local(raw).astype(F32)
        pre = (raw * own_local(factor)).astype(BF16)
        if loop_index == 0:
            hidden = gather_local(jax.nn.silu(pre.astype(F32)).astype(BF16))
        else:
            pre = gather_local(pre).astype(F32)
            hidden = jax.nn.silu(pre).astype(BF16)
        hiddens.append(hidden)
        update = dot(hidden, down_weight, ((1,), (0,))).astype(BF16)
        update = scatter_node(update).astype(F32)
        before_home = x_home
        x_home = (x_home.astype(F32) + update).astype(BF16)
        if loop_index < LOOPS - 1:
            x = gather_node(x_home)
    result = exchange(x_home)

    g = gather_node(g_home)
    slope = dot(g, down_weight, ((1,), (1,))).astype(BF16)
    slope = gather_local(scatter_local(slope)).astype(F32)
    sigma = jax.nn.sigmoid(pre)
    pre_grad = slope * sigma * (1.0 + pre * (1.0 - sigma))
    inner = jnp.sum(pre_grad * pre, axis=-1, keepdims=True)
    inner = lax.psum(inner, "node") / (features * factor)
    normed_grad = dot(pre_grad.astype(BF16), up_weight, ((1,), (1,))).astype(BF16)
    normed_grad = scatter_node(normed_grad).astype(F32)
    start = (node_index // halves) * rows
    factor_home = lax.dynamic_slice_in_dim(factor, start, rows, 0)
    inner_home = lax.dynamic_slice_in_dim(inner, start, rows, 0)
    back = factor_home * (normed_grad * gains_home) - before_home.astype(F32) * (
        factor_home * factor_home * factor_home * inner_home
    )
    below = (g_home.astype(F32) + back).astype(BF16)
    below = gather_node(below)
    grad_down = dot(
        jnp.concatenate(hiddens, axis=0), jnp.concatenate([below, g], axis=0), ((0,), (0,))
    ).astype(BF16)
    return (result, grad_down)


def solution(mesh):
    n_node, n_local = mesh.shape["node"], mesh.shape["local"]

    def per_device(*arrays):
        return body(n_node, n_local, *arrays)

    in_specs = (
        P("local", "node"),
        P("local", "node"),
        P(None, "node"),
        P("local", "node"),
        P("local", "node"),
        P("node", "local"),
        P("node", "local"),
    )
    out_specs = (P("local", "node"), P("node", "local"))
    return jax.shard_map(
        per_device, mesh=mesh, in_specs=in_specs, out_specs=out_specs, check_vma=False
    )
```

time: 1030 us -> 523 us (0.51)
  waiting for transfers between devices: 852 us -> 377 us
  other arithmetic: 48.8 us -> 21.9 us
  matrix products: 57.2 us -> 32.3 us
    all_gather x4 -> x7, waiting for transfers between devices: 491 us -> 181 us  [the longest x3 116 us: gather_local(): return lax.all_gather(block, 'local', axis=0, tiled=True)]
    psum x2 -> x0, waiting for transfers between devices: 114 us -> none  [per_device(): lax.psum(partial_out.astype(jnp.bfloat16), 'node').astype(jnp.float32)]
    reduce_scatter x1 -> x6, waiting for transfers between devices: 244 us -> 163 us  [the longest x3 93.3 us: scatter_local(): return lax.psum_scatter(partial, 'local', scatter_dimension=0, tiled=True)]
    psum x0 -> x3, blocking collectives: none -> 33.1 us  [the longest x2 21.8 us: factor_of(): sums = lax.psum(jnp.sum(widened * widened, axis=-1, keepdims=True), 'local')]
    ppermute x0 -> x3, waiting for transfers between devices: none -> 31.9 us  [exchange(): return lax.ppermute(block, ('node', 'local'), swap)]
    all_gather x3 -> x1, blocking collectives: 35.8 us -> 8.04 us  [body(): gains_all = lax.all_gather(gain, 'node', axis=1, tiled=True).astype(F32)]
    convert_element_type x6 -> x8, other arithmetic: 43.4 us -> 16.5 us  [the longest x1 4.55 us: dequant_rows(): (widened * scales.astype(F32)[:, None, :]).reshape(quanta.shape)]
    dot_general x6 -> x7, matrix products: 57.2 us -> 32.3 us  [dot(): lax.dot_general(left, right, (dims, ((), ())), preferred_element_type=F32)]
  transfers between devices with their start and end apart: 7 -> 16, of which waited for: 6 -> 16; matrix products, arithmetic and copies ran while one was open for 3% -> 8% of each run, Pallas kernels for 0% -> 0%
where the time goes in v1:
time: 523 us; the launch traced here: 521 us
  waiting for transfers between devices  377 us (72%)
  blocking collectives  41.1 us (8%)
  matrix products  32.3 us (6%)
  local copies, waits for them, and re-layouts  24.8 us (5%)
  other arithmetic  21.9 us (4%)
  between operations  14.2 us (3%)
  starting transfers between devices  9.99 us (2%)
    all_gather x3, waiting for transfers between devices, gather_local(): return lax.all_gather(block, 'local', axis=0, tiled=True)  116 us
    reduce_scatter x3, waiting for transfers between devices, scatter_local(): return lax.psum_scatter(partial, 'local', scatter_dimension=0, tiled=True)  93.3 us
    reduce_scatter x3, waiting for transfers between devices, scatter_node(): return lax.psum_scatter(parts, 'node', scatter_dimension=0, tiled=False)  69.9 us
    all_gather x4, waiting for transfers between devices, gather_node(): parts = lax.all_gather(block, 'node', axis=0, tiled=False)  65 us
    dot_general x7, matrix products, dot(): lax.dot_general(left, right, (dims, ((), ())), preferred_element_type=F32)  32.3 us
    ppermute x3, waiting for transfers between devices, exchange(): return lax.ppermute(block, ('node', 'local'), swap)  31.9 us
    psum x2, blocking collectives, factor_of(): sums = lax.psum(jnp.sum(widened * widened, axis=-1, keepdims=True), 'local')  21.8 us
    psum x1, blocking collectives, body(): inner = lax.psum(inner, 'node') / (features * factor)  11.3 us
  transfers between devices with their start and end apart: 16, of which 16 were waited for; matrix products, arithmetic and copies ran while one was open for 8% of the time, Pallas kernels for 0%

profile of v1, /device:TPU:2, one launch (start us, length us, event | category | flops | bytes accessed | tf_op | source)
XLA Modules:
  0.0 521.1 jit_solution(7592629978221991102)
XLA Ops:
  7.2 3.5 collective-permute-start
  10.7 10.4 %collective-permute-done = bf16[128,512]{1,0:T(8,128)(2,1)S(1)} collective-permute-done((bf16[128,512]{1,0:T(8,128)(2,1)}, bf16[128,512]{1,0:T(8,128)(2,1)S(1)}, u32[]{:S(2)}, u32[]{:S(2)}) %collective-permute-start) | collective-permute-done | bytes 131104 | tf_op jit(solution)/shard_map/ppermute | solution.py:42
  22.6 8.0 %all_gather.38 = bf16[1,4096]{1,0:T(2,128)(2,1)S(1)} all-gather(bf16[1,512]{1,0:T(2,128)(2,1)} %param.9), channel_id=1, replica_groups=mesh['node'=8,'local'=4] {'node'}, dimensions={1}, use_global_device_ids=true | all-gather | bytes 9216 | tf_op jit(solution)/shard_map/all_gather | solution.py:71
  30.6 4.5 fusion.1
  35.2 10.5 %all-gather.18.cloned.1.call-done = bf16[1024,512]{1,0:T(8,128)(2,1)} async-done(((bf16[128,512]{1,0:T(8,128)(2,1)}), bf16[1024,512]{1,0:T(8,128)(2,1)}) %all-gather.18.cloned.1.call-update) | async-done | bytes 1048592 | tf_op jit(solution)/shard_map/all_gather | solution.py:45
  45.7 2.5 copy.32
  48.6 3.4 convolution_convert_fusion.3
  52.4 11.8 %psum.21 = f32[512,1]{0,1:T(1,128)S(1)} all-reduce(f32[512,1]{0,1:T(1,128)S(1)} %bitcast.96), channel_id=1, replica_groups=mesh['node'=8,'local'=4] {'local'}, use_global_device_ids=true, to_apply=%region_3.4 | all-reduce | flops 512 | bytes 4096 | tf_op jit(solution)/shard_map/psum | solution.py:65
  64.2 27.5 %reduce-scatter.7.cloned.1.call-done = bf16[128,1792]{1,0:T(8,128)(2,1)} async-done(((bf16[512,1792]{1,0:T(8,128)(2,1)}), bf16[128,1792]{1,0:T(8,128)(2,1)}) %reduce-scatter.7.cloned.1.call-update) | async-done | bytes 458768 | tf_op jit(solution)/shard_map/reduce_scatter | solution.py:55
  91.7 2.1 fusion.26
  94.1 2.0 mul.159
  96.2 3.7 fusion
  99.9 34.5 %all-gather.12.cloned.1.call-done = bf16[512,1792]{1,0:T(8,128)(2,1)} async-done(((bf16[128,1792]{1,0:T(8,128)(2,1)}), bf16[512,1792]{1,0:T(8,128)(2,1)}) %all-gather.12.cloned.1.call-update) | async-done | bytes 1835024 | tf_op jit(solution)/shard_map/all_gather | solution.py:58
  134.4 4.7 convolution_convert_fusion.5
  139.9 1.1 copy.35
  141.1 2.2 collective-permute-start.2
  143.3 11.4 %collective-permute-done.2 = bf16[128,512]{1,0:T(8,128)(2,1)S(1)} collective-permute-done((bf16[128,512]{1,0:T(8,128)(2,1)S(1)}, bf16[128,512]{1,0:T(8,128)(2,1)S(1)}, u32[]{:S(2)}, u32[]{:S(2)}) %collective-permute-start.2) | collective-permute-done | bytes 131104 | tf_op jit(solution)/shard_map/ppermute | solution.py:42
  155.5 20.6 %reduce-scatter.9.cloned.1.call-done = bf16[1,128,512]{2,1,0:T(8,128)(2,1)} async-done(((bf16[8,128,512]{2,1,0:T(8,128)(2,1)}), bf16[1,128,512]{2,1,0:T(8,128)(2,1)}) %reduce-scatter.9.cloned.1.call-update) | async-done | bytes 131088 | tf_op jit(solution)/shard_map/reduce_scatter | solution.py:52
  176.1 1.6 fusion.33
  178.0 23.4 %all-gather.22.cloned.1.call-done = bf16[1024,512]{1,0:T(8,128)(2,1)} async-done(((bf16[128,512]{1,0:T(8,128)(2,1)}), bf16[1024,512]{1,0:T(8,128)(2,1)}) %all-gather.22.cloned.1.call-update) | async-done | bytes 1048592 | tf_op jit(solution)/shard_map/all_gather | solution.py:45
  201.4 2.5 copy.39
  204.1 1.0 copy-done.10
  205.1 3.4 fusion.12
  208.5 18.7 %all-gather.20.cloned.1.call-done = bf16[1024,512]{1,0:T(8,128)(2,1)} async-done(((bf16[128,512]{1,0:T(8,128)(2,1)}), bf16[1024,512]{1,0:T(8,128)(2,1)}) %all-gather.20.cloned.1.call-update) | async-done | bytes 1048592 | tf_op jit(solution)/shard_map/all_gather | solution.py:45
  227.2 2.5 copy.36
  230.2 3.4 convolution_convert_fusion.2
  233.6 35.3 %reduce-scatter.15.cloned.1.call-done = bf16[128,1792]{1,0:T(8,128)(2,1)} async-done(((bf16[512,1792]{1,0:T(8,128)(2,1)}), bf16[128,1792]{1,0:T(8,128)(2,1)}) %reduce-scatter.15.cloned.1.call-update) | async-done | bytes 458768 | tf_op jit(solution)/shard_map/reduce_scatter | solution.py:55
  269.4 9.9 %psum.22 = f32[512,1]{0,1:T(1,128)S(1)} all-reduce(f32[512,1]{0,1:T(1,128)S(1)} %bitcast.95), channel_id=1, replica_groups=mesh['node'=8,'local'=4] {'local'}, use_global_device_ids=true, to_apply=%region_8.9 | all-reduce | flops 512 | bytes 4096 | tf_op jit(solution)/shard_map/psum | solution.py:65
  279.3 30.5 %reduce-scatter.11.cloned.1.call-done = bf16[128,1792]{1,0:T(8,128)(2,1)} async-done(((bf16[512,1792]{1,0:T(8,128)(2,1)}), bf16[128,1792]{1,0:T(8,128)(2,1)}) %reduce-scatter.11.cloned.1.call-update) | async-done | bytes 458768 | tf_op jit(solution)/shard_map/reduce_scatter | solution.py:55
  309.9 2.0 multiply_convert_fusion.4
  311.9 40.1 %all-gather.16.cloned.1.call-done = bf16[512,1792]{1,0:T(8,128)(2,1)} async-done(((bf16[128,1792]{1,0:T(8,128)(2,1)}), bf16[512,1792]{1,0:T(8,128)(2,1)}) %all-gather.16.cloned.1.call-update) | async-done | bytes 1835024 | tf_op jit(solution)/shard_map/all_gather | solution.py:58
  352.0 41.7 %all-gather.14.cloned.1.call-done = bf16[512,1792]{1,0:T(8,128)(2,1)} async-done(((bf16[128,1792]{1,0:T(8,128)(2,1)}), bf16[512,1792]{1,0:T(8,128)(2,1)}) %all-gather.14.cloned.1.call-update) | async-done | bytes 1835024 | tf_op jit(solution)/shard_map/all_gather | solution.py:58
  393.7 7.0 %fusion.18 = bf16[512,1024]{1,0:T(8,128)(2,1)} fusion(bf16[1024,1792]{1,0:T(8,128)(2,1)} %fusion.1, bf16[512,1792]{1,0:T(8,128)(2,1)} %all-gather.14.cloned.1.call-done, bf16[512,1792]{1,0:T(8,128)(2,1)} %all-gather.16.cloned.1.call-done), kind=kOutput, calls=%fused_computation.32 | convolution fusion | flops 1889665024 | bytes 8388608 | tf_op jit(solution)/shard_map/dot_general | solution.py:25
  400.7 2.0 reshape.76
  402.7 1.2 copy.41
  404.1 5.1 convolution_convert_fusion.4
  409.3 2.0 reshape.72
  411.2 1.2 copy.38
  412.6 4.8 fusion.8
  417.4 11.3 %psum.23 = f32[512,1]{0,1:T(1,128)S(1)} all-reduce(f32[512,1]{0,1:T(1,128)S(1)} %bitcast.93), channel_id=1, replica_groups=mesh['node'=8,'local'=4] {'node'}, use_global_device_ids=true, to_apply=%region_13.14 | all-reduce | flops 512 | bytes 4096 | tf_op jit(solution)/shard_map/psum | solution.py:108
  428.7 10.2 %reduce-scatter.17.cloned.1.call-done = bf16[1,128,512]{2,1,0:T(8,128)(2,1)} async-done(((bf16[8,128,512]{2,1,0:T(8,128)(2,1)}), bf16[1,128,512]{2,1,0:T(8,128)(2,1)}) %reduce-scatter.17.cloned.1.call-update) | async-done | bytes 131088 | tf_op jit(solution)/shard_map/reduce_scatter | solution.py:52
  439.0 39.1 %reduce-scatter.13.cloned.1.call-done = bf16[1,128,512]{2,1,0:T(8,128)(2,1)} async-done(((bf16[8,128,512]{2,1,0:T(8,128)(2,1)}), bf16[1,128,512]{2,1,0:T(8,128)(2,1)}) %reduce-scatter.13.cloned.1.call-update) | async-done | bytes 131088 | tf_op jit(solution)/shard_map/reduce_scatter | solution.py:52
  478.0 1.8 fusion.31
  479.8 3.4 collective-permute-start.1
  483.2 10.1 %collective-permute-done.1 = bf16[128,512]{1,0:T(8,128)(2,1)S(1)} collective-permute-done((bf16[128,512]{1,0:T(8,128)(2,1)S(1)}, bf16[128,512]{1,0:T(8,128)(2,1)S(1)}, u32[]{:S(2)}, u32[]{:S(2)}) %collective-permute-start.1) | collective-permute-done | bytes 131104 | tf_op jit(solution)/shard_map/ppermute | solution.py:42
  493.3 12.4 %all-gather.24.cloned.1.call-done = bf16[1024,512]{1,0:T(8,128)(2,1)} async-done(((bf16[128,512]{1,0:T(8,128)(2,1)}), bf16[1024,512]{1,0:T(8,128)(2,1)}) %all-gather.24.cloned.1.call-update) | async-done | bytes 1048592 | tf_op jit(solution)/shard_map/all_gather | solution.py:45
  505.8 2.4 copy.42
  508.5 5.5 %convolution_convert_fusion = bf16[1792,1024]{1,0:T(8,128)(2,1)} fusion(bf16[512,1792]{1,0:T(8,128)(2,1)S(1)} %copy-done.8, bf16[512,1792]{1,0:T(8,128)(2,1)S(1)} %copy-done.17, bf16[512,1024]{1,0:T(8,128)(2,1)S(1)} %bitcast.87, bf16[512,1024]{1,0:T(8,128)(2,1)S(1)} %bitcast.90), kind=kOutput, calls=%fused_computation.8 | convolution fusion | flops 3771465728 | bytes 9437184 | tf_op jit(solution)/shard_map/dot_general | solution.py:25
  (82 shorter events, 7.1 us)
Async XLA Ops:
  7.2 38.5 %all-gather.18.cloned.1.call-start = ((), (), s32[]{:S(2)}) async-start(), calls=%async_computation.15 | async-start | bytes 1179648 | tf_op jit(solution)/shard_map/all_gather | solution.py:45
  7.2 13.9 %collective-permute-start = (bf16[128,512]{1,0:T(8,128)(2,1)}, bf16[128,512]{1,0:T(8,128)(2,1)S(1)}, u32[]{:S(2)}, u32[]{:S(2)}) collective-permute-start(bf16[128,512]{1,0:T(8,128)(2,1)} %param.7), channel_id=1, source_target_pairs={{0,0},{1,8},{2,16},{3,24},{4,4},{5,12},{6,20},{7,28},{8,1},{9,9},{... | collective-permute-start | bytes 393224 | tf_op jit(solution)/shard_map/ppermute | solution.py:42
  21.1 0.7 copy-start.12
  21.7 69.9 %reduce-scatter.7.cloned.1.call-start = ((), (), s32[]{:S(2)}) async-start(), calls=%async_computation.6 | async-start | bytes 2293760 | tf_op jit(solution)/shard_map/reduce_scatter | solution.py:55
  45.7 2.9 copy-start.4
  48.6 3.4 copy-start.1
  52.0 41.9 %copy-start.16 = (bf16[1792,8]{0,1:T(8,128)(2,1)S(1)}, bf16[1792,8]{0,1:T(8,128)(2,1)}, u32[]{:S(2)}) copy-start(bf16[1792,8]{0,1:T(8,128)(2,1)} %param.13) | copy-start | bytes 86020
  52.0 82.4 %all-gather.12.cloned.1.call-start = ((), (), s32[]{:S(2)}) async-start(), calls=%async_computation.7 | async-start | bytes 2293760 | tf_op jit(solution)/shard_map/all_gather | solution.py:58
  93.8 82.3 %reduce-scatter.9.cloned.1.call-start = ((), (), s32[]{:S(2)}) async-start(), calls=%async_computation.8 | async-start | bytes 1179648 | tf_op jit(solution)/shard_map/reduce_scatter | solution.py:52
  94.1 2.1 copy-start.2
  139.1 2.0 copy-start.18
  139.1 37.0 %copy-start.13 = (bf16[128,512]{1,0:T(8,128)(2,1)S(1)}, bf16[128,512]{1,0:T(8,128)(2,1)}, u32[]{:S(2)}) copy-start(bf16[128,512]{1,0:T(8,128)(2,1)} %copy-done.12) | copy-start | bytes 393220
  141.1 60.3 %all-gather.22.cloned.1.call-start = ((), (), s32[]{:S(2)}) async-start(), calls=%async_computation.17 | async-start | bytes 1179648 | tf_op jit(solution)/shard_map/all_gather | solution.py:45
  141.1 13.6 %collective-permute-start.2 = (bf16[128,512]{1,0:T(8,128)(2,1)S(1)}, bf16[128,512]{1,0:T(8,128)(2,1)S(1)}, u32[]{:S(2)}, u32[]{:S(2)}) collective-permute-start(bf16[128,512]{1,0:T(8,128)(2,1)S(1)} %copy-done.18), channel_id=1, source_target_pairs={{0,0},{1,8},{2,16},{3,24},{4,4},{5,12},{6,20},{7,28},{8,1},{9,9},{... | collective-permute-start | bytes 393224 | tf_op jit(solution)/shard_map/ppermute | solution.py:42
  154.8 0.7 copy-start.14
  155.5 71.8 %all-gather.20.cloned.1.call-start = ((), (), s32[]{:S(2)}) async-start(), calls=%async_computation.16 | async-start | bytes 1179648 | tf_op jit(solution)/shard_map/all_gather | solution.py:45
  177.8 91.2 %reduce-scatter.15.cloned.1.call-start = ((), (), s32[]{:S(2)}) async-start(), calls=%async_computation.12 | async-start | bytes 2293760 | tf_op jit(solution)/shard_map/reduce_scatter | solution.py:55
  201.4 3.7 copy-start.3
  204.1 1.0 copy-start.10
  208.5 101.4 %reduce-scatter.11.cloned.1.call-start = ((), (), s32[]{:S(2)}) async-start(), calls=%async_computation.9 | async-start | bytes 2293760 | tf_op jit(solution)/shard_map/reduce_scatter | solution.py:55
  227.2 2.9 copy-start.5
  230.2 38.9 %copy-start = (bf16[1024,512]{1,0:T(8,128)(2,1)S(1)}, bf16[1024,512]{1,0:T(8,128)(2,1)}, u32[]{:S(2)}) copy-start(bf16[1024,512]{1,0:T(8,128)(2,1)} %all-gather.20.cloned.1.call-done) | copy-start | bytes 3145732
  233.6 118.4 %all-gather.16.cloned.1.call-start = ((), (), s32[]{:S(2)}) async-start(), calls=%async_computation.13 | async-start | bytes 2293760 | tf_op jit(solution)/shard_map/all_gather | solution.py:58
  269.0 124.7 %all-gather.14.cloned.1.call-start = ((), (), s32[]{:S(2)}) async-start(), calls=%async_computation.10 | async-start | bytes 2293760 | tf_op jit(solution)/shard_map/all_gather | solution.py:58
  311.8 127.1 %reduce-scatter.17.cloned.1.call-start = ((), (), s32[]{:S(2)}) async-start(), calls=%async_computation.14 | async-start | bytes 1179648 | tf_op jit(solution)/shard_map/reduce_scatter | solution.py:52
  400.7 3.4 copy-start.7
  403.9 74.2 %reduce-scatter.13.cloned.1.call-start = ((), (), s32[]{:S(2)}) async-start(), calls=%async_computation.11 | async-start | bytes 1179648 | tf_op jit(solution)/shard_map/reduce_scatter | solution.py:52
  409.3 3.4 copy-start.6
  412.4 65.6 %copy-start.9 = (bf16[128,512]{1,0:T(8,128)(2,1)S(1)}, bf16[128,512]{1,0:T(8,128)(2,1)}, u32[]{:S(2)}) copy-start(bf16[128,512]{1,0:T(8,128)(2,1)} %fusion.33) | copy-start | bytes 393220
  412.4 65.6 %copy-start.15 = (bf16[128,512]{1,0:T(8,128)(2,1)S(1)}, bf16[128,512]{1,0:T(8,128)(2,1)}, u32[]{:S(2)}) copy-start(bf16[128,512]{1,0:T(8,128)(2,1)} %copy-done.14) | copy-start | bytes 393220
  412.5 93.3 %all-gather.24.cloned.1.call-start = ((), (), s32[]{:S(2)}) async-start(), calls=%async_computation.18 | async-start | bytes 1179648 | tf_op jit(solution)/shard_map/all_gather | solution.py:45
  417.4 91.0 %copy-start.8 = (bf16[512,1792]{1,0:T(8,128)(2,1)S(1)}, bf16[512,1792]{1,0:T(8,128)(2,1)}, u32[]{:S(2)}) copy-start(bf16[512,1792]{1,0:T(8,128)(2,1)} %get-tuple-element.3) | copy-start | bytes 5505028
  417.4 91.0 %copy-start.11 = (bf16[64,8,2,512]{3,1,2,0:T(8,128)(2,1)S(1)}, bf16[64,8,2,512]{3,1,2,0:T(8,128)(2,1)}, u32[]{:S(2)}) copy-start(bf16[64,8,2,512]{3,1,2,0:T(8,128)(2,1)} %copy-done.10) | copy-start | bytes 3145732
  479.8 13.5 %collective-permute-start.1 = (bf16[128,512]{1,0:T(8,128)(2,1)S(1)}, bf16[128,512]{1,0:T(8,128)(2,1)S(1)}, u32[]{:S(2)}, u32[]{:S(2)}) collective-permute-start(bf16[128,512]{1,0:T(8,128)(2,1)S(1)} %get-tuple-element.5), channel_id=1, source_target_pairs={{0,0},{1,8},{2,16},{3,24},{4,4},{5,12},{6,20},{7,28},{8,1},{9,9},{... | collective-permute-start | bytes 393224 | tf_op jit(solution)/shard_map/ppermute | solution.py:42
  505.8 2.7 copy-start.17
Sparse Core Ops, SparseCore 0:
  21.9 23.7 all-gather.17
  52.1 39.4 reduce-scatter.6
  93.9 40.4 all-gather.11
  141.2 34.8 reduce-scatter.8
  177.9 23.4 all-gather.21
  203.7 23.4 all-gather.19
  229.5 39.4 reduce-scatter.14
  271.3 38.5 reduce-scatter.10
  311.4 40.5 all-gather.15
  353.4 40.2 all-gather.13
  404.0 34.9 reduce-scatter.16
  442.0 35.9 reduce-scatter.12
  480.5 25.2 all-gather.23

commit v2 on v1

v2 whole, which is shorter than its diff:
```python
import jax
import jax.numpy as jnp
from jax import lax
from jax.sharding import PartitionSpec as P

LOOPS = 2
LANES = 128
PAD = 16
epsilon = 1e-05
F32 = jnp.float32
BF16 = jnp.bfloat16


def dequant_rows(quanta, scales):
    blocks = scales.shape[0]
    widened = quanta.astype(F32).reshape(blocks, quanta.shape[0] // blocks, quanta.shape[1])
    return (widened * scales.astype(F32)[:, None, :]).reshape(quanta.shape).astype(BF16)


def dequant_cols(quanta, scales):
    blocks = scales.shape[1]
    widened = quanta.astype(F32).reshape(quanta.shape[0], blocks, quanta.shape[1] // blocks)
    return (widened * scales.astype(F32)[:, :, None]).reshape(quanta.shape).astype(BF16)


def dot(left, right, dims):
    return lax.dot_general(left, right, (dims, ((), ())), preferred_element_type=F32)


def body(n_node, n_local, tokens, cotangent, gain, up_q, up_scale, down_q, down_scale):
    rows, cols = tokens.shape
    halves = n_node // n_local
    chips = n_local
    features = cols * n_node
    z = lax.axis_index("local")
    node = lax.axis_index("node")
    chip, core = node // halves, node % halves

    swap = [
        ((halves * c + j) * n_local + l, (halves * l + j) * n_local + c)
        for c in range(n_local)
        for j in range(halves)
        for l in range(n_local)
    ]

    def exchange(block):
        return lax.ppermute(block, ("node", "local"), swap)

    def core_swap(block):
        return lax.ppermute(block, "node", [(n, n ^ 1) for n in range(n_node)])

    def chip_swap(block, shift):
        return lax.ppermute(block, "node", [(n, n ^ (2 * shift)) for n in range(n_node)])

    def take(array, index):
        return lax.dynamic_slice_in_dim(array, index * rows, rows, 0)

    def put(array, block, index):
        return lax.dynamic_update_slice_in_dim(array, block, index * rows, 0)

    def gather_chips(block):
        out = jnp.zeros((rows * chips, block.shape[1]), block.dtype)
        out = put(out, block, chip)
        for shift in range(1, chips):
            out = put(out, chip_swap(block, shift), chip ^ shift)
        return out

    def gather_node(block):
        mine = gather_chips(block)
        other = core_swap(mine)
        return jnp.where(
            core == 0,
            jnp.concatenate([mine, other], axis=1),
            jnp.concatenate([other, mine], axis=1),
        )

    def scatter_node(partial, column=None):
        parts = [partial[:, :cols], partial[:, cols:]]
        keep = jnp.where(core == 0, parts[0], parts[1])
        send = jnp.where(core == 0, parts[1], parts[0])
        if column is not None:
            high = column.astype(BF16)
            low = (column - high.astype(F32)).astype(BF16)
            shape = (column.shape[0], LANES // 2)
            tail = [jnp.broadcast_to(high, shape), jnp.broadcast_to(low, shape)]
            keep = jnp.concatenate([keep] + tail, axis=1)
            send = jnp.concatenate([send] + tail, axis=1)
        both = (keep.astype(F32) + core_swap(send).astype(F32)).astype(BF16)
        total = take(both, chip).astype(F32)
        for shift in range(1, chips):
            total = total + chip_swap(take(both, chip ^ shift), shift).astype(F32)
        if column is None:
            return total
        return total[:, :cols], total[:, cols : cols + 1] + total[:, -1:]

    def scatter_local(partial):
        right = left = None
        for step in range(1, n_local):
            send_right = take(partial, jnp.minimum(z + n_local - step, n_local - 1))
            send_left = take(partial, jnp.maximum(z - n_local + step, 0))
            if step > 1:
                send_right = (send_right.astype(F32) + right.astype(F32)).astype(BF16)
                send_left = (send_left.astype(F32) + left.astype(F32)).astype(BF16)
            right = lax.ppermute(send_right, "local", [(s, s + 1) for s in range(step)])
            left = lax.ppermute(
                send_left, "local", [(n_local - 1 - s, n_local - 2 - s) for s in range(step)]
            )
        return take(partial, z).astype(F32) + right.astype(F32) + left.astype(F32)

    def gather_local(block):
        right, left = [block], [block]
        for step in range(1, n_local):
            right.append(
                lax.ppermute(right[-1], "local", [(s, s + 1) for s in range(step - 1, n_local - 1)])
            )
            left.append(
                lax.ppermute(
                    left[-1],
                    "local",
                    [(n_local - 1 - s, n_local - 2 - s) for s in range(step - 1, n_local - 1)],
                )
            )
        out = jnp.zeros((rows * n_local, block.shape[1]), block.dtype)
        out = put(out, block, z)
        for ahead in range(1, n_local):
            behind = n_local - ahead
            piece = jnp.where(z >= behind, right[behind], left[ahead])
            out = put(out, piece, (z + ahead) % n_local)
        return out

    def factor_of(values):
        widened = values.astype(F32)
        own = jnp.sum(widened * widened, axis=-1).reshape(n_local, rows)
        sums = own
        for shift in range(1, n_local):
            sums = sums + lax.ppermute(
                own, "local", [(s, (s + shift) % n_local) for s in range(n_local)]
            )
        return lax.rsqrt(sums.reshape(n_local * rows, 1) / features + epsilon)

    first = exchange(
        jnp.concatenate([tokens, jnp.broadcast_to(gain, (PAD, cols))], axis=0)
    )
    x_home, gains_home = first[:rows], first[rows : rows + 1]
    g_home = exchange(cotangent)
    up_weight = dequant_rows(up_q, up_scale)
    down_weight = dequant_cols(down_q, down_scale)

    gains_other = core_swap(first[rows:])[:1]
    gains = jnp.where(
        core == 0,
        jnp.concatenate([gains_home, gains_other], axis=1),
        jnp.concatenate([gains_other, gains_home], axis=1),
    ).astype(F32)
    gains_home = gains_home.astype(F32)
    x = gather_node(x_home)
    hiddens = []
    for loop_index in range(LOOPS):
        factor = factor_of(x)
        scaled = (x.astype(F32) * gains).astype(BF16)
        raw = dot(scaled, up_weight, ((1,), (0,))).astype(BF16)
        pre = scatter_local(raw) * take(factor, z)
        if loop_index == 0:
            hidden = gather_local(jax.nn.silu(pre).astype(BF16))
        else:
            pre = gather_local(pre.astype(BF16)).astype(F32)
            hidden = jax.nn.silu(pre).astype(BF16)
        hiddens.append(hidden)
        update = dot(hidden, down_weight, ((1,), (0,))).astype(BF16)
        update = scatter_node(update)
        before_home = x_home
        x_home = (x_home.astype(F32) + update).astype(BF16)
        if loop_index < LOOPS - 1:
            x = gather_node(x_home)
    result = exchange(x_home)

    g = gather_node(g_home)
    slope = dot(g, down_weight, ((1,), (1,))).astype(BF16)
    slope = gather_local(scatter_local(slope).astype(BF16)).astype(F32)
    sigma = jax.nn.sigmoid(pre)
    pre_grad = slope * sigma * (1.0 + pre * (1.0 - sigma))
    inner = jnp.sum(pre_grad * pre, axis=-1, keepdims=True) / (features * factor)
    normed_grad = dot(pre_grad.astype(BF16), up_weight, ((1,), (1,))).astype(BF16)
    normed_grad, inner_home = scatter_node(normed_grad, inner)
    factor_home = take(factor, chip)
    back = factor_home * (normed_grad * gains_home) - before_home.astype(F32) * (
        factor_home * factor_home * factor_home * inner_home
    )
    below = gather_node((g_home.astype(F32) + back).astype(BF16))
    grad_down = dot(
        jnp.concatenate(hiddens, axis=0), jnp.concatenate([below, g], axis=0), ((0,), (0,))
    ).astype(BF16)
    return (result, grad_down)


def solution(mesh):
    n_node, n_local = mesh.shape["node"], mesh.shape["local"]

    def per_device(*arrays):
        return body(n_node, n_local, *arrays)

    in_specs = (
        P("local", "node"),
        P("local", "node"),
        P(None, "node"),
        P("local", "node"),
        P("local", "node"),
        P("node", "local"),
        P("node", "local"),
    )
    out_specs = (P("local", "node"), P("node", "local"))
    return jax.shard_map(
        per_device, mesh=mesh, in_specs=in_specs, out_specs=out_specs, check_vma=False
    )
```

time: 523 us -> 364 us (0.70)
  waiting for transfers between devices: 377 us -> 160 us
  starting transfers between devices: 9.99 us -> 136 us
  blocking collectives: 41.1 us -> 0 us
  local copies, waits for them, and re-layouts: 24.8 us -> 8.16 us
  between operations: 14.2 us -> 1.87 us
  other arithmetic: 21.9 us -> 33.9 us
  matrix products: 32.3 us -> 22.4 us
    all_gather x7 -> x0, waiting for transfers between devices: 181 us -> none  [the longest x3 116 us: gather_local(): return lax.all_gather(block, 'local', axis=0, tiled=True)]
    reduce_scatter x6 -> x0, waiting for transfers between devices: 163 us -> none  [the longest x3 93.3 us: scatter_local(): return lax.psum_scatter(partial, 'local', scatter_dimension=0, tiled=True)]
    ppermute x0 -> x71, waiting for transfers between devices: none -> 131 us  [the longest x9 40.1 us: gather_local(): lax.ppermute(left[-1], 'local', [(n_local - 1 - s, n_local - 2 - s) for s...]
    ppermute x0 -> x71, starting transfers between devices: none -> 127 us  [the longest x9 40.1 us: scatter_local(): right = lax.ppermute(send_right, 'local', [(s, s + 1) for s in range(step)])]
    psum x3 -> x0, blocking collectives: 33.1 us -> none  [the longest x2 21.8 us: factor_of(): sums = lax.psum(jnp.sum(widened * widened, axis=-1, keepdims=True), 'local')]
    dot_general x7, matrix products: 32.3 us -> 22.4 us  [dot(): lax.dot_general(left, right, (dims, ((), ())), preferred_element_type=F32)]
    reshape x5 -> x0, local copies, waits for them, and re-layouts: 9.64 us -> none  [the longest x2 4.89 us: gather_node(): parts = parts.reshape((n_local, halves) + block.shape)]
    dynamic_update_slice x0 -> x14, other arithmetic: none -> 9.3 us  [put(): return lax.dynamic_update_slice_in_dim(array, block, index * rows, 0)]
  transfers between devices with their start and end apart: 16 -> 74, of which waited for: 16 -> 38; matrix products, arithmetic and copies ran while one was open for 8% -> 9% of each run, Pallas kernels for 0% -> 0%
where the time goes in v2:
time: 364 us; the launch traced here: 362 us
  waiting for transfers between devices  160 us (44%)
  starting transfers between devices  136 us (37%)
  other arithmetic  33.9 us (9%)
  matrix products  22.4 us (6%)
  local copies, waits for them, and re-layouts  8.16 us (2%)
    ppermute x9, waiting for transfers between devices, gather_local(): lax.ppermute(left[-1], 'local', [(n_local - 1 - s, n_local - 2 - s) for s...  40.1 us
    ppermute x9, starting transfers between devices, scatter_local(): right = lax.ppermute(send_right, 'local', [(s, s + 1) for s in range(step)])  40.1 us
    ppermute x9, waiting for transfers between devices, scatter_local(): right = lax.ppermute(send_right, 'local', [(s, s + 1) for s in range(step)])  34.5 us
    ppermute x21, waiting for transfers between devices, chip_swap(): lax.ppermute(block, 'node', [(n, n ^ 2 * shift) for n in range(n_node)])  32.9 us
    ppermute x3, waiting for transfers between devices, exchange(): return lax.ppermute(block, ('node', 'local'), swap)  29 us
    ppermute x6, starting transfers between devices, factor_of(): lax.ppermute(own, 'local', [(s, (s + shift) % n_local) for s in range(n_l...  24.5 us
    ppermute x21, starting transfers between devices, chip_swap(): lax.ppermute(block, 'node', [(n, n ^ 2 * shift) for n in range(n_node)])  23.8 us
    dot_general x7, matrix products, dot(): lax.dot_general(left, right, (dims, ((), ())), preferred_element_type=F32)  22.4 us
  transfers between devices with their start and end apart: 74, of which 38 were waited for; matrix products, arithmetic and copies ran while one was open for 9% of the time, Pallas kernels for 0%

profile of v2, /device:TPU:2, one launch (start us, length us, event | category | flops | bytes accessed | tf_op | source)
XLA Modules:
  0.0 362.3 jit_solution(17828697640597023348)
XLA Ops:
  2.3 3.5 collective-permute-start
  5.8 11.2 %collective-permute-done = bf16[144,512]{1,0:T(8,128)(2,1)S(1)} collective-permute-done((bf16[144,512]{1,0:T(8,128)(2,1)S(1)}, bf16[144,512]{1,0:T(8,128)(2,1)S(1)}, u32[]{:S(2)}, u32[]{:S(2)}) %collective-permute-start) | collective-permute-done | bytes 147488 | tf_op jit(solution)/shard_map/ppermute | solution.py:47
  17.2 3.4 collective-permute-start.3
  20.6 2.4 collective-permute-done.1
  24.6 4.5 %fusion.1 = bf16[1024,1792]{1,0:T(8,128)(2,1)} fusion(bf16[1024,1792]{1,0:T(8,128)(2,1)} %param.10, f32[8,1792]{1,0:T(8,128)S(1)} %convert_element_type.332), kind=kLoop, calls=%fused_computation.3 | loop fusion | flops 5505024 | bytes 7397376 | tf_op jit(solution)/shard_map/convert_element_type | solution.py:17
  30.5 4.1 %convolution_convert_fusion.3 = bf16[512,1792]{1,0:T(8,128)(2,1)S(1)} fusion(bf16[1024,1792]{1,0:T(8,128)(2,1)} %fusion.1, f32[1024]{0:T(1024)S(1)} %fusion.36, bf16[512,512]{1,0:T(8,128)(2,1)S(1)} %collective-permute-done.4, bf16[512,512]{1,0:T(8,128)(2,1)S(1)} %constant_dynamic-update-slice_fusion.15, pred[]{:T(512)S(6)} %eq.24), kind=kOutput, calls=%fused_computation.21 | convolution fusion | flops 1886257152 | bytes 6557697 | tf_op jit(solution)/shard_map/dot_general | solution.py:27
  35.7 3.1 collective-permute-start.6
  40.2 8.4 %collective-permute-done.6 = bf16[128,1792]{1,0:T(8,128)(2,1)} collective-permute-done((bf16[128,1792]{1,0:T(8,128)(2,1)}, bf16[128,1792]{1,0:T(8,128)(2,1)}, u32[]{:S(2)}, u32[]{:S(2)}) %collective-permute-start.6) | collective-permute-done | bytes 458784 | tf_op jit(solution)/shard_map/ppermute | solution.py:104
  50.4 5.1 %collective-permute-start.7 = (bf16[128,1792]{1,0:T(8,128)(2,1)}, bf16[128,1792]{1,0:T(8,128)(2,1)}, u32[]{:S(2)}, u32[]{:S(2)}) collective-permute-start(bf16[128,1792]{1,0:T(8,128)(2,1)} %add_convert_fusion.15), channel_id=1, source_target_pairs={{0,1},{1,2},{4,5},{5,6},{8,9},{9,10},{12,13},{13,14},{16,17},{17,1... | collective-permute-start | bytes 1376264 | tf_op jit(solution)/shard_map/ppermute | solution.py:104
  55.6 9.0 %collective-permute-done.7 = bf16[128,1792]{1,0:T(8,128)(2,1)} collective-permute-done((bf16[128,1792]{1,0:T(8,128)(2,1)}, bf16[128,1792]{1,0:T(8,128)(2,1)}, u32[]{:S(2)}, u32[]{:S(2)}) %collective-permute-start.7) | collective-permute-done | bytes 458784 | tf_op jit(solution)/shard_map/ppermute | solution.py:104
  68.3 5.0 %collective-permute-start.8 = (bf16[128,1792]{1,0:T(8,128)(2,1)}, bf16[128,1792]{1,0:T(8,128)(2,1)}, u32[]{:S(2)}, u32[]{:S(2)}) collective-permute-start(bf16[128,1792]{1,0:T(8,128)(2,1)} %get-tuple-element.24), channel_id=1, source_target_pairs={{0,1},{1,2},{2,3},{4,5},{5,6},{6,7},{8,9},{9,10},{10,11},{12,13},{... | collective-permute-start | bytes 1376264 | tf_op jit(solution)/shard_map/ppermute | solution.py:104
  76.9 12.2 %collective-permute-start.14 = (f32[4,128]{1,0:T(4,128)S(1)}, f32[4,128]{1,0:T(4,128)S(1)}, u32[]{:S(2)}, u32[]{:S(2)}) collective-permute-start(f32[4,128]{1,0:T(4,128)S(1)} %bitcast.35), channel_id=1, source_target_pairs={{0,3},{1,0},{2,1},{3,2},{4,7},{5,4},{6,5},{7,6},{8,11},{9,8},{10,9... | collective-permute-start | bytes 6152 | tf_op jit(solution)/shard_map/ppermute | solution.py:136
  90.4 4.8 %collective-permute-done.14 = f32[4,128]{1,0:T(4,128)S(1)} collective-permute-done((f32[4,128]{1,0:T(4,128)S(1)}, f32[4,128]{1,0:T(4,128)S(1)}, u32[]{:S(2)}, u32[]{:S(2)}) %collective-permute-start.14) | collective-permute-done | bytes 2080 | tf_op jit(solution)/shard_map/ppermute | solution.py:136
  96.9 2.4 constant_dynamic-update-slice_fusion.14
  99.2 2.5 collective-permute-start.15
  101.7 3.7 %collective-permute-start.49 = (bf16[128,512]{1,0:T(8,128)(2,1)S(1)}, bf16[128,512]{1,0:T(8,128)(2,1)S(1)}, u32[]{:S(2)}, u32[]{:S(2)}) collective-permute-start(bf16[128,512]{1,0:T(8,128)(2,1)S(1)} %copy-done.17), channel_id=1, source_target_pairs={{0,0},{1,8},{2,16},{3,24},{4,4},{5,12},{6,20},{7,28},{8,1},{9,9},{... | collective-permute-start | bytes 393224 | tf_op jit(solution)/shard_map/ppermute | solution.py:47
  105.4 6.1 %collective-permute-done.49 = bf16[128,512]{1,0:T(8,128)(2,1)S(1)} collective-permute-done((bf16[128,512]{1,0:T(8,128)(2,1)S(1)}, bf16[128,512]{1,0:T(8,128)(2,1)S(1)}, u32[]{:S(2)}, u32[]{:S(2)}) %collective-permute-start.49) | collective-permute-done | bytes 131104 | tf_op jit(solution)/shard_map/ppermute | solution.py:47
  111.7 3.1 collective-permute-start.51
  120.7 6.1 %collective-permute-done.18 = bf16[128,1792]{1,0:T(8,128)(2,1)S(1)} collective-permute-done((bf16[128,1792]{1,0:T(8,128)(2,1)}, bf16[128,1792]{1,0:T(8,128)(2,1)S(1)}, u32[]{:S(2)}, u32[]{:S(2)}) %collective-permute-start.18) | collective-permute-done | bytes 458784 | tf_op jit(solution)/shard_map/ppermute | solution.py:117
  131.6 3.8 %fusion = bf16[1792,1024]{1,0:T(8,128)(2,1)} fusion(f32[224,8,8,128]{3,2,1,0:T(8,128)S(1)} %bitcast.30, bf16[1792,1024]{1,0:T(8,128)(2,1)S(1)} %copy-done), kind=kLoop, calls=%fused_computation.1 | loop fusion | flops 5505024 | bytes 14680064 | tf_op jit(solution)/shard_map/convert_element_type | solution.py:23
  137.1 4.3 %collective-permute-done.19 = bf16[128,1792]{1,0:T(8,128)(2,1)} collective-permute-done((bf16[128,1792]{1,0:T(8,128)(2,1)S(1)}, bf16[128,1792]{1,0:T(8,128)(2,1)}, u32[]{:S(2)}, u32[]{:S(2)}) %collective-permute-start.19) | collective-permute-done | bytes 458784 | tf_op jit(solution)/shard_map/ppermute | solution.py:117
  144.1 8.0 %collective-permute-done.20 = bf16[128,1792]{1,0:T(8,128)(2,1)S(1)} collective-permute-done((bf16[128,1792]{1,0:T(8,128)(2,1)}, bf16[128,1792]{1,0:T(8,128)(2,1)S(1)}, u32[]{:S(2)}, u32[]{:S(2)}) %collective-permute-start.20) | collective-permute-done | bytes 458784 | tf_op jit(solution)/shard_map/ppermute | solution.py:117
  162.8 3.1 collective-permute-done.24
  168.8 4.7 %collective-permute-start.55 = (bf16[128,1792]{1,0:T(8,128)(2,1)S(1)}, bf16[128,1792]{1,0:T(8,128)(2,1)S(1)}, u32[]{:S(2)}, u32[]{:S(2)}) collective-permute-start(bf16[128,1792]{1,0:T(8,128)(2,1)S(1)} %add_convert_fusion.7), channel_id=1, source_target_pairs={{0,1},{1,2},{4,5},{5,6},{8,9},{9,10},{12,13},{13,14},{16,17},{17,1... | collective-permute-start | bytes 1376264 | tf_op jit(solution)/shard_map/ppermute | solution.py:104
  175.1 6.2 %collective-permute-done.26 = bf16[128,512]{1,0:T(8,128)(2,1)S(1)} collective-permute-done((bf16[128,512]{1,0:T(8,128)(2,1)S(1)}, bf16[128,512]{1,0:T(8,128)(2,1)S(1)}, u32[]{:S(2)}, u32[]{:S(2)}) %collective-permute-start.26) | collective-permute-done | bytes 131104 | tf_op jit(solution)/shard_map/ppermute | solution.py:53
  184.1 5.0 %collective-permute-start.56 = (bf16[128,1792]{1,0:T(8,128)(2,1)S(1)}, bf16[128,1792]{1,0:T(8,128)(2,1)S(1)}, u32[]{:S(2)}, u32[]{:S(2)}) collective-permute-start(bf16[128,1792]{1,0:T(8,128)(2,1)S(1)} %get-tuple-element.16), channel_id=1, source_target_pairs={{0,1},{1,2},{2,3},{4,5},{5,6},{6,7},{8,9},{9,10},{10,11},{12,13},{... | collective-permute-start | bytes 1376264 | tf_op jit(solution)/shard_map/ppermute | solution.py:104
  191.3 4.6 %collective-permute-start.29 = (bf16[128,1792]{1,0:T(8,128)(2,1)S(1)}, bf16[128,1792]{1,0:T(8,128)(2,1)S(1)}, u32[]{:S(2)}, u32[]{:S(2)}) collective-permute-start(bf16[128,1792]{1,0:T(8,128)(2,1)S(1)} %get-tuple-element.22), channel_id=1, source_target_pairs={{0,1},{4,5},{8,9},{12,13},{16,17},{20,21},{24,25},{28,29}} | collective-permute-start | bytes 1376264 | tf_op jit(solution)/shard_map/ppermute | solution.py:104
  198.0 9.7 %collective-permute-done.29 = bf16[128,1792]{1,0:T(8,128)(2,1)S(1)} collective-permute-done((bf16[128,1792]{1,0:T(8,128)(2,1)S(1)}, bf16[128,1792]{1,0:T(8,128)(2,1)S(1)}, u32[]{:S(2)}, u32[]{:S(2)}) %collective-permute-start.29) | collective-permute-done | bytes 458784 | tf_op jit(solution)/shard_map/ppermute | solution.py:104
  207.8 4.4 %collective-permute-start.30 = (bf16[128,1792]{1,0:T(8,128)(2,1)S(1)}, bf16[128,1792]{1,0:T(8,128)(2,1)S(1)}, u32[]{:S(2)}, u32[]{:S(2)}) collective-permute-start(bf16[128,1792]{1,0:T(8,128)(2,1)S(1)} %add_convert_fusion.11), channel_id=1, source_target_pairs={{0,1},{1,2},{4,5},{5,6},{8,9},{9,10},{12,13},{13,14},{16,17},{17,1... | collective-permute-start | bytes 1376264 | tf_op jit(solution)/shard_map/ppermute | solution.py:104
  218.0 5.1 %collective-permute-done.30 = bf16[128,1792]{1,0:T(8,128)(2,1)S(1)} collective-permute-done((bf16[128,1792]{1,0:T(8,128)(2,1)S(1)}, bf16[128,1792]{1,0:T(8,128)(2,1)S(1)}, u32[]{:S(2)}, u32[]{:S(2)}) %collective-permute-start.30) | collective-permute-done | bytes 458784 | tf_op jit(solution)/shard_map/ppermute | solution.py:104
  224.1 5.8 %collective-permute-done.60 = bf16[128,1792]{1,0:T(8,128)(2,1)S(1)} collective-permute-done((bf16[128,1792]{1,0:T(8,128)(2,1)S(1)}, bf16[128,1792]{1,0:T(8,128)(2,1)S(1)}, u32[]{:S(2)}, u32[]{:S(2)}) %collective-permute-start.60) | collective-permute-done | bytes 458784 | tf_op jit(solution)/shard_map/ppermute | solution.py:114
  231.8 6.6 %collective-permute-start.31 = (bf16[128,1792]{1,0:T(8,128)(2,1)S(1)}, bf16[128,1792]{1,0:T(8,128)(2,1)S(1)}, u32[]{:S(2)}, u32[]{:S(2)}) collective-permute-start(bf16[128,1792]{1,0:T(8,128)(2,1)S(1)} %get-tuple-element.20), channel_id=1, source_target_pairs={{0,1},{1,2},{2,3},{4,5},{5,6},{6,7},{8,9},{9,10},{10,11},{12,13},{... | collective-permute-start | bytes 1376264 | tf_op jit(solution)/shard_map/ppermute | solution.py:104
  240.2 4.9 %collective-permute-start.37 = (f32[4,128]{1,0:T(4,128)S(1)}, f32[4,128]{1,0:T(4,128)S(1)}, u32[]{:S(2)}, u32[]{:S(2)}) collective-permute-start(f32[4,128]{1,0:T(4,128)S(1)} %bitcast.32), channel_id=1, source_target_pairs={{0,3},{1,0},{2,1},{3,2},{4,7},{5,4},{6,5},{7,6},{8,11},{9,8},{10,9... | collective-permute-start | bytes 6152 | tf_op jit(solution)/shard_map/ppermute | solution.py:136
  247.9 3.8 %collective-permute-start.35 = (f32[4,128]{1,0:T(4,128)S(1)}, f32[4,128]{1,0:T(4,128)S(1)}, u32[]{:S(2)}, u32[]{:S(2)}) collective-permute-start(f32[4,128]{1,0:T(4,128)S(1)} %bitcast.34), channel_id=1, source_target_pairs={{0,1},{1,2},{2,3},{3,0},{4,5},{5,6},{6,7},{7,4},{8,9},{9,10},{10,1... | collective-permute-start | bytes 6152 | tf_op jit(solution)/shard_map/ppermute | solution.py:136
  251.7 2.3 collective-permute-done.37
  254.7 3.5 collective-permute-done.36
  260.0 4.6 %collective-permute-start.38 = (bf16[128,1792]{1,0:T(8,128)(2,1)S(1)}, bf16[128,1792]{1,0:T(8,128)(2,1)S(1)}, u32[]{:S(2)}, u32[]{:S(2)}) collective-permute-start(bf16[128,1792]{1,0:T(8,128)(2,1)S(1)} %get-tuple-element.9), channel_id=1, source_target_pairs={{0,1},{1,2},{2,3},{4,5},{5,6},{6,7},{8,9},{9,10},{10,11},{12,13},{... | collective-permute-start | bytes 1376264 | tf_op jit(solution)/shard_map/ppermute | solution.py:114
  266.8 4.4 %collective-permute-done.38 = bf16[128,1792]{1,0:T(8,128)(2,1)S(1)} collective-permute-done((bf16[128,1792]{1,0:T(8,128)(2,1)S(1)}, bf16[128,1792]{1,0:T(8,128)(2,1)S(1)}, u32[]{:S(2)}, u32[]{:S(2)}) %collective-permute-start.38) | collective-permute-done | bytes 458784 | tf_op jit(solution)/shard_map/ppermute | solution.py:114
  273.5 5.9 %collective-permute-done.41 = bf16[128,1792]{1,0:T(8,128)(2,1)S(1)} collective-permute-done((bf16[128,1792]{1,0:T(8,128)(2,1)S(1)}, bf16[128,1792]{1,0:T(8,128)(2,1)S(1)}, u32[]{:S(2)}, u32[]{:S(2)}) %collective-permute-start.41) | collective-permute-done | bytes 458784 | tf_op jit(solution)/shard_map/ppermute | solution.py:117
  283.1 7.6 %collective-permute-done.42 = bf16[128,1792]{1,0:T(8,128)(2,1)} collective-permute-done((bf16[128,1792]{1,0:T(8,128)(2,1)S(1)}, bf16[128,1792]{1,0:T(8,128)(2,1)}, u32[]{:S(2)}, u32[]{:S(2)}) %collective-permute-start.42) | collective-permute-done | bytes 458784 | tf_op jit(solution)/shard_map/ppermute | solution.py:117
  293.6 7.8 %collective-permute-done.43 = bf16[128,1792]{1,0:T(8,128)(2,1)S(1)} collective-permute-done((bf16[128,1792]{1,0:T(8,128)(2,1)}, bf16[128,1792]{1,0:T(8,128)(2,1)S(1)}, u32[]{:S(2)}, u32[]{:S(2)}) %collective-permute-start.43) | collective-permute-done | bytes 458784 | tf_op jit(solution)/shard_map/ppermute | solution.py:117
  301.5 3.7 %fusion.8 = (f32[512]{0:T(512)S(1)}, bf16[512,1792]{1,0:T(8,128)(2,1)S(1)}) fusion(bf16[512,1792]{1,0:T(8,128)(2,1)S(1)} %select_dynamic-update-slice_fusion.3, bf16[512,1792]{1,0:T(8,128)(2,1)} %select_dynamic-update-slice_fusion), kind=kLoop, calls=%fused_computation.15 | loop fusion | flops 12844544 | bytes 5507072 | tf_op jit(solution)/shard_map/reduce_sum | solution.py:182
  305.2 4.4 %fusion.21 = bf16[512,1024]{1,0:T(8,128)(2,1)S(1)} fusion(bf16[1024,1792]{1,0:T(8,128)(2,1)S(1)} %copy-done.4, bf16[512,1792]{1,0:T(8,128)(2,1)S(1)} %select_dynamic-update-slice_fusion.3, bf16[512,1792]{1,0:T(8,128)(2,1)} %select_dynamic-update-slice_fusion), kind=kOutput, calls=%fused_computation.35 | convolution fusion | flops 1889665024 | bytes 8388608 | tf_op jit(solution)/shard_map/dot_general | solution.py:27
  317.8 4.2 %collective-permute-done.69 = bf16[128,640]{1,0:T(8,128)(2,1)S(1)} collective-permute-done((bf16[128,640]{1,0:T(8,128)(2,1)S(1)}, bf16[128,640]{1,0:T(8,128)(2,1)S(1)}, u32[]{:S(2)}, u32[]{:S(2)}) %collective-permute-start.69) | collective-permute-done | bytes 163872 | tf_op jit(solution)/shard_map/ppermute | solution.py:53
  335.7 3.8 %collective-permute-done.47 = bf16[128,512]{1,0:T(8,128)(2,1)S(1)} collective-permute-done((bf16[128,512]{1,0:T(8,128)(2,1)S(1)}, bf16[128,512]{1,0:T(8,128)(2,1)S(1)}, u32[]{:S(2)}, u32[]{:S(2)}) %collective-permute-start.47) | collective-permute-done | bytes 131104 | tf_op jit(solution)/shard_map/ppermute | solution.py:53
  339.5 2.3 collective-permute-done.46
  344.1 11.7 %collective-permute-done.48 = bf16[128,512]{1,0:T(8,128)(2,1)S(1)} collective-permute-done((bf16[128,512]{1,0:T(8,128)(2,1)S(1)}, bf16[128,512]{1,0:T(8,128)(2,1)S(1)}, u32[]{:S(2)}, u32[]{:S(2)}) %collective-permute-start.48) | collective-permute-done | bytes 131104 | tf_op jit(solution)/shard_map/ppermute | solution.py:47
  356.1 5.5 %convolution_convert_fusion = bf16[1792,1024]{1,0:T(8,128)(2,1)} fusion(bf16[512,1792]{1,0:T(8,128)(2,1)S(1)} %get-tuple-element.15, bf16[512,1792]{1,0:T(8,128)(2,1)S(1)} %copy-done.8, bf16[512,1024]{1,0:T(8,128)(2,1)S(1)} %copy-done.10, bf16[512,1024]{1,0:T(8,128)(2,1)S(1)} %maximum_select_fusion.3), kind=kOutput, calls=%fused_computation.8 | convolution fusion | flops 3771465728 | bytes 9437184 | tf_op jit(solution)/shard_map/dot_general | solution.py:27
  (230 shorter events, 108.2 us)
Async XLA Ops:
  2.3 14.7 %collective-permute-start = (bf16[144,512]{1,0:T(8,128)(2,1)S(1)}, bf16[144,512]{1,0:T(8,128)(2,1)S(1)}, u32[]{:S(2)}, u32[]{:S(2)}) collective-permute-start(bf16[144,512]{1,0:T(8,128)(2,1)S(1)} %pad_maximum_fusion.4), channel_id=1, source_target_pairs={{0,0},{1,8},{2,16},{3,24},{4,4},{5,12},{6,20},{7,28},{8,1},{9,9},{... | collective-permute-start | bytes 442376 | tf_op jit(solution)/shard_map/ppermute | solution.py:47
  35.7 12.9 %collective-permute-start.6 = (bf16[128,1792]{1,0:T(8,128)(2,1)}, bf16[128,1792]{1,0:T(8,128)(2,1)}, u32[]{:S(2)}, u32[]{:S(2)}) collective-permute-start(bf16[128,1792]{1,0:T(8,128)(2,1)} %get-tuple-element.26), channel_id=1, source_target_pairs={{0,1},{4,5},{8,9},{12,13},{16,17},{20,21},{24,25},{28,29}} | collective-permute-start | bytes 1376264 | tf_op jit(solution)/shard_map/ppermute | solution.py:104
  38.8 16.8 %collective-permute-start.9 = (bf16[128,1792]{1,0:T(8,128)(2,1)}, bf16[128,1792]{1,0:T(8,128)(2,1)}, u32[]{:S(2)}, u32[]{:S(2)}) collective-permute-start(bf16[128,1792]{1,0:T(8,128)(2,1)} %get-tuple-element.27), channel_id=1, source_target_pairs={{3,2},{7,6},{11,10},{15,14},{19,18},{23,22},{27,26},{31,30}} | collective-permute-start | bytes 1376264 | tf_op jit(solution)/shard_map/ppermute | solution.py:105
  50.4 14.2 %collective-permute-start.7 = (bf16[128,1792]{1,0:T(8,128)(2,1)}, bf16[128,1792]{1,0:T(8,128)(2,1)}, u32[]{:S(2)}, u32[]{:S(2)}) collective-permute-start(bf16[128,1792]{1,0:T(8,128)(2,1)} %add_convert_fusion.15), channel_id=1, source_target_pairs={{0,1},{1,2},{4,5},{5,6},{8,9},{9,10},{12,13},{13,14},{16,17},{17,1... | collective-permute-start | bytes 1376264 | tf_op jit(solution)/shard_map/ppermute | solution.py:104
  68.3 28.4 %collective-permute-start.8 = (bf16[128,1792]{1,0:T(8,128)(2,1)}, bf16[128,1792]{1,0:T(8,128)(2,1)}, u32[]{:S(2)}, u32[]{:S(2)}) collective-permute-start(bf16[128,1792]{1,0:T(8,128)(2,1)} %get-tuple-element.24), channel_id=1, source_target_pairs={{0,1},{1,2},{2,3},{4,5},{5,6},{6,7},{8,9},{9,10},{10,11},{12,13},{... | collective-permute-start | bytes 1376264 | tf_op jit(solution)/shard_map/ppermute | solution.py:104
  75.3 21.5 %collective-permute-start.11 = (bf16[128,1792]{1,0:T(8,128)(2,1)}, bf16[128,1792]{1,0:T(8,128)(2,1)}, u32[]{:S(2)}, u32[]{:S(2)}) collective-permute-start(bf16[128,1792]{1,0:T(8,128)(2,1)} %add_convert_fusion.12), channel_id=1, source_target_pairs={{3,2},{2,1},{1,0},{7,6},{6,5},{5,4},{11,10},{10,9},{9,8},{15,14},{... | collective-permute-start | bytes 1376264 | tf_op jit(solution)/shard_map/ppermute | solution.py:105
  76.9 18.3 %collective-permute-start.14 = (f32[4,128]{1,0:T(4,128)S(1)}, f32[4,128]{1,0:T(4,128)S(1)}, u32[]{:S(2)}, u32[]{:S(2)}) collective-permute-start(f32[4,128]{1,0:T(4,128)S(1)} %bitcast.35), channel_id=1, source_target_pairs={{0,3},{1,0},{2,1},{3,2},{4,7},{5,4},{6,5},{7,6},{8,11},{9,8},{10,9... | collective-permute-start | bytes 6152 | tf_op jit(solution)/shard_map/ppermute | solution.py:136
  99.2 17.3 %collective-permute-start.15 = (bf16[128,1792]{1,0:T(8,128)(2,1)}, bf16[128,1792]{1,0:T(8,128)(2,1)S(1)}, u32[]{:S(2)}, u32[]{:S(2)}) collective-permute-start(bf16[128,1792]{1,0:T(8,128)(2,1)} %get-tuple-element.13), channel_id=1, source_target_pairs={{0,1},{1,2},{2,3},{4,5},{5,6},{6,7},{8,9},{9,10},{10,11},{12,13},{... | collective-permute-start | bytes 1376264 | tf_op jit(solution)/shard_map/ppermute | solution.py:114
  101.7 9.7 %collective-permute-start.49 = (bf16[128,512]{1,0:T(8,128)(2,1)S(1)}, bf16[128,512]{1,0:T(8,128)(2,1)S(1)}, u32[]{:S(2)}, u32[]{:S(2)}) collective-permute-start(bf16[128,512]{1,0:T(8,128)(2,1)S(1)} %copy-done.17), channel_id=1, source_target_pairs={{0,0},{1,8},{2,16},{3,24},{4,4},{5,12},{6,20},{7,28},{8,1},{9,9},{... | collective-permute-start | bytes 393224 | tf_op jit(solution)/shard_map/ppermute | solution.py:47
  115.3 11.6 %collective-permute-start.18 = (bf16[128,1792]{1,0:T(8,128)(2,1)}, bf16[128,1792]{1,0:T(8,128)(2,1)S(1)}, u32[]{:S(2)}, u32[]{:S(2)}) collective-permute-start(bf16[128,1792]{1,0:T(8,128)(2,1)} %get-tuple-element.13), channel_id=1, source_target_pairs={{3,2},{2,1},{1,0},{7,6},{6,5},{5,4},{11,10},{10,9},{9,8},{15,14},{... | collective-permute-start | bytes 1376264 | tf_op jit(solution)/shard_map/ppermute | solution.py:117
  116.6 11.6 %collective-permute-start.16 = (bf16[128,1792]{1,0:T(8,128)(2,1)S(1)}, bf16[128,1792]{1,0:T(8,128)(2,1)}, u32[]{:S(2)}, u32[]{:S(2)}) collective-permute-start(bf16[128,1792]{1,0:T(8,128)(2,1)S(1)} %collective-permute-done.15), channel_id=1, source_target_pairs={{1,2},{2,3},{5,6},{6,7},{9,10},{10,11},{13,14},{14,15},{17,18},{18... | collective-permute-start | bytes 1376264 | tf_op jit(solution)/shard_map/ppermute | solution.py:114
  120.7 14.7 %collective-permute-start.53 = (bf16[512,512]{1,0:T(8,128)(2,1)S(1)}, bf16[512,512]{1,0:T(8,128)(2,1)}, u32[]{:S(2)}, u32[]{:S(2)}) collective-permute-start(bf16[512,512]{1,0:T(8,128)(2,1)S(1)} %constant_dynamic-update-slice_fusion.5), channel_id=1, source_target_pairs={{0,4},{4,0},{8,12},{12,8},{16,20},{20,16},{24,28},{28,24},{1,5},{5... | collective-permute-start | bytes 1572872 | tf_op jit(solution)/shard_map/ppermute | solution.py:50
  126.8 14.5 %collective-permute-start.19 = (bf16[128,1792]{1,0:T(8,128)(2,1)S(1)}, bf16[128,1792]{1,0:T(8,128)(2,1)}, u32[]{:S(2)}, u32[]{:S(2)}) collective-permute-start(bf16[128,1792]{1,0:T(8,128)(2,1)S(1)} %collective-permute-done.18), channel_id=1, source_target_pairs={{2,1},{1,0},{6,5},{5,4},{10,9},{9,8},{14,13},{13,12},{18,17},{17,1... | collective-permute-start | bytes 1376264 | tf_op jit(solution)/shard_map/ppermute | solution.py:117
  128.1 14.7 %collective-permute-start.17 = (bf16[128,1792]{1,0:T(8,128)(2,1)}, bf16[128,1792]{1,0:T(8,128)(2,1)}, u32[]{:S(2)}, u32[]{:S(2)}) collective-permute-start(bf16[128,1792]{1,0:T(8,128)(2,1)} %collective-permute-done.16), channel_id=1, source_target_pairs={{2,3},{6,7},{10,11},{14,15},{18,19},{22,23},{26,27},{30,31}} | collective-permute-start | bytes 1376264 | tf_op jit(solution)/shard_map/ppermute | solution.py:114
  141.4 10.8 %collective-permute-start.20 = (bf16[128,1792]{1,0:T(8,128)(2,1)}, bf16[128,1792]{1,0:T(8,128)(2,1)S(1)}, u32[]{:S(2)}, u32[]{:S(2)}) collective-permute-start(bf16[128,1792]{1,0:T(8,128)(2,1)} %collective-permute-done.19), channel_id=1, source_target_pairs={{1,0},{5,4},{9,8},{13,12},{17,16},{21,20},{25,24},{29,28}} | collective-permute-start | bytes 1376264 | tf_op jit(solution)/shard_map/ppermute | solution.py:117
  156.7 12.0 %collective-permute-start.54 = (bf16[128,1792]{1,0:T(8,128)(2,1)S(1)}, bf16[128,1792]{1,0:T(8,128)(2,1)S(1)}, u32[]{:S(2)}, u32[]{:S(2)}) collective-permute-start(bf16[128,1792]{1,0:T(8,128)(2,1)S(1)} %get-tuple-element.18), channel_id=1, source_target_pairs={{0,1},{4,5},{8,9},{12,13},{16,17},{20,21},{24,25},{28,29}} | collective-permute-start | bytes 1376264 | tf_op jit(solution)/shard_map/ppermute | solution.py:104
  158.7 8.5 %collective-permute-start.23 = (bf16[128,512]{1,0:T(8,128)(2,1)S(1)}, bf16[128,512]{1,0:T(8,128)(2,1)S(1)}, u32[]{:S(2)}, u32[]{:S(2)}) collective-permute-start(bf16[128,512]{1,0:T(8,128)(2,1)S(1)} %get-tuple-element.38), channel_id=1, source_target_pairs={{0,16},{4,20},{8,24},{12,28},{16,0},{20,4},{24,8},{28,12},{1,17},{... | collective-permute-start | bytes 393224 | tf_op jit(solution)/shard_map/ppermute | solution.py:53
  162.1 19.3 %collective-permute-start.57 = (bf16[128,1792]{1,0:T(8,128)(2,1)S(1)}, bf16[128,1792]{1,0:T(8,128)(2,1)S(1)}, u32[]{:S(2)}, u32[]{:S(2)}) collective-permute-start(bf16[128,1792]{1,0:T(8,128)(2,1)S(1)} %get-tuple-element.19), channel_id=1, source_target_pairs={{3,2},{7,6},{11,10},{15,14},{19,18},{23,22},{27,26},{31,30}} | collective-permute-start | bytes 1376264 | tf_op jit(solution)/shard_map/ppermute | solution.py:105
  168.8 14.3 %collective-permute-start.55 = (bf16[128,1792]{1,0:T(8,128)(2,1)S(1)}, bf16[128,1792]{1,0:T(8,128)(2,1)S(1)}, u32[]{:S(2)}, u32[]{:S(2)}) collective-permute-start(bf16[128,1792]{1,0:T(8,128)(2,1)S(1)} %add_convert_fusion.7), channel_id=1, source_target_pairs={{0,1},{1,2},{4,5},{5,6},{8,9},{9,10},{12,13},{13,14},{16,17},{17,1... | collective-permute-start | bytes 1376264 | tf_op jit(solution)/shard_map/ppermute | solution.py:104
  183.4 12.5 %collective-permute-start.58 = (bf16[128,1792]{1,0:T(8,128)(2,1)S(1)}, bf16[128,1792]{1,0:T(8,128)(2,1)S(1)}, u32[]{:S(2)}, u32[]{:S(2)}) collective-permute-start(bf16[128,1792]{1,0:T(8,128)(2,1)S(1)} %get-tuple-element.17), channel_id=1, source_target_pairs={{3,2},{2,1},{7,6},{6,5},{11,10},{10,9},{15,14},{14,13},{19,18},{18... | collective-permute-start | bytes 1376264 | tf_op jit(solution)/shard_map/ppermute | solution.py:105
  184.1 28.1 %collective-permute-start.56 = (bf16[128,1792]{1,0:T(8,128)(2,1)S(1)}, bf16[128,1792]{1,0:T(8,128)(2,1)S(1)}, u32[]{:S(2)}, u32[]{:S(2)}) collective-permute-start(bf16[128,1792]{1,0:T(8,128)(2,1)S(1)} %get-tuple-element.16), channel_id=1, source_target_pairs={{0,1},{1,2},{2,3},{4,5},{5,6},{6,7},{8,9},{9,10},{10,11},{12,13},{... | collective-permute-start | bytes 1376264 | tf_op jit(solution)/shard_map/ppermute | solution.py:104
  191.3 16.4 %collective-permute-start.29 = (bf16[128,1792]{1,0:T(8,128)(2,1)S(1)}, bf16[128,1792]{1,0:T(8,128)(2,1)S(1)}, u32[]{:S(2)}, u32[]{:S(2)}) collective-permute-start(bf16[128,1792]{1,0:T(8,128)(2,1)S(1)} %get-tuple-element.22), channel_id=1, source_target_pairs={{0,1},{4,5},{8,9},{12,13},{16,17},{20,21},{24,25},{28,29}} | collective-permute-start | bytes 1376264 | tf_op jit(solution)/shard_map/ppermute | solution.py:104
  196.0 16.2 %collective-permute-start.59 = (bf16[128,1792]{1,0:T(8,128)(2,1)S(1)}, bf16[128,1792]{1,0:T(8,128)(2,1)S(1)}, u32[]{:S(2)}, u32[]{:S(2)}) collective-permute-start(bf16[128,1792]{1,0:T(8,128)(2,1)S(1)} %add_convert_fusion.4), channel_id=1, source_target_pairs={{3,2},{2,1},{1,0},{7,6},{6,5},{5,4},{11,10},{10,9},{9,8},{15,14},{... | collective-permute-start | bytes 1376264 | tf_op jit(solution)/shard_map/ppermute | solution.py:105
  197.3 20.7 %collective-permute-start.32 = (bf16[128,1792]{1,0:T(8,128)(2,1)S(1)}, bf16[128,1792]{1,0:T(8,128)(2,1)S(1)}, u32[]{:S(2)}, u32[]{:S(2)}) collective-permute-start(bf16[128,1792]{1,0:T(8,128)(2,1)S(1)} %get-tuple-element.23), channel_id=1, source_target_pairs={{3,2},{7,6},{11,10},{15,14},{19,18},{23,22},{27,26},{31,30}} | collective-permute-start | bytes 1376264 | tf_op jit(solution)/shard_map/ppermute | solution.py:105
  207.8 15.3 %collective-permute-start.30 = (bf16[128,1792]{1,0:T(8,128)(2,1)S(1)}, bf16[128,1792]{1,0:T(8,128)(2,1)S(1)}, u32[]{:S(2)}, u32[]{:S(2)}) collective-permute-start(bf16[128,1792]{1,0:T(8,128)(2,1)S(1)} %add_convert_fusion.11), channel_id=1, source_target_pairs={{0,1},{1,2},{4,5},{5,6},{8,9},{9,10},{12,13},{13,14},{16,17},{17,1... | collective-permute-start | bytes 1376264 | tf_op jit(solution)/shard_map/ppermute | solution.py:104
  214.7 15.2 %collective-permute-start.60 = (bf16[128,1792]{1,0:T(8,128)(2,1)S(1)}, bf16[128,1792]{1,0:T(8,128)(2,1)S(1)}, u32[]{:S(2)}, u32[]{:S(2)}) collective-permute-start(bf16[128,1792]{1,0:T(8,128)(2,1)S(1)} %get-tuple-element.7), channel_id=1, source_target_pairs={{0,1},{1,2},{2,3},{4,5},{5,6},{6,7},{8,9},{9,10},{10,11},{12,13},{... | collective-permute-start | bytes 1376264 | tf_op jit(solution)/shard_map/ppermute | solution.py:114
  216.7 13.8 %collective-permute-start.63 = (bf16[128,1792]{1,0:T(8,128)(2,1)S(1)}, bf16[128,1792]{1,0:T(8,128)(2,1)S(1)}, u32[]{:S(2)}, u32[]{:S(2)}) collective-permute-start(bf16[128,1792]{1,0:T(8,128)(2,1)S(1)} %get-tuple-element.7), channel_id=1, source_target_pairs={{3,2},{2,1},{1,0},{7,6},{6,5},{5,4},{11,10},{10,9},{9,8},{15,14},{... | collective-permute-start | bytes 1376264 | tf_op jit(solution)/shard_map/ppermute | solution.py:117
  223.4 15.1 %collective-permute-start.33 = (bf16[128,1792]{1,0:T(8,128)(2,1)S(1)}, bf16[128,1792]{1,0:T(8,128)(2,1)S(1)}, u32[]{:S(2)}, u32[]{:S(2)}) collective-permute-start(bf16[128,1792]{1,0:T(8,128)(2,1)S(1)} %get-tuple-element.21), channel_id=1, source_target_pairs={{3,2},{2,1},{7,6},{6,5},{11,10},{10,9},{15,14},{14,13},{19,18},{18... | collective-permute-start | bytes 1376264 | tf_op jit(solution)/shard_map/ppermute | solution.py:105
  229.9 15.3 %collective-permute-start.61 = (bf16[128,1792]{1,0:T(8,128)(2,1)S(1)}, bf16[128,1792]{1,0:T(8,128)(2,1)S(1)}, u32[]{:S(2)}, u32[]{:S(2)}) collective-permute-start(bf16[128,1792]{1,0:T(8,128)(2,1)S(1)} %collective-permute-done.60), channel_id=1, source_target_pairs={{1,2},{2,3},{5,6},{6,7},{9,10},{10,11},{13,14},{14,15},{17,18},{18... | collective-permute-start | bytes 1376264 | tf_op jit(solution)/shard_map/ppermute | solution.py:114
  230.5 17.4 %collective-permute-start.64 = (bf16[128,1792]{1,0:T(8,128)(2,1)S(1)}, bf16[128,1792]{1,0:T(8,128)(2,1)S(1)}, u32[]{:S(2)}, u32[]{:S(2)}) collective-permute-start(bf16[128,1792]{1,0:T(8,128)(2,1)S(1)} %collective-permute-done.63), channel_id=1, source_target_pairs={{2,1},{1,0},{6,5},{5,4},{10,9},{9,8},{14,13},{13,12},{18,17},{17,1... | collective-permute-start | bytes 1376264 | tf_op jit(solution)/shard_map/ppermute | solution.py:117
  231.8 27.7 %collective-permute-start.31 = (bf16[128,1792]{1,0:T(8,128)(2,1)S(1)}, bf16[128,1792]{1,0:T(8,128)(2,1)S(1)}, u32[]{:S(2)}, u32[]{:S(2)}) collective-permute-start(bf16[128,1792]{1,0:T(8,128)(2,1)S(1)} %get-tuple-element.20), channel_id=1, source_target_pairs={{0,1},{1,2},{2,3},{4,5},{5,6},{6,7},{8,9},{9,10},{10,11},{12,13},{... | collective-permute-start | bytes 1376264 | tf_op jit(solution)/shard_map/ppermute | solution.py:104
  238.6 21.0 %collective-permute-start.34 = (bf16[128,1792]{1,0:T(8,128)(2,1)S(1)}, bf16[128,1792]{1,0:T(8,128)(2,1)S(1)}, u32[]{:S(2)}, u32[]{:S(2)}) collective-permute-start(bf16[128,1792]{1,0:T(8,128)(2,1)S(1)} %add_convert_fusion.8), channel_id=1, source_target_pairs={{3,2},{2,1},{1,0},{7,6},{6,5},{5,4},{11,10},{10,9},{9,8},{15,14},{... | collective-permute-start | bytes 1376264 | tf_op jit(solution)/shard_map/ppermute | solution.py:105
  240.2 13.8 %collective-permute-start.37 = (f32[4,128]{1,0:T(4,128)S(1)}, f32[4,128]{1,0:T(4,128)S(1)}, u32[]{:S(2)}, u32[]{:S(2)}) collective-permute-start(f32[4,128]{1,0:T(4,128)S(1)} %bitcast.32), channel_id=1, source_target_pairs={{0,3},{1,0},{2,1},{3,2},{4,7},{5,4},{6,5},{7,6},{8,11},{9,8},{10,9... | collective-permute-start | bytes 6152 | tf_op jit(solution)/shard_map/ppermute | solution.py:136
  245.1 13.1 %collective-permute-start.36 = (f32[4,128]{1,0:T(4,128)S(1)}, f32[4,128]{1,0:T(4,128)S(1)}, u32[]{:S(2)}, u32[]{:S(2)}) collective-permute-start(f32[4,128]{1,0:T(4,128)S(1)} %bitcast.33), channel_id=1, source_target_pairs={{0,2},{1,3},{2,0},{3,1},{4,6},{5,7},{6,4},{7,5},{8,10},{9,11},{10,... | collective-permute-start | bytes 6152 | tf_op jit(solution)/shard_map/ppermute | solution.py:136
  247.9 11.6 %collective-permute-start.35 = (f32[4,128]{1,0:T(4,128)S(1)}, f32[4,128]{1,0:T(4,128)S(1)}, u32[]{:S(2)}, u32[]{:S(2)}) collective-permute-start(f32[4,128]{1,0:T(4,128)S(1)} %bitcast.34), channel_id=1, source_target_pairs={{0,1},{1,2},{2,3},{3,0},{4,5},{5,6},{6,7},{7,4},{8,9},{9,10},{10,1... | collective-permute-start | bytes 6152 | tf_op jit(solution)/shard_map/ppermute | solution.py:136
  254.1 10.5 %collective-permute-start.62 = (bf16[128,1792]{1,0:T(8,128)(2,1)S(1)}, bf16[128,1792]{1,0:T(8,128)(2,1)S(1)}, u32[]{:S(2)}, u32[]{:S(2)}) collective-permute-start(bf16[128,1792]{1,0:T(8,128)(2,1)S(1)} %collective-permute-done.61), channel_id=1, source_target_pairs={{2,3},{6,7},{10,11},{14,15},{18,19},{22,23},{26,27},{30,31}} | collective-permute-start | bytes 1376264 | tf_op jit(solution)/shard_map/ppermute | solution.py:114
  258.3 23.8 %collective-permute-start.65 = (bf16[128,1792]{1,0:T(8,128)(2,1)S(1)}, bf16[128,1792]{1,0:T(8,128)(2,1)S(1)}, u32[]{:S(2)}, u32[]{:S(2)}) collective-permute-start(bf16[128,1792]{1,0:T(8,128)(2,1)S(1)} %collective-permute-done.64), channel_id=1, source_target_pairs={{1,0},{5,4},{9,8},{13,12},{17,16},{21,20},{25,24},{29,28}} | collective-permute-start | bytes 1376264 | tf_op jit(solution)/shard_map/ppermute | solution.py:117
  260.0 11.2 %collective-permute-start.38 = (bf16[128,1792]{1,0:T(8,128)(2,1)S(1)}, bf16[128,1792]{1,0:T(8,128)(2,1)S(1)}, u32[]{:S(2)}, u32[]{:S(2)}) collective-permute-start(bf16[128,1792]{1,0:T(8,128)(2,1)S(1)} %get-tuple-element.9), channel_id=1, source_target_pairs={{0,1},{1,2},{2,3},{4,5},{5,6},{6,7},{8,9},{9,10},{10,11},{12,13},{... | collective-permute-start | bytes 1376264 | tf_op jit(solution)/shard_map/ppermute | solution.py:114
  265.5 13.9 %collective-permute-start.41 = (bf16[128,1792]{1,0:T(8,128)(2,1)S(1)}, bf16[128,1792]{1,0:T(8,128)(2,1)S(1)}, u32[]{:S(2)}, u32[]{:S(2)}) collective-permute-start(bf16[128,1792]{1,0:T(8,128)(2,1)S(1)} %get-tuple-element.9), channel_id=1, source_target_pairs={{3,2},{2,1},{1,0},{7,6},{6,5},{5,4},{11,10},{10,9},{9,8},{15,14},{... | collective-permute-start | bytes 1376264 | tf_op jit(solution)/shard_map/ppermute | solution.py:117
  271.1 9.5 %collective-permute-start.39 = (bf16[128,1792]{1,0:T(8,128)(2,1)S(1)}, bf16[128,1792]{1,0:T(8,128)(2,1)}, u32[]{:S(2)}, u32[]{:S(2)}) collective-permute-start(bf16[128,1792]{1,0:T(8,128)(2,1)S(1)} %collective-permute-done.38), channel_id=1, source_target_pairs={{1,2},{2,3},{5,6},{6,7},{9,10},{10,11},{13,14},{14,15},{17,18},{18... | collective-permute-start | bytes 1376264 | tf_op jit(solution)/shard_map/ppermute | solution.py:114
  279.3 11.4 %collective-permute-start.42 = (bf16[128,1792]{1,0:T(8,128)(2,1)S(1)}, bf16[128,1792]{1,0:T(8,128)(2,1)}, u32[]{:S(2)}, u32[]{:S(2)}) collective-permute-start(bf16[128,1792]{1,0:T(8,128)(2,1)S(1)} %collective-permute-done.41), channel_id=1, source_target_pairs={{2,1},{1,0},{6,5},{5,4},{10,9},{9,8},{14,13},{13,12},{18,17},{17,1... | collective-permute-start | bytes 1376264 | tf_op jit(solution)/shard_map/ppermute | solution.py:117
  280.6 11.6 %collective-permute-start.40 = (bf16[128,1792]{1,0:T(8,128)(2,1)}, bf16[128,1792]{1,0:T(8,128)(2,1)}, u32[]{:S(2)}, u32[]{:S(2)}) collective-permute-start(bf16[128,1792]{1,0:T(8,128)(2,1)} %collective-permute-done.39), channel_id=1, source_target_pairs={{2,3},{6,7},{10,11},{14,15},{18,19},{22,23},{26,27},{30,31}} | collective-permute-start | bytes 1376264 | tf_op jit(solution)/shard_map/ppermute | solution.py:114
  290.8 10.6 %collective-permute-start.43 = (bf16[128,1792]{1,0:T(8,128)(2,1)}, bf16[128,1792]{1,0:T(8,128)(2,1)S(1)}, u32[]{:S(2)}, u32[]{:S(2)}) collective-permute-start(bf16[128,1792]{1,0:T(8,128)(2,1)} %collective-permute-done.42), channel_id=1, source_target_pairs={{1,0},{5,4},{9,8},{13,12},{17,16},{21,20},{25,24},{29,28}} | collective-permute-start | bytes 1376264 | tf_op jit(solution)/shard_map/ppermute | solution.py:117
  314.1 7.9 %collective-permute-start.69 = (bf16[128,640]{1,0:T(8,128)(2,1)S(1)}, bf16[128,640]{1,0:T(8,128)(2,1)S(1)}, u32[]{:S(2)}, u32[]{:S(2)}) collective-permute-start(bf16[128,640]{1,0:T(8,128)(2,1)S(1)} %get-tuple-element.31), channel_id=1, source_target_pairs={{0,24},{4,28},{8,16},{12,20},{16,8},{20,12},{24,0},{28,4},{1,25},{... | collective-permute-start | bytes 491528 | tf_op jit(solution)/shard_map/ppermute | solution.py:53
  314.2 8.7 %collective-permute-start.68 = (bf16[128,640]{1,0:T(8,128)(2,1)S(1)}, bf16[128,640]{1,0:T(8,128)(2,1)S(1)}, u32[]{:S(2)}, u32[]{:S(2)}) collective-permute-start(bf16[128,640]{1,0:T(8,128)(2,1)S(1)} %get-tuple-element.32), channel_id=1, source_target_pairs={{0,16},{4,20},{8,24},{12,28},{16,0},{20,4},{24,8},{28,12},{1,17},{... | collective-permute-start | bytes 491528 | tf_op jit(solution)/shard_map/ppermute | solution.py:53
  332.0 23.7 %collective-permute-start.73 = (bf16[512,512]{1,0:T(8,128)(2,1)S(1)}, bf16[512,512]{1,0:T(8,128)(2,1)S(1)}, u32[]{:S(2)}, u32[]{:S(2)}) collective-permute-start(bf16[512,512]{1,0:T(8,128)(2,1)S(1)} %constant_dynamic-update-slice_fusion), channel_id=1, source_target_pairs={{0,4},{4,0},{8,12},{12,8},{16,20},{20,16},{24,28},{28,24},{1,5},{5... | collective-permute-start | bytes 1572872 | tf_op jit(solution)/shard_map/ppermute | solution.py:50
  333.8 8.0 %collective-permute-start.46 = (bf16[128,512]{1,0:T(8,128)(2,1)S(1)}, bf16[128,512]{1,0:T(8,128)(2,1)S(1)}, u32[]{:S(2)}, u32[]{:S(2)}) collective-permute-start(bf16[128,512]{1,0:T(8,128)(2,1)S(1)} %get-tuple-element.35), channel_id=1, source_target_pairs={{0,16},{4,20},{8,24},{12,28},{16,0},{20,4},{24,8},{28,12},{1,17},{... | collective-permute-start | bytes 393224 | tf_op jit(solution)/shard_map/ppermute | solution.py:53
  341.9 13.9 %collective-permute-start.48 = (bf16[128,512]{1,0:T(8,128)(2,1)S(1)}, bf16[128,512]{1,0:T(8,128)(2,1)S(1)}, u32[]{:S(2)}, u32[]{:S(2)}) collective-permute-start(bf16[128,512]{1,0:T(8,128)(2,1)S(1)} %fusion.29), channel_id=1, source_target_pairs={{0,0},{1,8},{2,16},{3,24},{4,4},{5,12},{6,20},{7,28},{8,1},{9,9},{... | collective-permute-start | bytes 393224 | tf_op jit(solution)/shard_map/ppermute | solution.py:47
  (44 other events, 464.2 us)

commit v3 on v1

v3 whole, which is shorter than its diff:
```python
import jax
import jax.numpy as jnp
from jax import lax
from jax.sharding import PartitionSpec as P

LANES = 128
PAD = 16
CHUNKS = 2
epsilon = 1e-05
F32 = jnp.float32
BF16 = jnp.bfloat16


def dequant_rows(quanta, scales):
    blocks = scales.shape[0]
    widened = quanta.astype(F32).reshape(blocks, quanta.shape[0] // blocks, quanta.shape[1])
    return (widened * scales.astype(F32)[:, None, :]).reshape(quanta.shape).astype(BF16)


def dequant_cols(quanta, scales):
    blocks = scales.shape[1]
    widened = quanta.astype(F32).reshape(quanta.shape[0], blocks, quanta.shape[1] // blocks)
    return (widened * scales.astype(F32)[:, :, None]).reshape(quanta.shape).astype(BF16)


def dot(left, right, dims):
    return lax.dot_general(left, right, (dims, ((), ())), preferred_element_type=F32)


def split_pair(column):
    high = column.astype(BF16)
    low = (column - high.astype(F32)).astype(BF16)
    shape = (column.shape[0], LANES // 2)
    return [jnp.broadcast_to(high, shape), jnp.broadcast_to(low, shape)]


def join_pair(lanes):
    lanes = lanes.astype(F32)
    return lanes[:, :1] + lanes[:, -1:]


def body(n_node, n_local, tokens, cotangent, gain, up_q, up_scale, down_q, down_scale):
    rows, cols = tokens.shape
    part = rows // CHUNKS
    hidden_units = up_q.shape[1]
    halves = n_node // n_local
    chips = n_local
    features = cols * n_node
    z = lax.axis_index("local")
    node = lax.axis_index("node")
    chip, core = node // halves, node % halves
    last = n_local - 1

    swap = [
        ((halves * c + j) * n_local + l, (halves * l + j) * n_local + c)
        for c in range(n_local)
        for j in range(halves)
        for l in range(n_local)
    ]

    def exchange(block):
        return lax.ppermute(block, ("node", "local"), swap)

    def core_swap(block):
        return lax.ppermute(block, "node", [(n, n ^ 1) for n in range(n_node)])

    def chip_swap(block, shift):
        return lax.ppermute(block, "node", [(n, n ^ (2 * shift)) for n in range(n_node)])

    def send_right(block, senders):
        return lax.ppermute(block, "local", [(s, s + 1) for s in senders])

    def send_left(block, senders):
        return lax.ppermute(block, "local", [(last - s, last - 1 - s) for s in senders])

    def take(array, index):
        width = array.shape[1]
        array = array.reshape(-1, n_local, part, width)
        return lax.dynamic_slice_in_dim(array, index, 1, 1).reshape(-1, width)

    def put(array, block, index):
        width = array.shape[1]
        stacked = array.reshape(-1, n_local, part, width)
        block = block.reshape(-1, 1, part, width)
        return lax.dynamic_update_slice_in_dim(stacked, block, index, 1).reshape(array.shape)

    def order(own, other):
        return jnp.where(
            core == 0,
            jnp.concatenate([own, other], axis=1),
            jnp.concatenate([other, own], axis=1),
        )

    def gather_node(block):
        mine = jnp.zeros((block.shape[0] * chips, block.shape[1]), block.dtype)
        mine = put(mine, block, chip)
        for shift in range(1, chips):
            mine = put(mine, chip_swap(block, shift), chip ^ shift)
        return order(mine, core_swap(mine))

    def scatter_node(partial, tail=None):
        first, second = partial[:, :cols], partial[:, cols:]
        keep = jnp.where(core == 0, first, second)
        send = jnp.where(core == 0, second, first)
        if tail is not None:
            keep = jnp.concatenate([keep] + tail, axis=1)
            send = jnp.concatenate([send] + tail, axis=1)
        both = (keep.astype(F32) + core_swap(send).astype(F32)).astype(BF16)
        total = take(both, chip).astype(F32)
        for shift in range(1, chips):
            total = total + chip_swap(take(both, chip ^ shift), shift).astype(F32)
        return total

    def line(block, partial):
        right = left = None
        rights, lefts = [], []
        everyone = range(last)
        if block is not None:
            right, left = send_right(block, everyone), send_left(block, everyone)
            rights.append(right)
            lefts.append(left)
            if partial is None:
                for step in range(1, last):
                    right = send_right(right, range(step, last))
                    left = send_left(left, range(step, last))
                    rights.append(right)
                    lefts.append(left)
        total = None
        if partial is not None:
            for step in range(1, n_local):
                to_right = take(partial, jnp.minimum(z + n_local - step, last))
                to_left = take(partial, jnp.maximum(z - n_local + step, 0))
                if right is not None:
                    zero = jnp.zeros((), F32)
                    to_right = jnp.where(z < step, to_right.astype(F32), zero)
                    to_left = jnp.where(last - z < step, to_left.astype(F32), zero)
                    to_right = (right.astype(F32) + to_right).astype(BF16)
                    to_left = (left.astype(F32) + to_left).astype(BF16)
                senders = everyone if block is not None else range(step)
                right, left = send_right(to_right, senders), send_left(to_left, senders)
                rights.append(right)
                lefts.append(left)
            total = take(partial, z).astype(F32) + right.astype(F32) + left.astype(F32)
        out = None
        if block is not None:
            out = jnp.zeros((part * n_local, block.shape[1]), block.dtype)
            out = put(out, block, z)
            for ahead in range(1, n_local):
                behind = n_local - ahead
                piece = jnp.where(z >= behind, rights[behind - 1], lefts[ahead - 1])
                out = put(out, piece, (z + ahead) % n_local)
        return out, total

    def widen(block):
        return jnp.pad(block, ((0, 0), (0, LANES)))

    def chunk_of(array, h):
        size = part * n_local
        return array[h * size : (h + 1) * size]

    def up_partial(values):
        widened = values.astype(F32)
        squares = jnp.sum((widened * widened).reshape(values.shape[0], -1, LANES), axis=1)
        product = dot((widened * gains).astype(BF16), up_weight, ((1,), (0,)))
        return jnp.concatenate([product.astype(BF16), squares.astype(BF16)], axis=1)

    def finish_pre(total):
        mean = jnp.sum(total[:, hidden_units:], axis=-1, keepdims=True) / features
        factor = lax.rsqrt(mean + epsilon)
        return total[:, :hidden_units] * factor, factor

    first = exchange(jnp.concatenate([tokens, jnp.broadcast_to(gain, (PAD, cols))], axis=0))
    up_weight = dequant_rows(up_q, up_scale)
    down_weight = dequant_cols(down_q, down_scale)
    first, up_weight, down_weight = lax.optimization_barrier((first, up_weight, down_weight))
    x_home, gain_rows = first[:rows], first[rows:]
    gains = order(gain_rows, core_swap(gain_rows))[:1].astype(F32)
    gains_home = gain_rows[:1].astype(F32)
    g_home = exchange(cotangent)

    x = gather_node(x_home)
    partials = [up_partial(chunk_of(x, h)) for h in range(CHUNKS)]
    _, total = line(None, partials[0])
    hidden_own = jax.nn.silu(finish_pre(total)[0]).astype(BF16)
    hidden_a, total = line(widen(hidden_own), partials[1])
    hidden_a = hidden_a[:, :hidden_units]
    hidden_own = jax.nn.silu(finish_pre(total)[0]).astype(BF16)

    g = gather_node(g_home)
    slopes = [
        dot(chunk_of(g, h), down_weight, ((1,), (1,))).astype(BF16) for h in range(CHUNKS)
    ]
    hidden_b, total = line(hidden_own, slopes[0])
    hidden_first = [hidden_a, hidden_b]
    updates = [dot(hidden, down_weight, ((1,), (0,))).astype(BF16) for hidden in hidden_first]
    update = scatter_node(jnp.concatenate(updates, axis=0))
    x1_home = (x_home.astype(F32) + update).astype(BF16)
    slope_a, total = line(total.astype(BF16), slopes[1])

    x = gather_node(x1_home)
    partials = [up_partial(chunk_of(x, h)) for h in range(CHUNKS)]
    slope_b, total = line(widen(total.astype(BF16)), partials[0])
    slope_b = slope_b[:, :hidden_units]

    def pack_pre(total):
        pre, factor = finish_pre(total)
        return jnp.concatenate([pre.astype(BF16)] + split_pair(factor), axis=1)

    packed_a, total = line(pack_pre(total), partials[1])
    packed_b, _ = line(pack_pre(total), None)

    hidden_second, below = [], []
    for h, (packed, slope) in enumerate([(packed_a, slope_a), (packed_b, slope_b)]):
        pre = packed[:, :hidden_units].astype(F32)
        sigma = jax.nn.sigmoid(pre)
        hidden_second.append((pre * sigma).astype(BF16))
        pre_grad = slope.astype(F32) * sigma * (1.0 + pre * (1.0 - sigma))
        inner = jnp.sum(pre_grad * pre, axis=-1, keepdims=True)
        normed_grad = dot(pre_grad.astype(BF16), up_weight, ((1,), (1,))).astype(BF16)
        total = scatter_node(normed_grad, split_pair(inner))
        factor = join_pair(take(packed[:, hidden_units:], chip))
        inner = join_pair(total[:, cols:]) / (features * factor)
        back = factor * (total[:, :cols] * gains_home) - chunk_home(x1_home, h, part).astype(F32) * (
            factor * factor * factor * inner
        )
        grad_home = (chunk_home(g_home, h, part).astype(F32) + back).astype(BF16)
        below.append(gather_node(grad_home))
    updates = [dot(hidden, down_weight, ((1,), (0,))).astype(BF16) for hidden in hidden_second]
    update = scatter_node(jnp.concatenate(updates, axis=0))
    result = exchange((x1_home.astype(F32) + update).astype(BF16))
    grad_down = dot(
        jnp.concatenate(hidden_first + hidden_second, axis=0),
        jnp.concatenate(below + [g], axis=0),
        ((0,), (0,)),
    ).astype(BF16)
    return (result, grad_down)


def chunk_home(array, h, part):
    return array[h * part : (h + 1) * part]


def solution(mesh):
    n_node, n_local = mesh.shape["node"], mesh.shape["local"]

    def per_device(*arrays):
        return body(n_node, n_local, *arrays)

    in_specs = (
        P("local", "node"),
        P("local", "node"),
        P(None, "node"),
        P("local", "node"),
        P("local", "node"),
        P("node", "local"),
        P("node", "local"),
    )
    out_specs = (P("local", "node"), P("node", "local"))
    return jax.shard_map(
        per_device, mesh=mesh, in_specs=in_specs, out_specs=out_specs, check_vma=False
    )
```

time: 523 us -> 386 us (0.74)
  waiting for transfers between devices: 377 us -> 176 us
  starting transfers between devices: 9.99 us -> 148 us
  blocking collectives: 41.1 us -> 0 us
  local copies, waits for them, and re-layouts: 24.8 us -> 9.79 us
  matrix products: 32.3 us -> 19.7 us
  between operations: 14.2 us -> 2.92 us
    all_gather x7 -> x0, waiting for transfers between devices: 181 us -> none  [the longest x3 116 us: gather_local(): return lax.all_gather(block, 'local', axis=0, tiled=True)]
    ppermute x0 -> x89, waiting for transfers between devices: none -> 167 us  [the longest x26 101 us: send_left(): lax.ppermute(block, 'local', [(last - s, last - 1 - s) for s in senders])]
    reduce_scatter x6 -> x0, waiting for transfers between devices: 163 us -> none  [the longest x3 93.3 us: scatter_local(): return lax.psum_scatter(partial, 'local', scatter_dimension=0, tiled=True)]
    ppermute x0 -> x89, starting transfers between devices: none -> 141 us  [the longest x26 63.8 us: send_right(): return lax.ppermute(block, 'local', [(s, s + 1) for s in senders])]
    psum x3 -> x0, blocking collectives: 33.1 us -> none  [the longest x2 21.8 us: factor_of(): sums = lax.psum(jnp.sum(widened * widened, axis=-1, keepdims=True), 'local')]
    ppermute x3, waiting for transfers between devices: 31.9 us -> 9.14 us  [exchange(): return lax.ppermute(block, ('node', 'local'), swap)]
    dot_general x7 -> x13, matrix products: 32.3 us -> 19.7 us  [dot(): lax.dot_general(left, right, (dims, ((), ())), preferred_element_type=F32)]
    reshape x5 -> x3, local copies, waits for them, and re-layouts: 9.64 us -> 0.93 us  [take(): return lax.dynamic_slice_in_dim(array, index, 1, 1).reshape(-1, width)]
  transfers between devices with their start and end apart: 16 -> 92, of which waited for: 16 -> 57; matrix products, arithmetic and copies ran while one was open for 8% -> 10% of each run, Pallas kernels for 0% -> 0%
where the time goes in v3:
time: 386 us; the launch traced here: 381 us
  waiting for transfers between devices  176 us (46%)
  starting transfers between devices  148 us (38%)
  other arithmetic  23.8 us (6%)
  matrix products  19.7 us (5%)
  local copies, waits for them, and re-layouts  9.79 us (3%)
    ppermute x26, waiting for transfers between devices, send_left(): lax.ppermute(block, 'local', [(last - s, last - 1 - s) for s in senders])  101 us
    ppermute x26, starting transfers between devices, send_right(): return lax.ppermute(block, 'local', [(s, s + 1) for s in senders])  63.8 us
    ppermute x26, waiting for transfers between devices, send_right(): return lax.ppermute(block, 'local', [(s, s + 1) for s in senders])  49.2 us
    ppermute x26, starting transfers between devices, send_left(): lax.ppermute(block, 'local', [(last - s, last - 1 - s) for s in senders])  45 us
    ppermute x27, starting transfers between devices, chip_swap(): lax.ppermute(block, 'node', [(n, n ^ 2 * shift) for n in range(n_node)])  30.1 us
    dot_general x13, matrix products, dot(): lax.dot_general(left, right, (dims, ((), ())), preferred_element_type=F32)  19.7 us
    ppermute x27, waiting for transfers between devices, chip_swap(): lax.ppermute(block, 'node', [(n, n ^ 2 * shift) for n in range(n_node)])  16.6 us
    ppermute x3, waiting for transfers between devices, exchange(): return lax.ppermute(block, ('node', 'local'), swap)  9.14 us
  transfers between devices with their start and end apart: 92, of which 57 were waited for; matrix products, arithmetic and copies ran while one was open for 10% of the time, Pallas kernels for 0%

profile of v3, /device:TPU:2, one launch (start us, length us, event | category | flops | bytes accessed | tf_op | source)
XLA Modules:
  0.0 381.0 jit_solution(14167169334130780304)
XLA Ops:
  2.3 3.5 collective-permute-start
  8.8 3.8 %fusion = bf16[1792,1024]{1,0:T(8,128)(2,1)} fusion(f32[224,8,8,128]{3,2,1,0:T(8,128)S(1)} %bitcast.342, bf16[1792,1024]{1,0:T(8,128)(2,1)S(1)} %copy-done), kind=kLoop, calls=%fused_computation.1 | loop fusion | flops 5505024 | bytes 14680064 | tf_op jit(solution)/shard_map/convert_element_type | solution.py:23
  12.6 2.6 fusion.1
  20.6 2.7 collective-permute-done.1
  26.6 2.6 collective-permute-start.21
  37.2 3.5 collective-permute-done.21
  41.6 2.6 collective-permute-start.24
  48.9 3.6 collective-permute-done.7
  53.9 7.6 %collective-permute-start.8 = (bf16[64,1920]{1,0:T(8,128)(2,1)S(1)}, bf16[64,1920]{1,0:T(8,128)(2,1)S(1)}, u32[]{:S(2)}, u32[]{:S(2)}) collective-permute-start(bf16[64,1920]{1,0:T(8,128)(2,1)S(1)} %get-tuple-element.55), channel_id=1, source_target_pairs={{0,1},{1,2},{2,3},{4,5},{5,6},{6,7},{8,9},{9,10},{10,11},{12,13},{... | collective-permute-start | bytes 737288 | tf_op jit(solution)/shard_map/ppermute | solution.py:71
  65.6 4.4 %collective-permute-start.12 = (bf16[64,1920]{1,0:T(8,128)(2,1)S(1)}, bf16[64,1920]{1,0:T(8,128)(2,1)S(1)}, u32[]{:S(2)}, u32[]{:S(2)}) collective-permute-start(bf16[64,1920]{1,0:T(8,128)(2,1)S(1)} %pad.7), channel_id=1, source_target_pairs={{0,1},{1,2},{2,3},{4,5},{5,6},{6,7},{8,9},{9,10},{10,11},{12,13},{... | collective-permute-start | bytes 737288 | tf_op jit(solution)/shard_map/ppermute | solution.py:71
  73.7 4.9 %collective-permute-done.15 = bf16[64,1920]{1,0:T(8,128)(2,1)S(1)} collective-permute-done((bf16[64,1920]{1,0:T(8,128)(2,1)S(1)}, bf16[64,1920]{1,0:T(8,128)(2,1)S(1)}, u32[]{:S(2)}, u32[]{:S(2)}) %collective-permute-start.15) | collective-permute-done | bytes 245792 | tf_op jit(solution)/shard_map/ppermute | solution.py:74
  78.7 4.2 %collective-permute-start.13 = (bf16[64,1920]{1,0:T(8,128)(2,1)S(1)}, bf16[64,1920]{1,0:T(8,128)(2,1)S(1)}, u32[]{:S(2)}, u32[]{:S(2)}) collective-permute-start(bf16[64,1920]{1,0:T(8,128)(2,1)S(1)} %get-tuple-element.53), channel_id=1, source_target_pairs={{0,1},{1,2},{2,3},{4,5},{5,6},{6,7},{8,9},{9,10},{10,11},{12,13},{... | collective-permute-start | bytes 737288 | tf_op jit(solution)/shard_map/ppermute | solution.py:71
  86.6 4.4 %collective-permute-done.16 = bf16[64,1920]{1,0:T(8,128)(2,1)S(1)} collective-permute-done((bf16[64,1920]{1,0:T(8,128)(2,1)S(1)}, bf16[64,1920]{1,0:T(8,128)(2,1)S(1)}, u32[]{:S(2)}, u32[]{:S(2)}) %collective-permute-start.16) | collective-permute-done | bytes 245792 | tf_op jit(solution)/shard_map/ppermute | solution.py:74
  91.2 3.9 %collective-permute-start.14 = (bf16[64,1920]{1,0:T(8,128)(2,1)S(1)}, bf16[64,1920]{1,0:T(8,128)(2,1)S(1)}, u32[]{:S(2)}, u32[]{:S(2)}) collective-permute-start(bf16[64,1920]{1,0:T(8,128)(2,1)S(1)} %get-tuple-element.51), channel_id=1, source_target_pairs={{0,1},{1,2},{2,3},{4,5},{5,6},{6,7},{8,9},{9,10},{10,11},{12,13},{... | collective-permute-start | bytes 737288 | tf_op jit(solution)/shard_map/ppermute | solution.py:71
  99.0 4.7 %collective-permute-done.17 = bf16[64,1920]{1,0:T(8,128)(2,1)S(1)} collective-permute-done((bf16[64,1920]{1,0:T(8,128)(2,1)S(1)}, bf16[64,1920]{1,0:T(8,128)(2,1)S(1)}, u32[]{:S(2)}, u32[]{:S(2)}) %collective-permute-start.17) | collective-permute-done | bytes 245792 | tf_op jit(solution)/shard_map/ppermute | solution.py:74
  106.8 3.3 collective-permute-done.18
  110.1 4.7 %collective-permute-done.19 = bf16[64,1920]{1,0:T(8,128)(2,1)S(1)} collective-permute-done((bf16[64,1920]{1,0:T(8,128)(2,1)S(1)}, bf16[64,1920]{1,0:T(8,128)(2,1)S(1)}, u32[]{:S(2)}, u32[]{:S(2)}) %collective-permute-start.19) | collective-permute-done | bytes 245792 | tf_op jit(solution)/shard_map/ppermute | solution.py:74
  118.3 4.6 %collective-permute-done.20 = bf16[64,1792]{1,0:T(8,128)(2,1)S(1)} collective-permute-done((bf16[64,1792]{1,0:T(8,128)(2,1)S(1)}, bf16[64,1792]{1,0:T(8,128)(2,1)S(1)}, u32[]{:S(2)}, u32[]{:S(2)}) %collective-permute-start.20) | collective-permute-done | bytes 229408 | tf_op jit(solution)/shard_map/ppermute | solution.py:71
  122.9 4.1 %collective-permute-done.28 = bf16[64,1792]{1,0:T(8,128)(2,1)S(1)} collective-permute-done((bf16[64,1792]{1,0:T(8,128)(2,1)S(1)}, bf16[64,1792]{1,0:T(8,128)(2,1)S(1)}, u32[]{:S(2)}, u32[]{:S(2)}) %collective-permute-start.28) | collective-permute-done | bytes 229408 | tf_op jit(solution)/shard_map/ppermute | solution.py:74
  130.8 3.7 collective-permute-done.26
  134.5 4.1 %collective-permute-done.29 = bf16[64,1792]{1,0:T(8,128)(2,1)S(1)} collective-permute-done((bf16[64,1792]{1,0:T(8,128)(2,1)S(1)}, bf16[64,1792]{1,0:T(8,128)(2,1)S(1)}, u32[]{:S(2)}, u32[]{:S(2)}) %collective-permute-start.29) | collective-permute-done | bytes 229408 | tf_op jit(solution)/shard_map/ppermute | solution.py:74
  145.2 4.1 %collective-permute-done.30 = bf16[64,1792]{1,0:T(8,128)(2,1)S(1)} collective-permute-done((bf16[64,1792]{1,0:T(8,128)(2,1)S(1)}, bf16[64,1792]{1,0:T(8,128)(2,1)S(1)}, u32[]{:S(2)}, u32[]{:S(2)}) %collective-permute-start.30) | collective-permute-done | bytes 229408 | tf_op jit(solution)/shard_map/ppermute | solution.py:74
  156.9 2.8 collective-permute-done.40
  167.1 4.1 %collective-permute-done.45 = bf16[64,1792]{1,0:T(8,128)(2,1)S(1)} collective-permute-done((bf16[64,1792]{1,0:T(8,128)(2,1)S(1)}, bf16[64,1792]{1,0:T(8,128)(2,1)S(1)}, u32[]{:S(2)}, u32[]{:S(2)}) %collective-permute-start.45) | collective-permute-done | bytes 229408 | tf_op jit(solution)/shard_map/ppermute | solution.py:74
  178.6 3.6 collective-permute-done.46
  188.2 4.3 %collective-permute-done.47 = bf16[64,1792]{1,0:T(8,128)(2,1)S(1)} collective-permute-done((bf16[64,1792]{1,0:T(8,128)(2,1)S(1)}, bf16[64,1792]{1,0:T(8,128)(2,1)S(1)}, u32[]{:S(2)}, u32[]{:S(2)}) %collective-permute-start.47) | collective-permute-done | bytes 229408 | tf_op jit(solution)/shard_map/ppermute | solution.py:74
  198.2 4.4 %collective-permute-done.48 = bf16[64,1792]{1,0:T(8,128)(2,1)S(1)} collective-permute-done((bf16[64,1792]{1,0:T(8,128)(2,1)S(1)}, bf16[64,1792]{1,0:T(8,128)(2,1)S(1)}, u32[]{:S(2)}, u32[]{:S(2)}) %collective-permute-start.48) | collective-permute-done | bytes 229408 | tf_op jit(solution)/shard_map/ppermute | solution.py:74
  208.3 4.4 %collective-permute-done.53 = bf16[64,1920]{1,0:T(8,128)(2,1)S(1)} collective-permute-done((bf16[64,1920]{1,0:T(8,128)(2,1)S(1)}, bf16[64,1920]{1,0:T(8,128)(2,1)S(1)}, u32[]{:S(2)}, u32[]{:S(2)}) %collective-permute-start.53) | collective-permute-done | bytes 245792 | tf_op jit(solution)/shard_map/ppermute | solution.py:74
  218.5 4.4 %collective-permute-done.54 = bf16[64,1920]{1,0:T(8,128)(2,1)S(1)} collective-permute-done((bf16[64,1920]{1,0:T(8,128)(2,1)S(1)}, bf16[64,1920]{1,0:T(8,128)(2,1)S(1)}, u32[]{:S(2)}, u32[]{:S(2)}) %collective-permute-start.54) | collective-permute-done | bytes 245792 | tf_op jit(solution)/shard_map/ppermute | solution.py:74
  225.0 13.0 %collective-permute-start.55 = (bf16[64,1920]{1,0:T(8,128)(2,1)S(1)}, bf16[64,1920]{1,0:T(8,128)(2,1)S(1)}, u32[]{:S(2)}, u32[]{:S(2)}) collective-permute-start(bf16[64,1920]{1,0:T(8,128)(2,1)S(1)} %get-tuple-element.46), channel_id=1, source_target_pairs={{3,2},{2,1},{1,0},{7,6},{6,5},{5,4},{11,10},{10,9},{9,8},{15,14},{... | collective-permute-start | bytes 737288 | tf_op jit(solution)/shard_map/ppermute | solution.py:74
  239.9 4.6 %collective-permute-start.52 = (bf16[64,1920]{1,0:T(8,128)(2,1)S(1)}, bf16[64,1920]{1,0:T(8,128)(2,1)S(1)}, u32[]{:S(2)}, u32[]{:S(2)}) collective-permute-start(bf16[64,1920]{1,0:T(8,128)(2,1)S(1)} %get-tuple-element.43), channel_id=1, source_target_pairs={{0,1},{1,2},{2,3},{4,5},{5,6},{6,7},{8,9},{9,10},{10,11},{12,13},{... | collective-permute-start | bytes 737288 | tf_op jit(solution)/shard_map/ppermute | solution.py:71
  248.1 4.4 %collective-permute-done.56 = bf16[64,1920]{1,0:T(8,128)(2,1)S(1)} collective-permute-done((bf16[64,1920]{1,0:T(8,128)(2,1)S(1)}, bf16[64,1920]{1,0:T(8,128)(2,1)S(1)}, u32[]{:S(2)}, u32[]{:S(2)}) %collective-permute-start.56) | collective-permute-done | bytes 245792 | tf_op jit(solution)/shard_map/ppermute | solution.py:74
  256.6 3.7 collective-permute-done.57
  260.3 4.7 %collective-permute-done.60 = bf16[64,1920]{1,0:T(8,128)(2,1)S(1)} collective-permute-done((bf16[64,1920]{1,0:T(8,128)(2,1)S(1)}, bf16[64,1920]{1,0:T(8,128)(2,1)S(1)}, u32[]{:S(2)}, u32[]{:S(2)}) %collective-permute-start.60) | collective-permute-done | bytes 245792 | tf_op jit(solution)/shard_map/ppermute | solution.py:74
  269.2 3.8 collective-permute-done.58
  272.9 4.6 %collective-permute-done.61 = bf16[64,1920]{1,0:T(8,128)(2,1)S(1)} collective-permute-done((bf16[64,1920]{1,0:T(8,128)(2,1)S(1)}, bf16[64,1920]{1,0:T(8,128)(2,1)S(1)}, u32[]{:S(2)}, u32[]{:S(2)}) %collective-permute-start.61) | collective-permute-done | bytes 245792 | tf_op jit(solution)/shard_map/ppermute | solution.py:74
  280.9 3.9 %collective-permute-done.59 = bf16[64,1920]{1,0:T(8,128)(2,1)S(1)} collective-permute-done((bf16[64,1920]{1,0:T(8,128)(2,1)S(1)}, bf16[64,1920]{1,0:T(8,128)(2,1)S(1)}, u32[]{:S(2)}, u32[]{:S(2)}) %collective-permute-start.59) | collective-permute-done | bytes 245792 | tf_op jit(solution)/shard_map/ppermute | solution.py:71
  284.9 4.1 %collective-permute-done.62 = bf16[64,1920]{1,0:T(8,128)(2,1)S(1)} collective-permute-done((bf16[64,1920]{1,0:T(8,128)(2,1)S(1)}, bf16[64,1920]{1,0:T(8,128)(2,1)S(1)}, u32[]{:S(2)}, u32[]{:S(2)}) %collective-permute-start.62) | collective-permute-done | bytes 245792 | tf_op jit(solution)/shard_map/ppermute | solution.py:74
  292.8 3.6 collective-permute-done.63
  296.4 5.2 %collective-permute-done.64 = bf16[64,1920]{1,0:T(8,128)(2,1)S(1)} collective-permute-done((bf16[64,1920]{1,0:T(8,128)(2,1)S(1)}, bf16[64,1920]{1,0:T(8,128)(2,1)S(1)}, u32[]{:S(2)}, u32[]{:S(2)}) %collective-permute-start.64) | collective-permute-done | bytes 245792 | tf_op jit(solution)/shard_map/ppermute | solution.py:74
  309.0 5.6 %collective-permute-done.68 = bf16[64,1920]{1,0:T(8,128)(2,1)S(1)} collective-permute-done((bf16[64,1920]{1,0:T(8,128)(2,1)S(1)}, bf16[64,1920]{1,0:T(8,128)(2,1)S(1)}, u32[]{:S(2)}, u32[]{:S(2)}) %collective-permute-start.68) | collective-permute-done | bytes 245792 | tf_op jit(solution)/shard_map/ppermute | solution.py:74
  316.7 6.0 %collective-permute-done.69 = bf16[64,1920]{1,0:T(8,128)(2,1)S(1)} collective-permute-done((bf16[64,1920]{1,0:T(8,128)(2,1)S(1)}, bf16[64,1920]{1,0:T(8,128)(2,1)S(1)}, u32[]{:S(2)}, u32[]{:S(2)}) %collective-permute-start.69) | collective-permute-done | bytes 245792 | tf_op jit(solution)/shard_map/ppermute | solution.py:74
  324.2 6.6 %collective-permute-done.70 = bf16[64,1920]{1,0:T(8,128)(2,1)S(1)} collective-permute-done((bf16[64,1920]{1,0:T(8,128)(2,1)S(1)}, bf16[64,1920]{1,0:T(8,128)(2,1)S(1)}, u32[]{:S(2)}, u32[]{:S(2)}) %collective-permute-start.70) | collective-permute-done | bytes 245792 | tf_op jit(solution)/shard_map/ppermute | solution.py:74
  349.6 2.4 collective-permute-start.81
  363.0 2.5 collective-permute-done.72
  365.6 2.9 collective-permute-done.73
  370.8 5.5 %convolution_convert_fusion = bf16[1792,1024]{1,0:T(8,128)(2,1)} fusion(bf16[256,1792]{1,0:T(8,128)(2,1)S(1)} %get-tuple-element.36, bf16[256,1792]{1,0:T(8,128)(2,1)S(1)} %get-tuple-element.34, bf16[256,1792]{1,0:T(8,128)(2,1)S(1)} %bitcast.396, bf16[256,1792]{1,0:T(8,128)(2,1)S(1)} %copy-done.25, bf16[512,1024]{1,0:T(8,128)(2,1)S(1)} %copy-done.10, ...), kind=kOutput, calls=%fused_computation.4 | convolution fusion | flops 3780902912 | bytes 9437184 | tf_op jit(solution)/shard_map/dot_general | solution.py:27
  376.3 3.9 %collective-permute-done.75 = bf16[128,512]{1,0:T(8,128)(2,1)S(1)} collective-permute-done((bf16[128,512]{1,0:T(8,128)(2,1)S(1)}, bf16[128,512]{1,0:T(8,128)(2,1)S(1)}, u32[]{:S(2)}, u32[]{:S(2)}) %collective-permute-start.75) | collective-permute-done | bytes 131104 | tf_op jit(solution)/shard_map/ppermute | solution.py:62
  (370 shorter events, 171.5 us)
Async XLA Ops:
  2.3 14.7 %collective-permute-start = (bf16[144,512]{1,0:T(8,128)(2,1)S(1)}, bf16[144,512]{1,0:T(8,128)(2,1)S(1)}, u32[]{:S(2)}, u32[]{:S(2)}) collective-permute-start(bf16[144,512]{1,0:T(8,128)(2,1)S(1)} %pad_maximum_fusion.14), channel_id=1, source_target_pairs={{0,0},{1,8},{2,16},{3,24},{4,4},{5,12},{6,20},{7,28},{8,1},{9,9},{... | collective-permute-start | bytes 442376 | tf_op jit(solution)/shard_map/ppermute | solution.py:62
  26.6 14.1 %collective-permute-start.21 = (bf16[128,512]{1,0:T(8,128)(2,1)}, bf16[128,512]{1,0:T(8,128)(2,1)S(1)}, u32[]{:S(2)}, u32[]{:S(2)}) collective-permute-start(bf16[128,512]{1,0:T(8,128)(2,1)} %param.8), channel_id=1, source_target_pairs={{0,0},{1,8},{2,16},{3,24},{4,4},{5,12},{6,20},{7,28},{8,1},{9,9},{... | collective-permute-start | bytes 393224 | tf_op jit(solution)/shard_map/ppermute | solution.py:62
  33.7 10.5 %collective-permute-start.6 = (bf16[64,1920]{1,0:T(8,128)(2,1)}, bf16[64,1920]{1,0:T(8,128)(2,1)}, u32[]{:S(2)}, u32[]{:S(2)}) collective-permute-start(bf16[64,1920]{1,0:T(8,128)(2,1)} %get-tuple-element.59), channel_id=1, source_target_pairs={{0,1},{4,5},{8,9},{12,13},{16,17},{20,21},{24,25},{28,29}} | collective-permute-start | bytes 737288 | tf_op jit(solution)/shard_map/ppermute | solution.py:71
  35.9 8.4 %collective-permute-start.9 = (bf16[64,1920]{1,0:T(8,128)(2,1)}, bf16[64,1920]{1,0:T(8,128)(2,1)}, u32[]{:S(2)}, u32[]{:S(2)}) collective-permute-start(bf16[64,1920]{1,0:T(8,128)(2,1)} %get-tuple-element.60), channel_id=1, source_target_pairs={{3,2},{7,6},{11,10},{15,14},{19,18},{23,22},{27,26},{31,30}} | collective-permute-start | bytes 737288 | tf_op jit(solution)/shard_map/ppermute | solution.py:74
  48.8 35.5 %collective-permute-start.25 = (bf16[512,512]{1,0:T(8,128)(2,1)S(1)}, bf16[512,512]{1,0:T(8,128)(2,1)S(1)}, u32[]{:S(2)}, u32[]{:S(2)}) collective-permute-start(bf16[512,512]{1,0:T(8,128)(2,1)S(1)} %bitcast.382), channel_id=1, source_target_pairs={{0,4},{4,0},{8,12},{12,8},{16,20},{20,16},{24,28},{28,24},{1,5},{5... | collective-permute-start | bytes 1572872 | tf_op jit(solution)/shard_map/ppermute | solution.py:65
  52.6 11.1 %collective-permute-start.11 = (bf16[64,1920]{1,0:T(8,128)(2,1)S(1)}, bf16[64,1920]{1,0:T(8,128)(2,1)S(1)}, u32[]{:S(2)}, u32[]{:S(2)}) collective-permute-start(bf16[64,1920]{1,0:T(8,128)(2,1)S(1)} %get-tuple-element.56), channel_id=1, source_target_pairs={{3,2},{2,1},{1,0},{7,6},{6,5},{5,4},{11,10},{10,9},{9,8},{15,14},{... | collective-permute-start | bytes 737288 | tf_op jit(solution)/shard_map/ppermute | solution.py:74
  53.9 11.3 %collective-permute-start.8 = (bf16[64,1920]{1,0:T(8,128)(2,1)S(1)}, bf16[64,1920]{1,0:T(8,128)(2,1)S(1)}, u32[]{:S(2)}, u32[]{:S(2)}) collective-permute-start(bf16[64,1920]{1,0:T(8,128)(2,1)S(1)} %get-tuple-element.55), channel_id=1, source_target_pairs={{0,1},{1,2},{2,3},{4,5},{5,6},{6,7},{8,9},{9,10},{10,11},{12,13},{... | collective-permute-start | bytes 737288 | tf_op jit(solution)/shard_map/ppermute | solution.py:71
  65.6 8.1 %collective-permute-start.12 = (bf16[64,1920]{1,0:T(8,128)(2,1)S(1)}, bf16[64,1920]{1,0:T(8,128)(2,1)S(1)}, u32[]{:S(2)}, u32[]{:S(2)}) collective-permute-start(bf16[64,1920]{1,0:T(8,128)(2,1)S(1)} %pad.7), channel_id=1, source_target_pairs={{0,1},{1,2},{2,3},{4,5},{5,6},{6,7},{8,9},{9,10},{10,11},{12,13},{... | collective-permute-start | bytes 737288 | tf_op jit(solution)/shard_map/ppermute | solution.py:71
  70.0 8.5 %collective-permute-start.15 = (bf16[64,1920]{1,0:T(8,128)(2,1)S(1)}, bf16[64,1920]{1,0:T(8,128)(2,1)S(1)}, u32[]{:S(2)}, u32[]{:S(2)}) collective-permute-start(bf16[64,1920]{1,0:T(8,128)(2,1)S(1)} %pad.7), channel_id=1, source_target_pairs={{3,2},{2,1},{1,0},{7,6},{6,5},{5,4},{11,10},{10,9},{9,8},{15,14},{... | collective-permute-start | bytes 737288 | tf_op jit(solution)/shard_map/ppermute | solution.py:74
  78.7 7.9 %collective-permute-start.13 = (bf16[64,1920]{1,0:T(8,128)(2,1)S(1)}, bf16[64,1920]{1,0:T(8,128)(2,1)S(1)}, u32[]{:S(2)}, u32[]{:S(2)}) collective-permute-start(bf16[64,1920]{1,0:T(8,128)(2,1)S(1)} %get-tuple-element.53), channel_id=1, source_target_pairs={{0,1},{1,2},{2,3},{4,5},{5,6},{6,7},{8,9},{9,10},{10,11},{12,13},{... | collective-permute-start | bytes 737288 | tf_op jit(solution)/shard_map/ppermute | solution.py:71
  82.9 8.1 %collective-permute-start.16 = (bf16[64,1920]{1,0:T(8,128)(2,1)S(1)}, bf16[64,1920]{1,0:T(8,128)(2,1)S(1)}, u32[]{:S(2)}, u32[]{:S(2)}) collective-permute-start(bf16[64,1920]{1,0:T(8,128)(2,1)S(1)} %get-tuple-element.54), channel_id=1, source_target_pairs={{3,2},{2,1},{1,0},{7,6},{6,5},{5,4},{11,10},{10,9},{9,8},{15,14},{... | collective-permute-start | bytes 737288 | tf_op jit(solution)/shard_map/ppermute | solution.py:74
  91.2 7.8 %collective-permute-start.14 = (bf16[64,1920]{1,0:T(8,128)(2,1)S(1)}, bf16[64,1920]{1,0:T(8,128)(2,1)S(1)}, u32[]{:S(2)}, u32[]{:S(2)}) collective-permute-start(bf16[64,1920]{1,0:T(8,128)(2,1)S(1)} %get-tuple-element.51), channel_id=1, source_target_pairs={{0,1},{1,2},{2,3},{4,5},{5,6},{6,7},{8,9},{9,10},{10,11},{12,13},{... | collective-permute-start | bytes 737288 | tf_op jit(solution)/shard_map/ppermute | solution.py:71
  95.1 8.6 %collective-permute-start.17 = (bf16[64,1920]{1,0:T(8,128)(2,1)S(1)}, bf16[64,1920]{1,0:T(8,128)(2,1)S(1)}, u32[]{:S(2)}, u32[]{:S(2)}) collective-permute-start(bf16[64,1920]{1,0:T(8,128)(2,1)S(1)} %get-tuple-element.52), channel_id=1, source_target_pairs={{3,2},{2,1},{1,0},{7,6},{6,5},{5,4},{11,10},{10,9},{9,8},{15,14},{... | collective-permute-start | bytes 737288 | tf_op jit(solution)/shard_map/ppermute | solution.py:74
  105.5 9.3 %collective-permute-start.19 = (bf16[64,1920]{1,0:T(8,128)(2,1)S(1)}, bf16[64,1920]{1,0:T(8,128)(2,1)S(1)}, u32[]{:S(2)}, u32[]{:S(2)}) collective-permute-start(bf16[64,1920]{1,0:T(8,128)(2,1)S(1)} %get-tuple-element.50), channel_id=1, source_target_pairs={{3,2},{2,1},{1,0},{7,6},{6,5},{5,4},{11,10},{10,9},{9,8},{15,14},{... | collective-permute-start | bytes 737288 | tf_op jit(solution)/shard_map/ppermute | solution.py:74
  116.9 10.1 %collective-permute-start.28 = (bf16[64,1792]{1,0:T(8,128)(2,1)S(1)}, bf16[64,1792]{1,0:T(8,128)(2,1)S(1)}, u32[]{:S(2)}, u32[]{:S(2)}) collective-permute-start(bf16[64,1792]{1,0:T(8,128)(2,1)S(1)} %get-tuple-element.29), channel_id=1, source_target_pairs={{3,2},{2,1},{1,0},{7,6},{6,5},{5,4},{11,10},{10,9},{9,8},{15,14},{... | collective-permute-start | bytes 688136 | tf_op jit(solution)/shard_map/ppermute | solution.py:74
  129.4 9.2 %collective-permute-start.29 = (bf16[64,1792]{1,0:T(8,128)(2,1)S(1)}, bf16[64,1792]{1,0:T(8,128)(2,1)S(1)}, u32[]{:S(2)}, u32[]{:S(2)}) collective-permute-start(bf16[64,1792]{1,0:T(8,128)(2,1)S(1)} %get-tuple-element.72), channel_id=1, source_target_pairs={{3,2},{2,1},{1,0},{7,6},{6,5},{5,4},{11,10},{10,9},{9,8},{15,14},{... | collective-permute-start | bytes 688136 | tf_op jit(solution)/shard_map/ppermute | solution.py:74
  141.0 8.4 %collective-permute-start.30 = (bf16[64,1792]{1,0:T(8,128)(2,1)S(1)}, bf16[64,1792]{1,0:T(8,128)(2,1)S(1)}, u32[]{:S(2)}, u32[]{:S(2)}) collective-permute-start(bf16[64,1792]{1,0:T(8,128)(2,1)S(1)} %get-tuple-element.70), channel_id=1, source_target_pairs={{3,2},{2,1},{1,0},{7,6},{6,5},{5,4},{11,10},{10,9},{9,8},{15,14},{... | collective-permute-start | bytes 688136 | tf_op jit(solution)/shard_map/ppermute | solution.py:74
  151.7 7.9 %collective-permute-start.40 = (bf16[64,1792]{1,0:T(8,128)(2,1)S(1)}, bf16[64,1792]{1,0:T(8,128)(2,1)S(1)}, u32[]{:S(2)}, u32[]{:S(2)}) collective-permute-start(bf16[64,1792]{1,0:T(8,128)(2,1)S(1)} %get-tuple-element.68), channel_id=1, source_target_pairs={{3,2},{2,1},{1,0},{7,6},{6,5},{5,4},{11,10},{10,9},{9,8},{15,14},{... | collective-permute-start | bytes 688136 | tf_op jit(solution)/shard_map/ppermute | solution.py:74
  154.6 8.5 %collective-permute-start.31 = (bf16[512,512]{1,0:T(8,128)(2,1)S(1)}, bf16[512,512]{1,0:T(8,128)(2,1)S(1)}, u32[]{:S(2)}, u32[]{:S(2)}) collective-permute-start(bf16[512,512]{1,0:T(8,128)(2,1)S(1)} %broadcast_select_fusion.1), channel_id=1, source_target_pairs={{0,4},{4,0},{8,12},{12,8},{16,20},{20,16},{24,28},{28,24},{1,5},{5... | collective-permute-start | bytes 1572872 | tf_op jit(solution)/shard_map/ppermute | solution.py:65
  161.7 9.5 %collective-permute-start.45 = (bf16[64,1792]{1,0:T(8,128)(2,1)S(1)}, bf16[64,1792]{1,0:T(8,128)(2,1)S(1)}, u32[]{:S(2)}, u32[]{:S(2)}) collective-permute-start(bf16[64,1792]{1,0:T(8,128)(2,1)S(1)} %get-tuple-element.19), channel_id=1, source_target_pairs={{3,2},{2,1},{1,0},{7,6},{6,5},{5,4},{11,10},{10,9},{9,8},{15,14},{... | collective-permute-start | bytes 688136 | tf_op jit(solution)/shard_map/ppermute | solution.py:74
  163.3 11.5 %collective-permute-start.32 = (bf16[128,512]{1,0:T(8,128)(2,1)S(1)}, bf16[128,512]{1,0:T(8,128)(2,1)S(1)}, u32[]{:S(2)}, u32[]{:S(2)}) collective-permute-start(bf16[128,512]{1,0:T(8,128)(2,1)S(1)} %bitcast.411), channel_id=1, source_target_pairs={{0,8},{4,12},{8,0},{12,4},{16,24},{20,28},{24,16},{28,20},{1,9},{5... | collective-permute-start | bytes 393224 | tf_op jit(solution)/shard_map/ppermute | solution.py:68
  164.8 10.0 %collective-permute-start.33 = (bf16[128,512]{1,0:T(8,128)(2,1)S(1)}, bf16[128,512]{1,0:T(8,128)(2,1)S(1)}, u32[]{:S(2)}, u32[]{:S(2)}) collective-permute-start(bf16[128,512]{1,0:T(8,128)(2,1)S(1)} %bitcast.409), channel_id=1, source_target_pairs={{0,16},{4,20},{8,24},{12,28},{16,0},{20,4},{24,8},{28,12},{1,17},{... | collective-permute-start | bytes 393224 | tf_op jit(solution)/shard_map/ppermute | solution.py:68
  164.8 10.1 %collective-permute-start.34 = (bf16[128,512]{1,0:T(8,128)(2,1)S(1)}, bf16[128,512]{1,0:T(8,128)(2,1)S(1)}, u32[]{:S(2)}, u32[]{:S(2)}) collective-permute-start(bf16[128,512]{1,0:T(8,128)(2,1)S(1)} %bitcast.408), channel_id=1, source_target_pairs={{0,24},{4,28},{8,16},{12,20},{16,8},{20,12},{24,0},{28,4},{1,25},{... | collective-permute-start | bytes 393224 | tf_op jit(solution)/shard_map/ppermute | solution.py:68
  173.5 8.7 %collective-permute-start.46 = (bf16[64,1792]{1,0:T(8,128)(2,1)S(1)}, bf16[64,1792]{1,0:T(8,128)(2,1)S(1)}, u32[]{:S(2)}, u32[]{:S(2)}) collective-permute-start(bf16[64,1792]{1,0:T(8,128)(2,1)S(1)} %get-tuple-element.66), channel_id=1, source_target_pairs={{3,2},{2,1},{1,0},{7,6},{6,5},{5,4},{11,10},{10,9},{9,8},{15,14},{... | collective-permute-start | bytes 688136 | tf_op jit(solution)/shard_map/ppermute | solution.py:74
  175.0 10.9 %collective-permute-start.35 = (bf16[128,512]{1,0:T(8,128)(2,1)S(1)}, bf16[128,512]{1,0:T(8,128)(2,1)S(1)}, u32[]{:S(2)}, u32[]{:S(2)}) collective-permute-start(bf16[128,512]{1,0:T(8,128)(2,1)S(1)} %fusion.105), channel_id=1, source_target_pairs={{0,8},{4,12},{8,0},{12,4},{16,24},{20,28},{24,16},{28,20},{1,9},{5... | collective-permute-start | bytes 393224 | tf_op jit(solution)/shard_map/ppermute | solution.py:68
  176.5 9.4 %collective-permute-start.36 = (bf16[128,512]{1,0:T(8,128)(2,1)S(1)}, bf16[128,512]{1,0:T(8,128)(2,1)S(1)}, u32[]{:S(2)}, u32[]{:S(2)}) collective-permute-start(bf16[128,512]{1,0:T(8,128)(2,1)S(1)} %fusion.105), channel_id=1, source_target_pairs={{0,16},{4,20},{8,24},{12,28},{16,0},{20,4},{24,8},{28,12},{1,17},{... | collective-permute-start | bytes 393224 | tf_op jit(solution)/shard_map/ppermute | solution.py:68
  176.5 9.4 %collective-permute-start.37 = (bf16[128,512]{1,0:T(8,128)(2,1)S(1)}, bf16[128,512]{1,0:T(8,128)(2,1)S(1)}, u32[]{:S(2)}, u32[]{:S(2)}) collective-permute-start(bf16[128,512]{1,0:T(8,128)(2,1)S(1)} %fusion.105), channel_id=1, source_target_pairs={{0,24},{4,28},{8,16},{12,20},{16,8},{20,12},{24,0},{28,4},{1,25},{... | collective-permute-start | bytes 393224 | tf_op jit(solution)/shard_map/ppermute | solution.py:68
  184.6 7.9 %collective-permute-start.47 = (bf16[64,1792]{1,0:T(8,128)(2,1)S(1)}, bf16[64,1792]{1,0:T(8,128)(2,1)S(1)}, u32[]{:S(2)}, u32[]{:S(2)}) collective-permute-start(bf16[64,1792]{1,0:T(8,128)(2,1)S(1)} %get-tuple-element.64), channel_id=1, source_target_pairs={{3,2},{2,1},{1,0},{7,6},{6,5},{5,4},{11,10},{10,9},{9,8},{15,14},{... | collective-permute-start | bytes 688136 | tf_op jit(solution)/shard_map/ppermute | solution.py:74
  186.0 20.0 %collective-permute-start.38 = (bf16[512,512]{1,0:T(8,128)(2,1)S(1)}, bf16[512,512]{1,0:T(8,128)(2,1)S(1)}, u32[]{:S(2)}, u32[]{:S(2)}) collective-permute-start(bf16[512,512]{1,0:T(8,128)(2,1)S(1)} %bitcast.384), channel_id=1, source_target_pairs={{0,4},{4,0},{8,12},{12,8},{16,20},{20,16},{24,28},{28,24},{1,5},{5... | collective-permute-start | bytes 1572872 | tf_op jit(solution)/shard_map/ppermute | solution.py:65
  194.7 7.9 %collective-permute-start.48 = (bf16[64,1792]{1,0:T(8,128)(2,1)S(1)}, bf16[64,1792]{1,0:T(8,128)(2,1)S(1)}, u32[]{:S(2)}, u32[]{:S(2)}) collective-permute-start(bf16[64,1792]{1,0:T(8,128)(2,1)S(1)} %get-tuple-element.62), channel_id=1, source_target_pairs={{3,2},{2,1},{1,0},{7,6},{6,5},{5,4},{11,10},{10,9},{9,8},{15,14},{... | collective-permute-start | bytes 688136 | tf_op jit(solution)/shard_map/ppermute | solution.py:74
  204.7 8.1 %collective-permute-start.53 = (bf16[64,1920]{1,0:T(8,128)(2,1)S(1)}, bf16[64,1920]{1,0:T(8,128)(2,1)S(1)}, u32[]{:S(2)}, u32[]{:S(2)}) collective-permute-start(bf16[64,1920]{1,0:T(8,128)(2,1)S(1)} %pad.8), channel_id=1, source_target_pairs={{3,2},{2,1},{1,0},{7,6},{6,5},{5,4},{11,10},{10,9},{9,8},{15,14},{... | collective-permute-start | bytes 737288 | tf_op jit(solution)/shard_map/ppermute | solution.py:74
  214.8 8.1 %collective-permute-start.54 = (bf16[64,1920]{1,0:T(8,128)(2,1)S(1)}, bf16[64,1920]{1,0:T(8,128)(2,1)S(1)}, u32[]{:S(2)}, u32[]{:S(2)}) collective-permute-start(bf16[64,1920]{1,0:T(8,128)(2,1)S(1)} %get-tuple-element.48), channel_id=1, source_target_pairs={{3,2},{2,1},{1,0},{7,6},{6,5},{5,4},{11,10},{10,9},{9,8},{15,14},{... | collective-permute-start | bytes 737288 | tf_op jit(solution)/shard_map/ppermute | solution.py:74
  223.1 16.6 %collective-permute-start.51 = (bf16[64,1920]{1,0:T(8,128)(2,1)S(1)}, bf16[64,1920]{1,0:T(8,128)(2,1)S(1)}, u32[]{:S(2)}, u32[]{:S(2)}) collective-permute-start(bf16[64,1920]{1,0:T(8,128)(2,1)S(1)} %get-tuple-element.45), channel_id=1, source_target_pairs={{0,1},{1,2},{2,3},{4,5},{5,6},{6,7},{8,9},{9,10},{10,11},{12,13},{... | collective-permute-start | bytes 737288 | tf_op jit(solution)/shard_map/ppermute | solution.py:71
  225.0 14.7 %collective-permute-start.55 = (bf16[64,1920]{1,0:T(8,128)(2,1)S(1)}, bf16[64,1920]{1,0:T(8,128)(2,1)S(1)}, u32[]{:S(2)}, u32[]{:S(2)}) collective-permute-start(bf16[64,1920]{1,0:T(8,128)(2,1)S(1)} %get-tuple-element.46), channel_id=1, source_target_pairs={{3,2},{2,1},{1,0},{7,6},{6,5},{5,4},{11,10},{10,9},{9,8},{15,14},{... | collective-permute-start | bytes 737288 | tf_op jit(solution)/shard_map/ppermute | solution.py:74
  239.9 8.2 %collective-permute-start.52 = (bf16[64,1920]{1,0:T(8,128)(2,1)S(1)}, bf16[64,1920]{1,0:T(8,128)(2,1)S(1)}, u32[]{:S(2)}, u32[]{:S(2)}) collective-permute-start(bf16[64,1920]{1,0:T(8,128)(2,1)S(1)} %get-tuple-element.43), channel_id=1, source_target_pairs={{0,1},{1,2},{2,3},{4,5},{5,6},{6,7},{8,9},{9,10},{10,11},{12,13},{... | collective-permute-start | bytes 737288 | tf_op jit(solution)/shard_map/ppermute | solution.py:71
  244.5 8.1 %collective-permute-start.56 = (bf16[64,1920]{1,0:T(8,128)(2,1)S(1)}, bf16[64,1920]{1,0:T(8,128)(2,1)S(1)}, u32[]{:S(2)}, u32[]{:S(2)}) collective-permute-start(bf16[64,1920]{1,0:T(8,128)(2,1)S(1)} %get-tuple-element.44), channel_id=1, source_target_pairs={{3,2},{2,1},{1,0},{7,6},{6,5},{5,4},{11,10},{10,9},{9,8},{15,14},{... | collective-permute-start | bytes 737288 | tf_op jit(solution)/shard_map/ppermute | solution.py:74
  255.2 9.8 %collective-permute-start.60 = (bf16[64,1920]{1,0:T(8,128)(2,1)S(1)}, bf16[64,1920]{1,0:T(8,128)(2,1)S(1)}, u32[]{:S(2)}, u32[]{:S(2)}) collective-permute-start(bf16[64,1920]{1,0:T(8,128)(2,1)S(1)} %concatenate.94), channel_id=1, source_target_pairs={{3,2},{2,1},{1,0},{7,6},{6,5},{5,4},{11,10},{10,9},{9,8},{15,14},{... | collective-permute-start | bytes 737288 | tf_op jit(solution)/shard_map/ppermute | solution.py:74
  265.2 7.7 %collective-permute-start.58 = (bf16[64,1920]{1,0:T(8,128)(2,1)S(1)}, bf16[64,1920]{1,0:T(8,128)(2,1)S(1)}, u32[]{:S(2)}, u32[]{:S(2)}) collective-permute-start(bf16[64,1920]{1,0:T(8,128)(2,1)S(1)} %get-tuple-element.41), channel_id=1, source_target_pairs={{0,1},{1,2},{2,3},{4,5},{5,6},{6,7},{8,9},{9,10},{10,11},{12,13},{... | collective-permute-start | bytes 737288 | tf_op jit(solution)/shard_map/ppermute | solution.py:71
  266.8 10.7 %collective-permute-start.61 = (bf16[64,1920]{1,0:T(8,128)(2,1)S(1)}, bf16[64,1920]{1,0:T(8,128)(2,1)S(1)}, u32[]{:S(2)}, u32[]{:S(2)}) collective-permute-start(bf16[64,1920]{1,0:T(8,128)(2,1)S(1)} %get-tuple-element.42), channel_id=1, source_target_pairs={{3,2},{2,1},{1,0},{7,6},{6,5},{5,4},{11,10},{10,9},{9,8},{15,14},{... | collective-permute-start | bytes 737288 | tf_op jit(solution)/shard_map/ppermute | solution.py:74
  279.6 9.4 %collective-permute-start.62 = (bf16[64,1920]{1,0:T(8,128)(2,1)S(1)}, bf16[64,1920]{1,0:T(8,128)(2,1)S(1)}, u32[]{:S(2)}, u32[]{:S(2)}) collective-permute-start(bf16[64,1920]{1,0:T(8,128)(2,1)S(1)} %get-tuple-element.40), channel_id=1, source_target_pairs={{3,2},{2,1},{1,0},{7,6},{6,5},{5,4},{11,10},{10,9},{9,8},{15,14},{... | collective-permute-start | bytes 737288 | tf_op jit(solution)/shard_map/ppermute | solution.py:74
  291.4 10.2 %collective-permute-start.64 = (bf16[64,1920]{1,0:T(8,128)(2,1)S(1)}, bf16[64,1920]{1,0:T(8,128)(2,1)S(1)}, u32[]{:S(2)}, u32[]{:S(2)}) collective-permute-start(bf16[64,1920]{1,0:T(8,128)(2,1)S(1)} %get-tuple-element.38), channel_id=1, source_target_pairs={{3,2},{2,1},{1,0},{7,6},{6,5},{5,4},{11,10},{10,9},{9,8},{15,14},{... | collective-permute-start | bytes 737288 | tf_op jit(solution)/shard_map/ppermute | solution.py:74
  305.6 9.0 %collective-permute-start.68 = (bf16[64,1920]{1,0:T(8,128)(2,1)S(1)}, bf16[64,1920]{1,0:T(8,128)(2,1)S(1)}, u32[]{:S(2)}, u32[]{:S(2)}) collective-permute-start(bf16[64,1920]{1,0:T(8,128)(2,1)S(1)} %concatenate.96), channel_id=1, source_target_pairs={{3,2},{2,1},{1,0},{7,6},{6,5},{5,4},{11,10},{10,9},{9,8},{15,14},{... | collective-permute-start | bytes 737288 | tf_op jit(solution)/shard_map/ppermute | solution.py:74
  314.6 8.1 %collective-permute-start.69 = (bf16[64,1920]{1,0:T(8,128)(2,1)S(1)}, bf16[64,1920]{1,0:T(8,128)(2,1)S(1)}, u32[]{:S(2)}, u32[]{:S(2)}) collective-permute-start(bf16[64,1920]{1,0:T(8,128)(2,1)S(1)} %collective-permute-done.68), channel_id=1, source_target_pairs={{2,1},{1,0},{6,5},{5,4},{10,9},{9,8},{14,13},{13,12},{18,17},{17,1... | collective-permute-start | bytes 737288 | tf_op jit(solution)/shard_map/ppermute | solution.py:74
  315.9 8.1 %collective-permute-start.67 = (bf16[64,1920]{1,0:T(8,128)(2,1)S(1)}, bf16[64,1920]{1,0:T(8,128)(2,1)S(1)}, u32[]{:S(2)}, u32[]{:S(2)}) collective-permute-start(bf16[64,1920]{1,0:T(8,128)(2,1)S(1)} %collective-permute-done.66), channel_id=1, source_target_pairs={{2,3},{6,7},{10,11},{14,15},{18,19},{22,23},{26,27},{30,31}} | collective-permute-start | bytes 737288 | tf_op jit(solution)/shard_map/ppermute | solution.py:71
  322.7 8.1 %collective-permute-start.70 = (bf16[64,1920]{1,0:T(8,128)(2,1)S(1)}, bf16[64,1920]{1,0:T(8,128)(2,1)S(1)}, u32[]{:S(2)}, u32[]{:S(2)}) collective-permute-start(bf16[64,1920]{1,0:T(8,128)(2,1)S(1)} %collective-permute-done.69), channel_id=1, source_target_pairs={{1,0},{5,4},{9,8},{13,12},{17,16},{21,20},{25,24},{29,28}} | collective-permute-start | bytes 737288 | tf_op jit(solution)/shard_map/ppermute | solution.py:74
  339.7 19.4 %collective-permute-start.71 = (bf16[512,512]{1,0:T(8,128)(2,1)S(1)}, bf16[512,512]{1,0:T(8,128)(2,1)S(1)}, u32[]{:S(2)}, u32[]{:S(2)}) collective-permute-start(bf16[512,512]{1,0:T(8,128)(2,1)S(1)} %broadcast_select_fusion), channel_id=1, source_target_pairs={{0,4},{4,0},{8,12},{12,8},{16,20},{20,16},{24,28},{28,24},{1,5},{5... | collective-permute-start | bytes 1572872 | tf_op jit(solution)/shard_map/ppermute | solution.py:65
  358.3 12.1 %collective-permute-start.83 = (bf16[256,512]{1,0:T(8,128)(2,1)S(1)}, bf16[256,512]{1,0:T(8,128)(2,1)S(1)}, u32[]{:S(2)}, u32[]{:S(2)}) collective-permute-start(bf16[256,512]{1,0:T(8,128)(2,1)S(1)} %bitcast.393), channel_id=1, source_target_pairs={{0,4},{4,0},{8,12},{12,8},{16,20},{20,16},{24,28},{28,24},{1,5},{5... | collective-permute-start | bytes 786440 | tf_op jit(solution)/shard_map/ppermute | solution.py:65
  368.5 11.7 %collective-permute-start.75 = (bf16[128,512]{1,0:T(8,128)(2,1)S(1)}, bf16[128,512]{1,0:T(8,128)(2,1)S(1)}, u32[]{:S(2)}, u32[]{:S(2)}) collective-permute-start(bf16[128,512]{1,0:T(8,128)(2,1)S(1)} %fusion.101), channel_id=1, source_target_pairs={{0,0},{1,8},{2,16},{3,24},{4,4},{5,12},{6,20},{7,28},{8,1},{9,9},{... | collective-permute-start | bytes 393224 | tf_op jit(solution)/shard_map/ppermute | solution.py:62
  (73 other events, 703.2 us)

commit v4 on v3

--- a/solution.py
+++ b/solution.py
@@ -5,7 +5,7 @@
 
 LANES = 128
 PAD = 16
-CHUNKS = 2
+CHUNKS = 1
 epsilon = 1e-05
 F32 = jnp.float32
 BF16 = jnp.bfloat16
@@ -49,7 +49,6 @@
     z = lax.axis_index("local")
     node = lax.axis_index("node")
     chip, core = node // halves, node % halves
-    last = n_local - 1
 
     swap = [
         ((halves * c + j) * n_local + l, (halves * l + j) * n_local + c)
@@ -66,12 +65,6 @@
 
     def chip_swap(block, shift):
         return lax.ppermute(block, "node", [(n, n ^ (2 * shift)) for n in range(n_node)])
-
-    def send_right(block, senders):
-        return lax.ppermute(block, "local", [(s, s + 1) for s in senders])
-
-    def send_left(block, senders):
-        return lax.ppermute(block, "local", [(last - s, last - 1 - s) for s in senders])
 
     def take(array, index):
         width = array.shape[1]
@@ -111,48 +104,24 @@
             total = total + chip_swap(take(both, chip ^ shift), shift).astype(F32)
         return total
 
-    def line(block, partial):
-        right = left = None
-        rights, lefts = [], []
-        everyone = range(last)
-        if block is not None:
-            right, left = send_right(block, everyone), send_left(block, everyone)
-            rights.append(right)
-            lefts.append(left)
-            if partial is None:
-                for step in range(1, last):
-                    right = send_right(right, range(step, last))
-                    left = send_left(left, range(step, last))
-                    rights.append(right)
-                    lefts.append(left)
-        total = None
-        if partial is not None:
-            for step in range(1, n_local):
-                to_right = take(partial, jnp.minimum(z + n_local - step, last))
-                to_left = take(partial, jnp.maximum(z - n_local + step, 0))
-                if right is not None:
-                    zero = jnp.zeros((), F32)
-                    to_right = jnp.where(z < step, to_right.astype(F32), zero)
-                    to_left = jnp.where(last - z < step, to_left.astype(F32), zero)
-                    to_right = (right.astype(F32) + to_right).astype(BF16)
-                    to_left = (left.astype(F32) + to_left).astype(BF16)
-                senders = everyone if block is not None else range(step)
-                right, left = send_right(to_right, senders), send_left(to_left, senders)
-                rights.append(right)
-                lefts.append(left)
-            total = take(partial, z).astype(F32) + right.astype(F32) + left.astype(F32)
-        out = None
-        if block is not None:
-            out = jnp.zeros((part * n_local, block.shape[1]), block.dtype)
-            out = put(out, block, z)
-            for ahead in range(1, n_local):
-                behind = n_local - ahead
-                piece = jnp.where(z >= behind, rights[behind - 1], lefts[ahead - 1])
-                out = put(out, piece, (z + ahead) % n_local)
-        return out, total
-
-    def widen(block):
-        return jnp.pad(block, ((0, 0), (0, LANES)))
+    def ring(block):
+        return lax.ppermute(block, "local", [(s, (s + 1) % n_local) for s in range(n_local)])
+
+    def ring_reduce(partial):
+        moving = take(partial, (z - 1) % n_local)
+        for step in range(2, n_local + 1):
+            moving = ring(moving).astype(F32) + take(partial, (z - step) % n_local).astype(F32)
+            if step < n_local:
+                moving = moving.astype(BF16)
+        return moving
+
+    def ring_gather(block):
+        out = jnp.zeros((part * n_local, block.shape[1]), block.dtype)
+        out = put(out, block, z)
+        for step in range(1, n_local):
+            block = ring(block)
+            out = put(out, block, (z - step) % n_local)
+        return out
 
     def chunk_of(array, h):
         size = part * n_local
@@ -179,55 +148,49 @@
     g_home = exchange(cotangent)
 
     x = gather_node(x_home)
-    partials = [up_partial(chunk_of(x, h)) for h in range(CHUNKS)]
-    _, total = line(None, partials[0])
-    hidden_own = jax.nn.silu(finish_pre(total)[0]).astype(BF16)
-    hidden_a, total = line(widen(hidden_own), partials[1])
-    hidden_a = hidden_a[:, :hidden_units]
-    hidden_own = jax.nn.silu(finish_pre(total)[0]).astype(BF16)
-
     g = gather_node(g_home)
     slopes = [
         dot(chunk_of(g, h), down_weight, ((1,), (1,))).astype(BF16) for h in range(CHUNKS)
     ]
-    hidden_b, total = line(hidden_own, slopes[0])
-    hidden_first = [hidden_a, hidden_b]
-    updates = [dot(hidden, down_weight, ((1,), (0,))).astype(BF16) for hidden in hidden_first]
+    hidden_first, updates = [], []
+    for h in range(CHUNKS):
+        pre, _ = finish_pre(ring_reduce(up_partial(chunk_of(x, h))))
+        hidden = jax.nn.silu(pre).astype(BF16)
+        hidden, slopes[h] = lax.optimization_barrier((hidden, slopes[h]))
+        slopes[h] = lax.psum_scatter(slopes[h], "local", scatter_dimension=0, tiled=True)
+        hidden = ring_gather(hidden)
+        hidden_first.append(hidden)
+        updates.append(dot(hidden, down_weight, ((1,), (0,))).astype(BF16))
     update = scatter_node(jnp.concatenate(updates, axis=0))
     x1_home = (x_home.astype(F32) + update).astype(BF16)
-    slope_a, total = line(total.astype(BF16), slopes[1])
+    x1_home, slopes = lax.optimization_barrier((x1_home, slopes))
+    slopes = [lax.all_gather(slope, "local", axis=0, tiled=True) for slope in slopes]
 
     x = gather_node(x1_home)
-    partials = [up_partial(chunk_of(x, h)) for h in range(CHUNKS)]
-    slope_b, total = line(widen(total.astype(BF16)), partials[0])
-    slope_b = slope_b[:, :hidden_units]
-
-    def pack_pre(total):
-        pre, factor = finish_pre(total)
-        return jnp.concatenate([pre.astype(BF16)] + split_pair(factor), axis=1)
-
-    packed_a, total = line(pack_pre(total), partials[1])
-    packed_b, _ = line(pack_pre(total), None)
-
-    hidden_second, below = [], []
-    for h, (packed, slope) in enumerate([(packed_a, slope_a), (packed_b, slope_b)]):
+    hidden_second, grads, updates = [], [], []
+    for h in range(CHUNKS):
+        pre, factor = finish_pre(ring_reduce(up_partial(chunk_of(x, h))))
+        packed = jnp.concatenate([pre.astype(BF16)] + split_pair(factor), axis=1)
+        packed = ring_gather(packed)
         pre = packed[:, :hidden_units].astype(F32)
         sigma = jax.nn.sigmoid(pre)
         hidden_second.append((pre * sigma).astype(BF16))
-        pre_grad = slope.astype(F32) * sigma * (1.0 + pre * (1.0 - sigma))
+        pre_grad = slopes[h].astype(F32) * sigma * (1.0 + pre * (1.0 - sigma))
         inner = jnp.sum(pre_grad * pre, axis=-1, keepdims=True)
         normed_grad = dot(pre_grad.astype(BF16), up_weight, ((1,), (1,))).astype(BF16)
         total = scatter_node(normed_grad, split_pair(inner))
         factor = join_pair(take(packed[:, hidden_units:], chip))
         inner = join_pair(total[:, cols:]) / (features * factor)
-        back = factor * (total[:, :cols] * gains_home) - chunk_home(x1_home, h, part).astype(F32) * (
-            factor * factor * factor * inner
-        )
-        grad_home = (chunk_home(g_home, h, part).astype(F32) + back).astype(BF16)
-        below.append(gather_node(grad_home))
-    updates = [dot(hidden, down_weight, ((1,), (0,))).astype(BF16) for hidden in hidden_second]
+        before = chunk_home(x1_home, h, part).astype(F32)
+        back = factor * (total[:, :cols] * gains_home) - before * (factor**3 * inner)
+        grads.append((chunk_home(g_home, h, part).astype(F32) + back).astype(BF16))
+        updates.append(dot(hidden_second[h], down_weight, ((1,), (0,))).astype(BF16))
     update = scatter_node(jnp.concatenate(updates, axis=0))
-    result = exchange((x1_home.astype(F32) + update).astype(BF16))
+    x2_home = (x1_home.astype(F32) + update).astype(BF16)
+    x2_home, grads = lax.optimization_barrier((x2_home, grads))
+    result = exchange(x2_home)
+    below = [gather_node(grad) for grad in grads]
+    result, below = lax.optimization_barrier((result, below))
     grad_down = dot(
         jnp.concatenate(hidden_first + hidden_second, axis=0),
         jnp.concatenate(below + [g], axis=0),

time: 386 us -> 369 us (0.956); the launches traced: 381 us -> 368 us
  starting transfers between devices: 148 us -> 39.8 us
  waiting for transfers between devices: 176 us -> 255 us
  between operations: 2.92 us -> 15 us
  matrix products: 19.7 us -> 28.7 us
    ppermute x52 -> x12, starting transfers between devices: 109 us -> 4.23 us  [ring(): lax.ppermute(block, 'local', [(s, (s + 1) % n_local) for s in range(n_loc...]
    ppermute x52 -> x12, waiting for transfers between devices: 150 us -> 198 us  [ring(): lax.ppermute(block, 'local', [(s, (s + 1) % n_local) for s in range(n_loc...]
    ppermute x3, waiting for transfers between devices: 9.14 us -> 23.7 us  [exchange(): return lax.ppermute(block, ('node', 'local'), swap)]
    ppermute x27 -> x21, waiting for transfers between devices: 16.6 us -> 28.6 us  [chip_swap(): lax.ppermute(block, 'node', [(n, n ^ 2 * shift) for n in range(n_node)])]
    dot_general x13 -> x7, matrix products: 19.7 us -> 28.7 us  [dot(): lax.dot_general(left, right, (dims, ((), ())), preferred_element_type=F32)]
    ppermute x10 -> x8, waiting for transfers between devices: 0.45 us -> 4.79 us  [core_swap(): return lax.ppermute(block, 'node', [(n, n ^ 1) for n in range(n_node)])]
    ppermute x27 -> x21, starting transfers between devices: 30.1 us -> 26.2 us  [chip_swap(): lax.ppermute(block, 'node', [(n, n ^ 2 * shift) for n in range(n_node)])]
  transfers between devices with their start and end apart: 92 -> 46, of which waited for: 57 -> 29; matrix products, arithmetic and copies ran while one was open for 10% -> 9% of each run, Pallas kernels for 0% -> 0%
where the time goes in v4:
time: 369 us; the launch traced here: 368 us
  waiting for transfers between devices  255 us (69%)
  starting transfers between devices  39.8 us (11%)
  matrix products  28.7 us (8%)
  other arithmetic  21.2 us (6%)
  between operations  15 us (4%)
  local copies, waits for them, and re-layouts  8.27 us (2%)
    ppermute x12, waiting for transfers between devices, ring(): lax.ppermute(block, 'local', [(s, (s + 1) % n_local) for s in range(n_loc...  198 us
    dot_general x7, matrix products, dot(): lax.dot_general(left, right, (dims, ((), ())), preferred_element_type=F32)  28.7 us
    ppermute x21, waiting for transfers between devices, chip_swap(): lax.ppermute(block, 'node', [(n, n ^ 2 * shift) for n in range(n_node)])  28.6 us
    ppermute x21, starting transfers between devices, chip_swap(): lax.ppermute(block, 'node', [(n, n ^ 2 * shift) for n in range(n_node)])  26.2 us
    ppermute x3, waiting for transfers between devices, exchange(): return lax.ppermute(block, ('node', 'local'), swap)  23.7 us
    ppermute x3, starting transfers between devices, exchange(): return lax.ppermute(block, ('node', 'local'), swap)  8.01 us
  transfers between devices with their start and end apart: 46, of which 29 were waited for; matrix products, arithmetic and copies ran while one was open for 9% of the time, Pallas kernels for 0%

profile of v4, /device:TPU:2, one launch (start us, length us, event | category | flops | bytes accessed | tf_op | source)
XLA Modules:
  0.0 368.4 jit_solution(12638865131171178316)
XLA Ops:
  8.8 3.5 collective-permute-start
  13.3 2.0 mul.126
  15.3 3.7 %fusion = bf16[1792,1024]{1,0:T(8,128)(2,1)} fusion(f32[224,8,8,128]{3,2,1,0:T(8,128)S(1)} %bitcast.135, bf16[1792,1024]{1,0:T(8,128)(2,1)S(1)} %copy-done), kind=kLoop, calls=%fused_computation.1 | loop fusion | flops 5505024 | bytes 14680064 | tf_op jit(solution)/shard_map/convert_element_type | solution.py:23
  19.1 4.6 %fusion.1 = bf16[1024,1792]{1,0:T(8,128)(2,1)} fusion(bf16[1024,1792]{1,0:T(8,128)(2,1)} %param.10, f32[8,1792]{1,0:T(8,128)S(1)} %convert_element_type.301), kind=kLoop, calls=%fused_computation.3 | loop fusion | flops 5505024 | bytes 7397376 | tf_op jit(solution)/shard_map/convert_element_type | solution.py:17
  23.8 3.6 collective-permute-start.2
  28.8 3.8 %collective-permute-done.2 = bf16[128,512]{1,0:T(8,128)(2,1)S(1)} collective-permute-done((bf16[128,512]{1,0:T(8,128)(2,1)S(1)}, bf16[128,512]{1,0:T(8,128)(2,1)S(1)}, u32[]{:S(2)}, u32[]{:S(2)}) %collective-permute-start.2) | collective-permute-done | bytes 131104 | tf_op jit(solution)/shard_map/ppermute | solution.py:67
  32.6 1.8 collective-permute-done.3
  34.6 2.6 collective-permute-start.9
  37.3 11.6 %collective-permute-done.9 = bf16[128,512]{1,0:T(8,128)(2,1)S(1)} collective-permute-done((bf16[128,512]{1,0:T(8,128)(2,1)S(1)}, bf16[128,512]{1,0:T(8,128)(2,1)S(1)}, u32[]{:S(2)}, u32[]{:S(2)}) %collective-permute-start.9) | collective-permute-done | bytes 131104 | tf_op jit(solution)/shard_map/ppermute | solution.py:61
  49.4 3.0 collective-permute-start.12
  55.3 4.1 %convolution_convert_fusion.3 = bf16[512,1792]{1,0:T(8,128)(2,1)S(1)} fusion(bf16[1024,1792]{1,0:T(8,128)(2,1)} %fusion.1, bf16[512,512]{1,0:T(8,128)(2,1)S(1)} %collective-permute-done.4, bf16[512,512]{1,0:T(8,128)(2,1)S(1)} %bitcast.159, f32[1024]{0:T(1024)S(1)} %bitcast.166, pred[]{:T(512)S(6)} %eq.29), kind=kOutput, calls=%fused_computation.21 | convolution fusion | flops 1886257152 | bytes 6557697 | tf_op jit(solution)/shard_map/dot_general | solution.py:27
  60.9 13.8 %collective-permute-done.6 = bf16[128,1920]{1,0:T(8,128)(2,1)S(1)} collective-permute-done((bf16[128,1920]{1,0:T(8,128)(2,1)S(1)}, bf16[128,1920]{1,0:T(8,128)(2,1)S(1)}, u32[]{:S(2)}, u32[]{:S(2)}) %collective-permute-start.6) | collective-permute-done | bytes 491552 | tf_op jit(solution)/shard_map/ppermute | solution.py:108
  76.0 14.2 %collective-permute-done.7 = bf16[128,1920]{1,0:T(8,128)(2,1)} collective-permute-done((bf16[128,1920]{1,0:T(8,128)(2,1)}, bf16[128,1920]{1,0:T(8,128)(2,1)}, u32[]{:S(2)}, u32[]{:S(2)}) %collective-permute-start.7) | collective-permute-done | bytes 491552 | tf_op jit(solution)/shard_map/ppermute | solution.py:108
  91.5 5.4 %convolution_convert_fusion.2 = bf16[512,1792]{1,0:T(8,128)(2,1)} fusion(bf16[512,1024]{1,0:T(8,128)(2,1)S(1)} %maximum_select_fusion.3, bf16[1792,1024]{1,0:T(8,128)(2,1)} %fusion), kind=kOutput, calls=%fused_computation.20 | convolution fusion | flops 1879965696 | bytes 6553600 | tf_op jit(solution)/shard_map/dot_general | solution.py:27
  96.9 7.9 %collective-permute-done.8 = bf16[128,1920]{1,0:T(8,128)(2,1)S(1)} collective-permute-done((bf16[128,1920]{1,0:T(8,128)(2,1)S(1)}, bf16[128,1920]{1,0:T(8,128)(2,1)S(1)}, u32[]{:S(2)}, u32[]{:S(2)}) %collective-permute-start.8) | collective-permute-done | bytes 491552 | tf_op jit(solution)/shard_map/ppermute | solution.py:108
  105.9 14.1 %collective-permute-done.14 = bf16[128,1792]{1,0:T(8,128)(2,1)S(1)} collective-permute-done((bf16[128,1792]{1,0:T(8,128)(2,1)S(1)}, bf16[128,1792]{1,0:T(8,128)(2,1)S(1)}, u32[]{:S(2)}, u32[]{:S(2)}) %collective-permute-start.14) | collective-permute-done | bytes 458784 | tf_op jit(solution)/shard_map/ppermute | solution.py:108
  120.0 23.5 %collective-permute-done.15 = bf16[128,1792]{1,0:T(8,128)(2,1)S(1)} collective-permute-done((bf16[128,1792]{1,0:T(8,128)(2,1)S(1)}, bf16[128,1792]{1,0:T(8,128)(2,1)S(1)}, u32[]{:S(2)}, u32[]{:S(2)}) %collective-permute-start.15) | collective-permute-done | bytes 458784 | tf_op jit(solution)/shard_map/ppermute | solution.py:108
  143.7 22.6 %collective-permute-done.16 = bf16[128,1792]{1,0:T(8,128)(2,1)S(1)} collective-permute-done((bf16[128,1792]{1,0:T(8,128)(2,1)S(1)}, bf16[128,1792]{1,0:T(8,128)(2,1)S(1)}, u32[]{:S(2)}, u32[]{:S(2)}) %collective-permute-start.16) | collective-permute-done | bytes 458784 | tf_op jit(solution)/shard_map/ppermute | solution.py:108
  166.4 2.1 convolution_convert_fusion.5
  168.6 1.9 collective-permute-done.17
  170.9 3.4 collective-permute-start.20
  174.3 2.8 collective-permute-done.18
  177.1 2.1 collective-permute-done.19
  179.4 1.7 collective-permute-start.21
  183.0 2.1 collective-permute-done.21
  185.2 3.0 collective-permute-done.22
  188.4 1.8 collective-permute-done.24
  191.8 4.1 %convolution_convert_fusion.1 = bf16[512,1792]{1,0:T(8,128)(2,1)S(1)} fusion(bf16[1024,1792]{1,0:T(8,128)(2,1)} %fusion.1, bf16[512,512]{1,0:T(8,128)(2,1)S(1)} %collective-permute-done.24, bf16[512,512]{1,0:T(8,128)(2,1)S(1)} %bitcast.161, f32[1024]{0:T(1024)S(1)} %bitcast.167, pred[]{:T(512)S(6)} %eq.29), kind=kOutput, calls=%fused_computation.19 | convolution fusion | flops 1886257152 | bytes 6557697 | tf_op jit(solution)/shard_map/dot_general | solution.py:27
  196.2 15.0 %collective-permute-done.25 = bf16[128,1920]{1,0:T(8,128)(2,1)S(1)} collective-permute-done((bf16[128,1920]{1,0:T(8,128)(2,1)S(1)}, bf16[128,1920]{1,0:T(8,128)(2,1)S(1)}, u32[]{:S(2)}, u32[]{:S(2)}) %collective-permute-start.25) | collective-permute-done | bytes 491552 | tf_op jit(solution)/shard_map/ppermute | solution.py:108
  211.4 14.2 %collective-permute-done.26 = bf16[128,1920]{1,0:T(8,128)(2,1)S(1)} collective-permute-done((bf16[128,1920]{1,0:T(8,128)(2,1)S(1)}, bf16[128,1920]{1,0:T(8,128)(2,1)S(1)}, u32[]{:S(2)}, u32[]{:S(2)}) %collective-permute-start.26) | collective-permute-done | bytes 491552 | tf_op jit(solution)/shard_map/ppermute | solution.py:108
  226.6 13.8 %collective-permute-done.27 = bf16[128,1920]{1,0:T(8,128)(2,1)S(1)} collective-permute-done((bf16[128,1920]{1,0:T(8,128)(2,1)}, bf16[128,1920]{1,0:T(8,128)(2,1)S(1)}, u32[]{:S(2)}, u32[]{:S(2)}) %collective-permute-start.27) | collective-permute-done | bytes 491552 | tf_op jit(solution)/shard_map/ppermute | solution.py:108
  241.1 25.1 %collective-permute-done.28 = bf16[128,1920]{1,0:T(8,128)(2,1)S(1)} collective-permute-done((bf16[128,1920]{1,0:T(8,128)(2,1)S(1)}, bf16[128,1920]{1,0:T(8,128)(2,1)S(1)}, u32[]{:S(2)}, u32[]{:S(2)}) %collective-permute-start.28) | collective-permute-done | bytes 491552 | tf_op jit(solution)/shard_map/ppermute | solution.py:108
  266.2 3.6 collective-permute-start.29
  270.1 20.8 %collective-permute-done.29 = bf16[128,1920]{1,0:T(8,128)(2,1)S(1)} collective-permute-done((bf16[128,1920]{1,0:T(8,128)(2,1)S(1)}, bf16[128,1920]{1,0:T(8,128)(2,1)S(1)}, u32[]{:S(2)}, u32[]{:S(2)}) %collective-permute-start.29) | collective-permute-done | bytes 491552 | tf_op jit(solution)/shard_map/ppermute | solution.py:108
  291.0 13.1 %collective-permute-done.30 = bf16[128,1920]{1,0:T(8,128)(2,1)S(1)} collective-permute-done((bf16[128,1920]{1,0:T(8,128)(2,1)S(1)}, bf16[128,1920]{1,0:T(8,128)(2,1)S(1)}, u32[]{:S(2)}, u32[]{:S(2)}) %collective-permute-start.30) | collective-permute-done | bytes 491552 | tf_op jit(solution)/shard_map/ppermute | solution.py:108
  304.2 5.4 %fusion.17 = bf16[512,1024]{1,0:T(8,128)(2,1)S(1)} fusion(bf16[1024,1792]{1,0:T(8,128)(2,1)} %fusion.1, bf16[512,1792]{1,0:T(8,128)(2,1)} %all-gather.2.cloned.1.call-done, bf16[512,1920]{1,0:T(8,128)(2,1)S(1)} %bitcast.144), kind=kOutput, calls=%fused_computation.33 | convolution fusion | flops 1889665024 | bytes 8388608 | tf_op jit(solution)/shard_map/dot_general | solution.py:27
  311.1 2.0 fusion.5
  313.6 2.1 convolution_convert_fusion.4
  325.2 2.3 collective-permute-done.37
  327.8 2.4 collective-permute-done.32
  330.2 2.1 collective-permute-done.33
  332.5 1.6 collective-permute-start.40
  334.4 1.6 collective-permute-start.42
  336.1 2.5 collective-permute-done.40
  338.6 2.4 collective-permute-done.41
  341.1 1.9 collective-permute-start.39
  343.3 12.1 %collective-permute-done.39 = bf16[128,512]{1,0:T(8,128)(2,1)S(1)} collective-permute-done((bf16[128,512]{1,0:T(8,128)(2,1)S(1)}, bf16[128,512]{1,0:T(8,128)(2,1)S(1)}, u32[]{:S(2)}, u32[]{:S(2)}) %collective-permute-start.39) | collective-permute-done | bytes 131104 | tf_op jit(solution)/shard_map/ppermute | solution.py:61
  355.4 5.5 %convolution_convert_fusion = bf16[1792,1024]{1,0:T(8,128)(2,1)} fusion(bf16[512,1792]{1,0:T(8,128)(2,1)S(1)} %get-tuple-element.30, bf16[512,1792]{1,0:T(8,128)(2,1)S(1)} %bitcast.163, bf16[512,1024]{1,0:T(8,128)(2,1)S(1)} %copy-done.7, bf16[512,1024]{1,0:T(8,128)(2,1)S(1)} %maximum_select_fusion.7), kind=kOutput, calls=%fused_computation.8 | convolution fusion | flops 3771465728 | bytes 9437184 | tf_op jit(solution)/shard_map/dot_general | solution.py:27
  (168 shorter events, 33.0 us)
Async XLA Ops:
  7.2 172.2 %reduce-scatter.2.cloned.1.call-start = ((), (), s32[]{:S(2)}) async-start(), calls=%async_computation.1 | async-start | bytes 2293760 | tf_op jit(solution)/shard_map/reduce_scatter | solution.py:160
  8.8 14.9 %collective-permute-start = (bf16[144,512]{1,0:T(8,128)(2,1)S(1)}, bf16[144,512]{1,0:T(8,128)(2,1)S(1)}, u32[]{:S(2)}, u32[]{:S(2)}) collective-permute-start(bf16[144,512]{1,0:T(8,128)(2,1)S(1)} %pad_maximum_fusion.6), channel_id=1, source_target_pairs={{0,0},{1,8},{2,16},{3,24},{4,4},{5,12},{6,20},{7,28},{8,1},{9,9},{... | collective-permute-start | bytes 442376 | tf_op jit(solution)/shard_map/ppermute | solution.py:61
  23.7 5.1 %collective-permute-start.1 = (bf16[128,512]{1,0:T(8,128)(2,1)S(1)}, bf16[128,512]{1,0:T(8,128)(2,1)S(1)}, u32[]{:S(2)}, u32[]{:S(2)}) collective-permute-start(bf16[128,512]{1,0:T(8,128)(2,1)S(1)} %slice.67), channel_id=1, source_target_pairs={{0,8},{4,12},{8,0},{12,4},{16,24},{20,28},{24,16},{28,20},{1,9},{5... | collective-permute-start | bytes 393224 | tf_op jit(solution)/shard_map/ppermute | solution.py:67
  23.8 8.8 %collective-permute-start.2 = (bf16[128,512]{1,0:T(8,128)(2,1)S(1)}, bf16[128,512]{1,0:T(8,128)(2,1)S(1)}, u32[]{:S(2)}, u32[]{:S(2)}) collective-permute-start(bf16[128,512]{1,0:T(8,128)(2,1)S(1)} %slice.67), channel_id=1, source_target_pairs={{0,16},{4,20},{8,24},{12,28},{16,0},{20,4},{24,8},{28,12},{1,17},{... | collective-permute-start | bytes 393224 | tf_op jit(solution)/shard_map/ppermute | solution.py:67
  27.4 7.1 %collective-permute-start.3 = (bf16[128,512]{1,0:T(8,128)(2,1)S(1)}, bf16[128,512]{1,0:T(8,128)(2,1)S(1)}, u32[]{:S(2)}, u32[]{:S(2)}) collective-permute-start(bf16[128,512]{1,0:T(8,128)(2,1)S(1)} %slice.67), channel_id=1, source_target_pairs={{0,24},{4,28},{8,16},{12,20},{16,8},{20,12},{24,0},{28,4},{1,25},{... | collective-permute-start | bytes 393224 | tf_op jit(solution)/shard_map/ppermute | solution.py:67
  34.5 19.2 %collective-permute-start.4 = (bf16[512,512]{1,0:T(8,128)(2,1)S(1)}, bf16[512,512]{1,0:T(8,128)(2,1)S(1)}, u32[]{:S(2)}, u32[]{:S(2)}) collective-permute-start(bf16[512,512]{1,0:T(8,128)(2,1)S(1)} %bitcast.158), channel_id=1, source_target_pairs={{0,4},{4,0},{8,12},{12,8},{16,20},{20,16},{24,28},{28,24},{1,5},{5... | collective-permute-start | bytes 1572872 | tf_op jit(solution)/shard_map/ppermute | solution.py:64
  34.6 14.3 %collective-permute-start.9 = (bf16[128,512]{1,0:T(8,128)(2,1)S(1)}, bf16[128,512]{1,0:T(8,128)(2,1)S(1)}, u32[]{:S(2)}, u32[]{:S(2)}) collective-permute-start(bf16[128,512]{1,0:T(8,128)(2,1)S(1)} %copy-done.11), channel_id=1, source_target_pairs={{0,0},{1,8},{2,16},{3,24},{4,4},{5,12},{6,20},{7,28},{8,1},{9,9},{... | collective-permute-start | bytes 393224 | tf_op jit(solution)/shard_map/ppermute | solution.py:61
  48.9 10.8 %collective-permute-start.10 = (bf16[128,512]{1,0:T(8,128)(2,1)S(1)}, bf16[128,512]{1,0:T(8,128)(2,1)}, u32[]{:S(2)}, u32[]{:S(2)}) collective-permute-start(bf16[128,512]{1,0:T(8,128)(2,1)S(1)} %collective-permute-done.9), channel_id=1, source_target_pairs={{0,8},{4,12},{8,0},{12,4},{16,24},{20,28},{24,16},{28,20},{1,9},{5... | collective-permute-start | bytes 393224 | tf_op jit(solution)/shard_map/ppermute | solution.py:67
  48.9 11.8 %collective-permute-start.11 = (bf16[128,512]{1,0:T(8,128)(2,1)S(1)}, bf16[128,512]{1,0:T(8,128)(2,1)S(1)}, u32[]{:S(2)}, u32[]{:S(2)}) collective-permute-start(bf16[128,512]{1,0:T(8,128)(2,1)S(1)} %collective-permute-done.9), channel_id=1, source_target_pairs={{0,16},{4,20},{8,24},{12,28},{16,0},{20,4},{24,8},{28,12},{1,17},{... | collective-permute-start | bytes 393224 | tf_op jit(solution)/shard_map/ppermute | solution.py:67
  49.4 11.3 %collective-permute-start.12 = (bf16[128,512]{1,0:T(8,128)(2,1)S(1)}, bf16[128,512]{1,0:T(8,128)(2,1)S(1)}, u32[]{:S(2)}, u32[]{:S(2)}) collective-permute-start(bf16[128,512]{1,0:T(8,128)(2,1)S(1)} %collective-permute-done.9), channel_id=1, source_target_pairs={{0,24},{4,28},{8,16},{12,20},{16,8},{20,12},{24,0},{28,4},{1,25},{... | collective-permute-start | bytes 393224 | tf_op jit(solution)/shard_map/ppermute | solution.py:67
  52.4 1.2 collective-permute-start.5
  59.6 15.1 %collective-permute-start.6 = (bf16[128,1920]{1,0:T(8,128)(2,1)S(1)}, bf16[128,1920]{1,0:T(8,128)(2,1)S(1)}, u32[]{:S(2)}, u32[]{:S(2)}) collective-permute-start(bf16[128,1920]{1,0:T(8,128)(2,1)S(1)} %dynamic-slice_bitcast_fusion.1), channel_id=1, source_target_pairs={{0,1},{1,2},{2,3},{3,0},{4,5},{5,6},{6,7},{7,4},{8,9},{9,10},{10,1... | collective-permute-start | bytes 1474568 | tf_op jit(solution)/shard_map/ppermute | solution.py:108
  60.7 15.0 %collective-permute-start.13 = (bf16[512,512]{1,0:T(8,128)(2,1)S(1)}, bf16[512,512]{1,0:T(8,128)(2,1)S(1)}, u32[]{:S(2)}, u32[]{:S(2)}) collective-permute-start(bf16[512,512]{1,0:T(8,128)(2,1)S(1)} %bitcast.152), channel_id=1, source_target_pairs={{0,4},{4,0},{8,12},{12,8},{16,20},{20,16},{24,28},{28,24},{1,5},{5... | collective-permute-start | bytes 1572872 | tf_op jit(solution)/shard_map/ppermute | solution.py:64
  75.7 14.6 %collective-permute-start.7 = (bf16[128,1920]{1,0:T(8,128)(2,1)}, bf16[128,1920]{1,0:T(8,128)(2,1)}, u32[]{:S(2)}, u32[]{:S(2)}) collective-permute-start(bf16[128,1920]{1,0:T(8,128)(2,1)} %fusion.37), channel_id=1, source_target_pairs={{0,1},{1,2},{2,3},{3,0},{4,5},{5,6},{6,7},{7,4},{8,9},{9,10},{10,1... | collective-permute-start | bytes 1474568 | tf_op jit(solution)/shard_map/ppermute | solution.py:108
  91.4 13.4 %collective-permute-start.8 = (bf16[128,1920]{1,0:T(8,128)(2,1)S(1)}, bf16[128,1920]{1,0:T(8,128)(2,1)S(1)}, u32[]{:S(2)}, u32[]{:S(2)}) collective-permute-start(bf16[128,1920]{1,0:T(8,128)(2,1)S(1)} %fusion.36), channel_id=1, source_target_pairs={{0,1},{1,2},{2,3},{3,0},{4,5},{5,6},{6,7},{7,4},{8,9},{9,10},{10,1... | collective-permute-start | bytes 1474568 | tf_op jit(solution)/shard_map/ppermute | solution.py:108
  105.4 14.6 %collective-permute-start.14 = (bf16[128,1792]{1,0:T(8,128)(2,1)S(1)}, bf16[128,1792]{1,0:T(8,128)(2,1)S(1)}, u32[]{:S(2)}, u32[]{:S(2)}) collective-permute-start(bf16[128,1792]{1,0:T(8,128)(2,1)S(1)} %multiply_convert_fusion.4), channel_id=1, source_target_pairs={{0,1},{1,2},{2,3},{3,0},{4,5},{5,6},{6,7},{7,4},{8,9},{9,10},{10,1... | collective-permute-start | bytes 1376264 | tf_op jit(solution)/shard_map/ppermute | solution.py:108
  105.4 198.7 %all-gather.2.cloned.1.call-start = ((), (), s32[]{:S(2)}) async-start(), calls=%async_computation.2 | async-start | bytes 2293760 | tf_op jit(solution)/shard_map/all_gather | solution.py:167
  105.8 60.6 %copy-start.1 = (bf16[1792,1024]{1,0:T(8,128)(2,1)S(1)}, bf16[1792,1024]{1,0:T(8,128)(2,1)}, u32[]{:S(2)}) copy-start(bf16[1792,1024]{1,0:T(8,128)(2,1)} %fusion) | copy-start | bytes 11010052
  119.9 23.5 %collective-permute-start.15 = (bf16[128,1792]{1,0:T(8,128)(2,1)S(1)}, bf16[128,1792]{1,0:T(8,128)(2,1)S(1)}, u32[]{:S(2)}, u32[]{:S(2)}) collective-permute-start(bf16[128,1792]{1,0:T(8,128)(2,1)S(1)} %collective-permute-done.14), channel_id=1, source_target_pairs={{0,1},{1,2},{2,3},{3,0},{4,5},{5,6},{6,7},{7,4},{8,9},{9,10},{10,1... | collective-permute-start | bytes 1376264 | tf_op jit(solution)/shard_map/ppermute | solution.py:108
  143.5 22.9 %collective-permute-start.16 = (bf16[128,1792]{1,0:T(8,128)(2,1)S(1)}, bf16[128,1792]{1,0:T(8,128)(2,1)S(1)}, u32[]{:S(2)}, u32[]{:S(2)}) collective-permute-start(bf16[128,1792]{1,0:T(8,128)(2,1)S(1)} %collective-permute-done.15), channel_id=1, source_target_pairs={{0,1},{1,2},{2,3},{3,0},{4,5},{5,6},{6,7},{7,4},{8,9},{9,10},{10,1... | collective-permute-start | bytes 1376264 | tf_op jit(solution)/shard_map/ppermute | solution.py:108
  168.5 2.0 collective-permute-start.17
  170.7 6.4 %collective-permute-start.18 = (bf16[128,512]{1,0:T(8,128)(2,1)S(1)}, bf16[128,512]{1,0:T(8,128)(2,1)S(1)}, u32[]{:S(2)}, u32[]{:S(2)}) collective-permute-start(bf16[128,512]{1,0:T(8,128)(2,1)S(1)} %get-tuple-element.40), channel_id=1, source_target_pairs={{0,8},{4,12},{8,0},{12,4},{16,24},{20,28},{24,16},{28,20},{1,9},{5... | collective-permute-start | bytes 393224 | tf_op jit(solution)/shard_map/ppermute | solution.py:67
  170.8 8.4 %collective-permute-start.19 = (bf16[128,512]{1,0:T(8,128)(2,1)S(1)}, bf16[128,512]{1,0:T(8,128)(2,1)S(1)}, u32[]{:S(2)}, u32[]{:S(2)}) collective-permute-start(bf16[128,512]{1,0:T(8,128)(2,1)S(1)} %get-tuple-element.42), channel_id=1, source_target_pairs={{0,16},{4,20},{8,24},{12,28},{16,0},{20,4},{24,8},{28,12},{1,17},{... | collective-permute-start | bytes 393224 | tf_op jit(solution)/shard_map/ppermute | solution.py:67
  170.9 8.3 %collective-permute-start.20 = (bf16[128,512]{1,0:T(8,128)(2,1)S(1)}, bf16[128,512]{1,0:T(8,128)(2,1)S(1)}, u32[]{:S(2)}, u32[]{:S(2)}) collective-permute-start(bf16[128,512]{1,0:T(8,128)(2,1)S(1)} %get-tuple-element.41), channel_id=1, source_target_pairs={{0,24},{4,28},{8,16},{12,20},{16,8},{20,12},{24,0},{28,4},{1,25},{... | collective-permute-start | bytes 393224 | tf_op jit(solution)/shard_map/ppermute | solution.py:67
  179.4 5.8 %collective-permute-start.21 = (bf16[128,512]{1,0:T(8,128)(2,1)S(1)}, bf16[128,512]{1,0:T(8,128)(2,1)S(1)}, u32[]{:S(2)}, u32[]{:S(2)}) collective-permute-start(bf16[128,512]{1,0:T(8,128)(2,1)S(1)} %fusion.51), channel_id=1, source_target_pairs={{0,8},{4,12},{8,0},{12,4},{16,24},{20,28},{24,16},{28,20},{1,9},{5... | collective-permute-start | bytes 393224 | tf_op jit(solution)/shard_map/ppermute | solution.py:67
  181.1 7.1 %collective-permute-start.22 = (bf16[128,512]{1,0:T(8,128)(2,1)S(1)}, bf16[128,512]{1,0:T(8,128)(2,1)S(1)}, u32[]{:S(2)}, u32[]{:S(2)}) collective-permute-start(bf16[128,512]{1,0:T(8,128)(2,1)S(1)} %fusion.51), channel_id=1, source_target_pairs={{0,16},{4,20},{8,24},{12,28},{16,0},{20,4},{24,8},{28,12},{1,17},{... | collective-permute-start | bytes 393224 | tf_op jit(solution)/shard_map/ppermute | solution.py:67
  181.4 6.8 %collective-permute-start.23 = (bf16[128,512]{1,0:T(8,128)(2,1)S(1)}, bf16[128,512]{1,0:T(8,128)(2,1)S(1)}, u32[]{:S(2)}, u32[]{:S(2)}) collective-permute-start(bf16[128,512]{1,0:T(8,128)(2,1)S(1)} %fusion.51), channel_id=1, source_target_pairs={{0,24},{4,28},{8,16},{12,20},{16,8},{20,12},{24,0},{28,4},{1,25},{... | collective-permute-start | bytes 393224 | tf_op jit(solution)/shard_map/ppermute | solution.py:67
  188.2 2.0 collective-permute-start.24
  196.1 15.1 %collective-permute-start.25 = (bf16[128,1920]{1,0:T(8,128)(2,1)S(1)}, bf16[128,1920]{1,0:T(8,128)(2,1)S(1)}, u32[]{:S(2)}, u32[]{:S(2)}) collective-permute-start(bf16[128,1920]{1,0:T(8,128)(2,1)S(1)} %dynamic-slice_bitcast_fusion), channel_id=1, source_target_pairs={{0,1},{1,2},{2,3},{3,0},{4,5},{5,6},{6,7},{7,4},{8,9},{9,10},{10,1... | collective-permute-start | bytes 1474568 | tf_op jit(solution)/shard_map/ppermute | solution.py:108
  211.4 14.3 %collective-permute-start.26 = (bf16[128,1920]{1,0:T(8,128)(2,1)S(1)}, bf16[128,1920]{1,0:T(8,128)(2,1)S(1)}, u32[]{:S(2)}, u32[]{:S(2)}) collective-permute-start(bf16[128,1920]{1,0:T(8,128)(2,1)S(1)} %fusion.35), channel_id=1, source_target_pairs={{0,1},{1,2},{2,3},{3,0},{4,5},{5,6},{6,7},{7,4},{8,9},{9,10},{10,1... | collective-permute-start | bytes 1474568 | tf_op jit(solution)/shard_map/ppermute | solution.py:108
  226.6 13.8 %collective-permute-start.27 = (bf16[128,1920]{1,0:T(8,128)(2,1)}, bf16[128,1920]{1,0:T(8,128)(2,1)S(1)}, u32[]{:S(2)}, u32[]{:S(2)}) collective-permute-start(bf16[128,1920]{1,0:T(8,128)(2,1)} %fusion.34), channel_id=1, source_target_pairs={{0,1},{1,2},{2,3},{3,0},{4,5},{5,6},{6,7},{7,4},{8,9},{9,10},{10,1... | collective-permute-start | bytes 1474568 | tf_op jit(solution)/shard_map/ppermute | solution.py:108
  241.0 25.2 %collective-permute-start.28 = (bf16[128,1920]{1,0:T(8,128)(2,1)S(1)}, bf16[128,1920]{1,0:T(8,128)(2,1)S(1)}, u32[]{:S(2)}, u32[]{:S(2)}) collective-permute-start(bf16[128,1920]{1,0:T(8,128)(2,1)S(1)} %concatenate.93), channel_id=1, source_target_pairs={{0,1},{1,2},{2,3},{3,0},{4,5},{5,6},{6,7},{7,4},{8,9},{9,10},{10,1... | collective-permute-start | bytes 1474568 | tf_op jit(solution)/shard_map/ppermute | solution.py:108
  266.2 24.6 %collective-permute-start.29 = (bf16[128,1920]{1,0:T(8,128)(2,1)S(1)}, bf16[128,1920]{1,0:T(8,128)(2,1)S(1)}, u32[]{:S(2)}, u32[]{:S(2)}) collective-permute-start(bf16[128,1920]{1,0:T(8,128)(2,1)S(1)} %collective-permute-done.28), channel_id=1, source_target_pairs={{0,1},{1,2},{2,3},{3,0},{4,5},{5,6},{6,7},{7,4},{8,9},{9,10},{10,1... | collective-permute-start | bytes 1474568 | tf_op jit(solution)/shard_map/ppermute | solution.py:108
  290.9 13.2 %collective-permute-start.30 = (bf16[128,1920]{1,0:T(8,128)(2,1)S(1)}, bf16[128,1920]{1,0:T(8,128)(2,1)S(1)}, u32[]{:S(2)}, u32[]{:S(2)}) collective-permute-start(bf16[128,1920]{1,0:T(8,128)(2,1)S(1)} %collective-permute-done.29), channel_id=1, source_target_pairs={{0,1},{1,2},{2,3},{3,0},{4,5},{5,6},{6,7},{7,4},{8,9},{9,10},{10,1... | collective-permute-start | bytes 1474568 | tf_op jit(solution)/shard_map/ppermute | solution.py:108
  313.5 2.9 collective-permute-start.35
  315.8 4.5 %collective-permute-start.31 = (bf16[512,512]{1,0:T(8,128)(2,1)S(1)}, bf16[512,512]{1,0:T(8,128)(2,1)S(1)}, u32[]{:S(2)}, u32[]{:S(2)}) collective-permute-start(bf16[512,512]{1,0:T(8,128)(2,1)S(1)} %broadcast_select_fusion.2), channel_id=1, source_target_pairs={{0,4},{4,0},{8,12},{12,8},{16,20},{20,16},{24,28},{28,24},{1,5},{5... | collective-permute-start | bytes 1572872 | tf_op jit(solution)/shard_map/ppermute | solution.py:64
  316.7 7.1 %collective-permute-start.36 = (bf16[128,640]{1,0:T(8,128)(2,1)S(1)}, bf16[128,640]{1,0:T(8,128)(2,1)S(1)}, u32[]{:S(2)}, u32[]{:S(2)}) collective-permute-start(bf16[128,640]{1,0:T(8,128)(2,1)S(1)} %get-tuple-element.34), channel_id=1, source_target_pairs={{0,8},{4,12},{8,0},{12,4},{16,24},{20,28},{24,16},{28,20},{1,9},{5... | collective-permute-start | bytes 491528 | tf_op jit(solution)/shard_map/ppermute | solution.py:67
  317.3 10.2 %collective-permute-start.37 = (bf16[128,640]{1,0:T(8,128)(2,1)S(1)}, bf16[128,640]{1,0:T(8,128)(2,1)S(1)}, u32[]{:S(2)}, u32[]{:S(2)}) collective-permute-start(bf16[128,640]{1,0:T(8,128)(2,1)S(1)} %get-tuple-element.36), channel_id=1, source_target_pairs={{0,16},{4,20},{8,24},{12,28},{16,0},{20,4},{24,8},{28,12},{1,17},{... | collective-permute-start | bytes 491528 | tf_op jit(solution)/shard_map/ppermute | solution.py:67
  318.7 8.8 %collective-permute-start.38 = (bf16[128,640]{1,0:T(8,128)(2,1)S(1)}, bf16[128,640]{1,0:T(8,128)(2,1)S(1)}, u32[]{:S(2)}, u32[]{:S(2)}) collective-permute-start(bf16[128,640]{1,0:T(8,128)(2,1)S(1)} %get-tuple-element.35), channel_id=1, source_target_pairs={{0,24},{4,28},{8,16},{12,20},{16,8},{20,12},{24,0},{28,4},{1,25},{... | collective-permute-start | bytes 491528 | tf_op jit(solution)/shard_map/ppermute | solution.py:67
  320.5 9.7 %collective-permute-start.32 = (bf16[128,512]{1,0:T(8,128)(2,1)S(1)}, bf16[128,512]{1,0:T(8,128)(2,1)S(1)}, u32[]{:S(2)}, u32[]{:S(2)}) collective-permute-start(bf16[128,512]{1,0:T(8,128)(2,1)S(1)} %get-tuple-element.37), channel_id=1, source_target_pairs={{0,8},{4,12},{8,0},{12,4},{16,24},{20,28},{24,16},{28,20},{1,9},{5... | collective-permute-start | bytes 393224 | tf_op jit(solution)/shard_map/ppermute | solution.py:67
  321.1 11.2 %collective-permute-start.33 = (bf16[128,512]{1,0:T(8,128)(2,1)S(1)}, bf16[128,512]{1,0:T(8,128)(2,1)S(1)}, u32[]{:S(2)}, u32[]{:S(2)}) collective-permute-start(bf16[128,512]{1,0:T(8,128)(2,1)S(1)} %get-tuple-element.39), channel_id=1, source_target_pairs={{0,16},{4,20},{8,24},{12,28},{16,0},{20,4},{24,8},{28,12},{1,17},{... | collective-permute-start | bytes 393224 | tf_op jit(solution)/shard_map/ppermute | solution.py:67
  323.8 8.4 %collective-permute-start.34 = (bf16[128,512]{1,0:T(8,128)(2,1)S(1)}, bf16[128,512]{1,0:T(8,128)(2,1)S(1)}, u32[]{:S(2)}, u32[]{:S(2)}) collective-permute-start(bf16[128,512]{1,0:T(8,128)(2,1)S(1)} %get-tuple-element.38), channel_id=1, source_target_pairs={{0,24},{4,28},{8,16},{12,20},{16,8},{20,12},{24,0},{28,4},{1,25},{... | collective-permute-start | bytes 393224 | tf_op jit(solution)/shard_map/ppermute | solution.py:67
  332.4 23.0 %copy-start.5 = (bf16[1,4,128,1792]{3,2,1,0:T(8,128)(2,1)S(1)}, bf16[1,4,128,1792]{3,2,1,0:T(8,128)(2,1)}, u32[]{:S(2)}) copy-start(bf16[1,4,128,1792]{3,2,1,0:T(8,128)(2,1)} %copy-done.4) | copy-start | bytes 5505028
  332.5 6.1 %collective-permute-start.40 = (bf16[128,512]{1,0:T(8,128)(2,1)S(1)}, bf16[128,512]{1,0:T(8,128)(2,1)S(1)}, u32[]{:S(2)}, u32[]{:S(2)}) collective-permute-start(bf16[128,512]{1,0:T(8,128)(2,1)S(1)} %get-tuple-element.21), channel_id=1, source_target_pairs={{0,8},{4,12},{8,0},{12,4},{16,24},{20,28},{24,16},{28,20},{1,9},{5... | collective-permute-start | bytes 393224 | tf_op jit(solution)/shard_map/ppermute | solution.py:67
  334.0 6.9 %collective-permute-start.41 = (bf16[128,512]{1,0:T(8,128)(2,1)S(1)}, bf16[128,512]{1,0:T(8,128)(2,1)S(1)}, u32[]{:S(2)}, u32[]{:S(2)}) collective-permute-start(bf16[128,512]{1,0:T(8,128)(2,1)S(1)} %get-tuple-element.21), channel_id=1, source_target_pairs={{0,16},{4,20},{8,24},{12,28},{16,0},{20,4},{24,8},{28,12},{1,17},{... | collective-permute-start | bytes 393224 | tf_op jit(solution)/shard_map/ppermute | solution.py:67
  334.4 6.6 %collective-permute-start.42 = (bf16[128,512]{1,0:T(8,128)(2,1)S(1)}, bf16[128,512]{1,0:T(8,128)(2,1)S(1)}, u32[]{:S(2)}, u32[]{:S(2)}) collective-permute-start(bf16[128,512]{1,0:T(8,128)(2,1)S(1)} %get-tuple-element.21), channel_id=1, source_target_pairs={{0,24},{4,28},{8,16},{12,20},{16,8},{20,12},{24,0},{28,4},{1,25},{... | collective-permute-start | bytes 393224 | tf_op jit(solution)/shard_map/ppermute | solution.py:67
  341.0 2.0 collective-permute-start.43
  341.1 14.3 %collective-permute-start.39 = (bf16[128,512]{1,0:T(8,128)(2,1)S(1)}, bf16[128,512]{1,0:T(8,128)(2,1)S(1)}, u32[]{:S(2)}, u32[]{:S(2)}) collective-permute-start(bf16[128,512]{1,0:T(8,128)(2,1)S(1)} %get-tuple-element.20), channel_id=1, source_target_pairs={{0,0},{1,8},{2,16},{3,24},{4,4},{5,12},{6,20},{7,28},{8,1},{9,9},{... | collective-permute-start | bytes 393224 | tf_op jit(solution)/shard_map/ppermute | solution.py:61
  (10 other events, 76.3 us)
Sparse Core Ops, SparseCore 0:
  105.6 61.4 reduce-scatter.1
  226.7 60.1 all-gather.1

commit v5 on v4

--- a/solution.py
+++ b/solution.py
@@ -5,7 +5,7 @@
 
 LANES = 128
 PAD = 16
-CHUNKS = 1
+CHUNKS = 2
 epsilon = 1e-05
 F32 = jnp.float32
 BF16 = jnp.bfloat16
@@ -104,6 +104,9 @@
             total = total + chip_swap(take(both, chip ^ shift), shift).astype(F32)
         return total
 
+    def after(value, *others):
+        return lax.optimization_barrier((value,) + others)[0]
+
     def ring(block):
         return lax.ppermute(block, "local", [(s, (s + 1) % n_local) for s in range(n_local)])
 
@@ -123,6 +126,16 @@
             out = put(out, block, (z - step) % n_local)
         return out
 
+    def local_reduce(partial, h):
+        if h % 2:
+            return ring_reduce(partial)
+        return lax.psum_scatter(partial, "local", scatter_dimension=0, tiled=True).astype(F32)
+
+    def local_gather(block, h):
+        if h % 2:
+            return ring_gather(block)
+        return lax.all_gather(block, "local", axis=0, tiled=True)
+
     def chunk_of(array, h):
         size = part * n_local
         return array[h * size : (h + 1) * size]
@@ -145,33 +158,30 @@
     x_home, gain_rows = first[:rows], first[rows:]
     gains = order(gain_rows, core_swap(gain_rows))[:1].astype(F32)
     gains_home = gain_rows[:1].astype(F32)
-    g_home = exchange(cotangent)
 
     x = gather_node(x_home)
-    g = gather_node(g_home)
+    g_home = exchange(after(cotangent, x))
+    partials = [up_partial(chunk_of(x, h)) for h in range(CHUNKS)]
+    g = gather_node(after(g_home, *partials))
     slopes = [
         dot(chunk_of(g, h), down_weight, ((1,), (1,))).astype(BF16) for h in range(CHUNKS)
     ]
-    hidden_first, updates = [], []
+    hidden_first, x1_homes = [], []
     for h in range(CHUNKS):
-        pre, _ = finish_pre(ring_reduce(up_partial(chunk_of(x, h))))
-        hidden = jax.nn.silu(pre).astype(BF16)
-        hidden, slopes[h] = lax.optimization_barrier((hidden, slopes[h]))
-        slopes[h] = lax.psum_scatter(slopes[h], "local", scatter_dimension=0, tiled=True)
-        hidden = ring_gather(hidden)
+        pre, _ = finish_pre(local_reduce(partials[h], h))
+        hidden = local_gather(jax.nn.silu(pre).astype(BF16), h)
         hidden_first.append(hidden)
-        updates.append(dot(hidden, down_weight, ((1,), (0,))).astype(BF16))
-    update = scatter_node(jnp.concatenate(updates, axis=0))
-    x1_home = (x_home.astype(F32) + update).astype(BF16)
-    x1_home, slopes = lax.optimization_barrier((x1_home, slopes))
-    slopes = [lax.all_gather(slope, "local", axis=0, tiled=True) for slope in slopes]
-
-    x = gather_node(x1_home)
-    hidden_second, grads, updates = [], [], []
+        slopes[h] = local_reduce(slopes[h], h).astype(BF16)
+        update = scatter_node(dot(hidden, down_weight, ((1,), (0,))).astype(BF16))
+        x1_homes.append((chunk_home(x_home, h, part).astype(F32) + update).astype(BF16))
+
+    hidden_second, grads, updates, below = [], [], [], []
     for h in range(CHUNKS):
-        pre, factor = finish_pre(ring_reduce(up_partial(chunk_of(x, h))))
+        x = gather_node(x1_homes[h])
+        pre, factor = finish_pre(local_reduce(up_partial(x), h))
         packed = jnp.concatenate([pre.astype(BF16)] + split_pair(factor), axis=1)
-        packed = ring_gather(packed)
+        slopes[h] = local_gather(slopes[h], h)
+        packed = local_gather(packed, h)
         pre = packed[:, :hidden_units].astype(F32)
         sigma = jax.nn.sigmoid(pre)
         hidden_second.append((pre * sigma).astype(BF16))
@@ -181,15 +191,16 @@
         total = scatter_node(normed_grad, split_pair(inner))
         factor = join_pair(take(packed[:, hidden_units:], chip))
         inner = join_pair(total[:, cols:]) / (features * factor)
-        before = chunk_home(x1_home, h, part).astype(F32)
+        before = x1_homes[h].astype(F32)
         back = factor * (total[:, :cols] * gains_home) - before * (factor**3 * inner)
         grads.append((chunk_home(g_home, h, part).astype(F32) + back).astype(BF16))
         updates.append(dot(hidden_second[h], down_weight, ((1,), (0,))).astype(BF16))
     update = scatter_node(jnp.concatenate(updates, axis=0))
+    x1_home = jnp.concatenate(x1_homes, axis=0)
     x2_home = (x1_home.astype(F32) + update).astype(BF16)
-    x2_home, grads = lax.optimization_barrier((x2_home, grads))
     result = exchange(x2_home)
-    below = [gather_node(grad) for grad in grads]
+    below = [gather_node(grad) for grad in grads[:-1]]
+    below.append(gather_node(after(grads[-1], x2_home)))
     result, below = lax.optimization_barrier((result, below))
     grad_down = dot(
         jnp.concatenate(hidden_first + hidden_second, axis=0),

time: 369 us -> 368 us (level)
  waiting for transfers between devices: 255 us -> 150 us
  blocking collectives: 0 us -> 76.2 us
  starting transfers between devices: 39.8 us -> 55.1 us
  local copies, waits for them, and re-layouts: 8.27 us -> 14.3 us
  other arithmetic: 21.2 us -> 26.3 us
    ppermute x12 -> x18, waiting for transfers between devices: 198 us -> 78.9 us  [ring(): lax.ppermute(block, 'local', [(s, (s + 1) % n_local) for s in range(n_loc...]
    all_gather x0 -> x3, blocking collectives: none -> 76.2 us  [local_gather(): return lax.all_gather(block, 'local', axis=0, tiled=True)]
    ppermute x21 -> x33, starting transfers between devices: 26.2 us -> 40 us  [chip_swap(): lax.ppermute(block, 'node', [(n, n ^ 2 * shift) for n in range(n_node)])]
    ppermute x3, waiting for transfers between devices: 23.7 us -> 32.5 us  [exchange(): return lax.ppermute(block, ('node', 'local'), swap)]
    ppermute x21 -> x33, waiting for transfers between devices: 28.6 us -> 37 us  [chip_swap(): lax.ppermute(block, 'node', [(n, n ^ 2 * shift) for n in range(n_node)])]
    dot_general x7 -> x13, matrix products: 28.7 us -> 29.6 us  [dot(): lax.dot_general(left, right, (dims, ((), ())), preferred_element_type=F32)]
  transfers between devices with their start and end apart: 46 -> 69, of which waited for: 29 -> 44; matrix products, arithmetic and copies ran while one was open for 9% -> 13% of each run, Pallas kernels for 0% -> 0%
where the time goes in v5:
time: 368 us; the launch traced here: 367 us
  waiting for transfers between devices  150 us (41%)
  blocking collectives  76.2 us (21%)
  starting transfers between devices  55.1 us (15%)
  matrix products  29.6 us (8%)
  other arithmetic  26.3 us (7%)
  between operations  15.2 us (4%)
  local copies, waits for them, and re-layouts  14.3 us (4%)
    ppermute x18, waiting for transfers between devices, ring(): lax.ppermute(block, 'local', [(s, (s + 1) % n_local) for s in range(n_loc...  78.9 us
    all_gather x3, blocking collectives, local_gather(): return lax.all_gather(block, 'local', axis=0, tiled=True)  76.2 us
    ppermute x33, starting transfers between devices, chip_swap(): lax.ppermute(block, 'node', [(n, n ^ 2 * shift) for n in range(n_node)])  40 us
    ppermute x33, waiting for transfers between devices, chip_swap(): lax.ppermute(block, 'node', [(n, n ^ 2 * shift) for n in range(n_node)])  37 us
    ppermute x3, waiting for transfers between devices, exchange(): return lax.ppermute(block, ('node', 'local'), swap)  32.5 us
    dot_general x13, matrix products, dot(): lax.dot_general(left, right, (dims, ((), ())), preferred_element_type=F32)  29.6 us
    ppermute x3, starting transfers between devices, exchange(): return lax.ppermute(block, ('node', 'local'), swap)  8.84 us
  transfers between devices with their start and end apart: 69, of which 44 were waited for; matrix products, arithmetic and copies ran while one was open for 13% of the time, Pallas kernels for 0%

profile of v5, /device:TPU:2, one launch (start us, length us, event | category | flops | bytes accessed | tf_op | source)
XLA Modules:
  0.0 366.7 jit_solution(11768833779178036415)
XLA Ops:
  8.8 3.5 collective-permute-start
  13.3 2.0 mul.210
  15.4 3.8 %fusion = bf16[1792,1024]{1,0:T(8,128)(2,1)} fusion(f32[224,8,8,128]{3,2,1,0:T(8,128)S(1)} %bitcast.214, bf16[1792,1024]{1,0:T(8,128)(2,1)S(1)} %copy-done.1), kind=kLoop, calls=%fused_computation.1 | loop fusion | flops 5505024 | bytes 14680064 | tf_op jit(solution)/shard_map/convert_element_type | solution.py:23
  19.2 2.6 fusion.1
  21.8 1.7 collective-permute-done
  23.7 1.8 collective-permute-start.2
  27.2 2.8 collective-permute-done.1
  30.8 1.8 collective-permute-done.3
  40.9 2.9 collective-permute-start.39
  44.1 4.9 %collective-permute-done.10 = bf16[64,1920]{1,0:T(8,128)(2,1)S(1)} collective-permute-done((bf16[64,1920]{1,0:T(8,128)(2,1)S(1)}, bf16[64,1920]{1,0:T(8,128)(2,1)S(1)}, u32[]{:S(2)}, u32[]{:S(2)}) %collective-permute-start.10) | collective-permute-done | bytes 245792 | tf_op jit(solution)/shard_map/ppermute | solution.py:111
  50.2 19.3 %collective-permute-done.39 = bf16[128,512]{1,0:T(8,128)(2,1)S(1)} collective-permute-done((bf16[128,512]{1,0:T(8,128)(2,1)S(1)}, bf16[128,512]{1,0:T(8,128)(2,1)S(1)}, u32[]{:S(2)}, u32[]{:S(2)}) %collective-permute-start.39) | collective-permute-done | bytes 131104 | tf_op jit(solution)/shard_map/ppermute | solution.py:61
  69.5 3.5 collective-permute-start.42
  73.2 2.7 collective-permute-done.40
  77.7 6.7 %collective-permute-done.12 = bf16[64,1920]{1,0:T(8,128)(2,1)S(1)} collective-permute-done((bf16[64,1920]{1,0:T(8,128)(2,1)S(1)}, bf16[64,1920]{1,0:T(8,128)(2,1)S(1)}, u32[]{:S(2)}, u32[]{:S(2)}) %collective-permute-start.12) | collective-permute-done | bytes 245792 | tf_op jit(solution)/shard_map/ppermute | solution.py:111
  87.8 7.3 %collective-permute-done.13 = bf16[64,1792]{1,0:T(8,128)(2,1)S(1)} collective-permute-done((bf16[64,1792]{1,0:T(8,128)(2,1)S(1)}, bf16[64,1792]{1,0:T(8,128)(2,1)S(1)}, u32[]{:S(2)}, u32[]{:S(2)}) %collective-permute-start.13) | collective-permute-done | bytes 229408 | tf_op jit(solution)/shard_map/ppermute | solution.py:111
  95.1 4.9 %collective-permute-done.52 = bf16[64,1792]{1,0:T(8,128)(2,1)S(1)} collective-permute-done((bf16[64,1792]{1,0:T(8,128)(2,1)S(1)}, bf16[64,1792]{1,0:T(8,128)(2,1)S(1)}, u32[]{:S(2)}, u32[]{:S(2)}) %collective-permute-start.52) | collective-permute-done | bytes 229408 | tf_op jit(solution)/shard_map/ppermute | solution.py:111
  100.1 5.2 %collective-permute-done.14 = bf16[64,1792]{1,0:T(8,128)(2,1)S(1)} collective-permute-done((bf16[64,1792]{1,0:T(8,128)(2,1)S(1)}, bf16[64,1792]{1,0:T(8,128)(2,1)S(1)}, u32[]{:S(2)}, u32[]{:S(2)}) %collective-permute-start.14) | collective-permute-done | bytes 229408 | tf_op jit(solution)/shard_map/ppermute | solution.py:111
  105.4 4.9 %collective-permute-done.53 = bf16[64,1792]{1,0:T(8,128)(2,1)S(1)} collective-permute-done((bf16[64,1792]{1,0:T(8,128)(2,1)S(1)}, bf16[64,1792]{1,0:T(8,128)(2,1)S(1)}, u32[]{:S(2)}, u32[]{:S(2)}) %collective-permute-start.53) | collective-permute-done | bytes 229408 | tf_op jit(solution)/shard_map/ppermute | solution.py:111
  110.6 4.4 %collective-permute-done.15 = bf16[64,1792]{1,0:T(8,128)(2,1)S(1)} collective-permute-done((bf16[64,1792]{1,0:T(8,128)(2,1)S(1)}, bf16[64,1792]{1,0:T(8,128)(2,1)S(1)}, u32[]{:S(2)}, u32[]{:S(2)}) %collective-permute-start.15) | collective-permute-done | bytes 229408 | tf_op jit(solution)/shard_map/ppermute | solution.py:111
  116.3 2.1 collective-permute-done.54
  118.8 2.0 collective-permute-start.18
  122.3 2.2 convolution_convert_fusion.2
  124.6 1.9 collective-permute-done.55
  136.7 33.6 %all_gather.9 = bf16[256,1792]{1,0:T(8,128)(2,1)S(1)} all-gather(bf16[64,1792]{1,0:T(8,128)(2,1)S(1)} %multiply_convert_fusion.5), channel_id=1, replica_groups=mesh['node'=8,'local'=4] {'local'}, dimensions={0}, use_global_device_ids=true | all-gather | bytes 1146880 | tf_op jit(solution)/shard_map/all_gather | solution.py:137
  170.3 3.5 convolution_convert_fusion.12
  175.4 3.2 convolution_convert_fusion.3
  184.7 2.4 collective-permute-done.9
  187.1 1.8 collective-permute-start.20
  194.7 4.2 %collective-permute-done.29 = bf16[64,1920]{1,0:T(8,128)(2,1)S(1)} collective-permute-done((bf16[64,1920]{1,0:T(8,128)(2,1)S(1)}, bf16[64,1920]{1,0:T(8,128)(2,1)S(1)}, u32[]{:S(2)}, u32[]{:S(2)}) %collective-permute-start.29) | collective-permute-done | bytes 245792 | tf_op jit(solution)/shard_map/ppermute | solution.py:111
  199.6 23.4 %all_gather.11 = bf16[256,1792]{1,0:T(8,128)(2,1)S(1)} all-gather(bf16[64,1792]{1,0:T(8,128)(2,1)} %reduce-scatter.8.cloned.1.call-done), channel_id=1, replica_groups=mesh['node'=8,'local'=4] {'local'}, dimensions={0}, use_global_device_ids=true | all-gather | bytes 1146880 | tf_op jit(solution)/shard_map/all_gather | solution.py:137
  223.0 1.7 concatenate.118
  224.8 1.8 multiply_reduce_fusion.1
  226.5 3.3 convolution_convert_fusion.4
  232.6 9.0 %collective-permute-done.31 = bf16[64,1920]{1,0:T(8,128)(2,1)S(1)} collective-permute-done((bf16[64,1920]{1,0:T(8,128)(2,1)S(1)}, bf16[64,1920]{1,0:T(8,128)(2,1)S(1)}, u32[]{:S(2)}, u32[]{:S(2)}) %collective-permute-start.31) | collective-permute-done | bytes 245792 | tf_op jit(solution)/shard_map/ppermute | solution.py:111
  241.7 14.4 %collective-permute-done.32 = bf16[64,1920]{1,0:T(8,128)(2,1)S(1)} collective-permute-done((bf16[64,1920]{1,0:T(8,128)(2,1)S(1)}, bf16[64,1920]{1,0:T(8,128)(2,1)S(1)}, u32[]{:S(2)}, u32[]{:S(2)}) %collective-permute-start.32) | collective-permute-done | bytes 245792 | tf_op jit(solution)/shard_map/ppermute | solution.py:111
  256.1 2.0 collective-permute-start.33
  258.1 8.8 %collective-permute-done.33 = bf16[64,1920]{1,0:T(8,128)(2,1)S(1)} collective-permute-done((bf16[64,1920]{1,0:T(8,128)(2,1)S(1)}, bf16[64,1920]{1,0:T(8,128)(2,1)S(1)}, u32[]{:S(2)}, u32[]{:S(2)}) %collective-permute-start.33) | collective-permute-done | bytes 245792 | tf_op jit(solution)/shard_map/ppermute | solution.py:111
  266.9 2.1 fusion.27
  272.5 2.7 collective-permute-start.59
  277.8 3.2 collective-permute-done.60
  282.8 19.3 %all_gather.10 = bf16[256,1920]{1,0:T(8,128)(2,1)S(1)} all-gather(bf16[64,1920]{1,0:T(8,128)(2,1)S(1)} %concatenate.122), channel_id=1, replica_groups=mesh['node'=8,'local'=4] {'local'}, dimensions={0}, use_global_device_ids=true | all-gather | bytes 1228800 | tf_op jit(solution)/shard_map/all_gather | solution.py:137
  302.1 3.8 %convolution_convert_fusion.8 = bf16[256,1024]{1,0:T(8,128)(2,1)S(1)} fusion(bf16[1024,1792]{1,0:T(8,128)(2,1)} %fusion.1, bf16[256,1792]{1,0:T(8,128)(2,1)S(1)} %all_gather.11, bf16[256,1920]{1,0:T(8,128)(2,1)S(1)} %all_gather.10), kind=kOutput, calls=%fused_computation.51 | convolution fusion | flops 944832512 | bytes 6029312 | tf_op jit(solution)/shard_map/dot_general | solution.py:27
  329.7 2.3 collective-permute-done.37
  332.1 2.0 collective-permute-start.62
  336.5 1.9 collective-permute-done.63
  339.8 2.5 collective-permute-start.38
  342.6 11.5 %collective-permute-done.38 = bf16[128,512]{1,0:T(8,128)(2,1)S(1)} collective-permute-done((bf16[128,512]{1,0:T(8,128)(2,1)S(1)}, bf16[128,512]{1,0:T(8,128)(2,1)S(1)}, u32[]{:S(2)}, u32[]{:S(2)}) %collective-permute-start.38) | collective-permute-done | bytes 131104 | tf_op jit(solution)/shard_map/ppermute | solution.py:61
  354.1 5.5 %convolution_convert_fusion = bf16[1792,1024]{1,0:T(8,128)(2,1)} fusion(bf16[256,1792]{1,0:T(8,128)(2,1)S(1)} %copy-done.14, bf16[256,1792]{1,0:T(8,128)(2,1)S(1)} %get-tuple-element.46, bf16[256,1792]{1,0:T(8,128)(2,1)S(1)} %bitcast.249, bf16[256,1792]{1,0:T(8,128)(2,1)S(1)} %copy-done.13, bf16[512,1024]{1,0:T(8,128)(2,1)S(1)} %copy-done.9, ...), kind=kOutput, calls=%fused_computation.4 | convolution fusion | flops 3780902912 | bytes 9437184 | tf_op jit(solution)/shard_map/dot_general | solution.py:27
  (294 shorter events, 87.0 us)
Async XLA Ops:
  7.2 128.2 %reduce-scatter.4.cloned.1.call-start = ((), (), s32[]{:S(2)}) async-start(), calls=%async_computation.3 | async-start | bytes 1228800 | tf_op jit(solution)/shard_map/reduce_scatter | solution.py:132
  8.8 14.7 %collective-permute-start = (bf16[144,512]{1,0:T(8,128)(2,1)S(1)}, bf16[144,512]{1,0:T(8,128)(2,1)S(1)}, u32[]{:S(2)}, u32[]{:S(2)}) collective-permute-start(bf16[144,512]{1,0:T(8,128)(2,1)S(1)} %pad_maximum_fusion.13), channel_id=1, source_target_pairs={{0,0},{1,8},{2,16},{3,24},{4,4},{5,12},{6,20},{7,28},{8,1},{9,9},{... | collective-permute-start | bytes 442376 | tf_op jit(solution)/shard_map/ppermute | solution.py:61
  23.6 6.4 %collective-permute-start.1 = (bf16[128,512]{1,0:T(8,128)(2,1)S(1)}, bf16[128,512]{1,0:T(8,128)(2,1)S(1)}, u32[]{:S(2)}, u32[]{:S(2)}) collective-permute-start(bf16[128,512]{1,0:T(8,128)(2,1)S(1)} %slice.142), channel_id=1, source_target_pairs={{0,8},{4,12},{8,0},{12,4},{16,24},{20,28},{24,16},{28,20},{1,9},{5... | collective-permute-start | bytes 393224 | tf_op jit(solution)/shard_map/ppermute | solution.py:67
  23.7 7.1 %collective-permute-start.2 = (bf16[128,512]{1,0:T(8,128)(2,1)S(1)}, bf16[128,512]{1,0:T(8,128)(2,1)S(1)}, u32[]{:S(2)}, u32[]{:S(2)}) collective-permute-start(bf16[128,512]{1,0:T(8,128)(2,1)S(1)} %slice.142), channel_id=1, source_target_pairs={{0,16},{4,20},{8,24},{12,28},{16,0},{20,4},{24,8},{28,12},{1,17},{... | collective-permute-start | bytes 393224 | tf_op jit(solution)/shard_map/ppermute | solution.py:67
  25.5 7.1 %collective-permute-start.3 = (bf16[128,512]{1,0:T(8,128)(2,1)S(1)}, bf16[128,512]{1,0:T(8,128)(2,1)S(1)}, u32[]{:S(2)}, u32[]{:S(2)}) collective-permute-start(bf16[128,512]{1,0:T(8,128)(2,1)S(1)} %slice.142), channel_id=1, source_target_pairs={{0,24},{4,28},{8,16},{12,20},{16,8},{20,12},{24,0},{28,4},{1,25},{... | collective-permute-start | bytes 393224 | tf_op jit(solution)/shard_map/ppermute | solution.py:67
  38.2 10.7 %collective-permute-start.10 = (bf16[64,1920]{1,0:T(8,128)(2,1)S(1)}, bf16[64,1920]{1,0:T(8,128)(2,1)S(1)}, u32[]{:S(2)}, u32[]{:S(2)}) collective-permute-start(bf16[64,1920]{1,0:T(8,128)(2,1)S(1)} %dynamic-slice_bitcast_fusion.1), channel_id=1, source_target_pairs={{0,1},{1,2},{2,3},{3,0},{4,5},{5,6},{6,7},{7,4},{8,9},{9,10},{10,1... | collective-permute-start | bytes 737288 | tf_op jit(solution)/shard_map/ppermute | solution.py:111
  40.9 28.6 %collective-permute-start.39 = (bf16[128,512]{1,0:T(8,128)(2,1)S(1)}, bf16[128,512]{1,0:T(8,128)(2,1)S(1)}, u32[]{:S(2)}, u32[]{:S(2)}) collective-permute-start(bf16[128,512]{1,0:T(8,128)(2,1)S(1)} %copy-done.18), channel_id=1, source_target_pairs={{0,0},{1,8},{2,16},{3,24},{4,4},{5,12},{6,20},{7,28},{8,1},{9,9},{... | collective-permute-start | bytes 393224 | tf_op jit(solution)/shard_map/ppermute | solution.py:61
  49.1 24.0 %collective-permute-start.11 = (bf16[64,1920]{1,0:T(8,128)(2,1)S(1)}, bf16[64,1920]{1,0:T(8,128)(2,1)S(1)}, u32[]{:S(2)}, u32[]{:S(2)}) collective-permute-start(bf16[64,1920]{1,0:T(8,128)(2,1)S(1)} %fusion.58), channel_id=1, source_target_pairs={{0,1},{1,2},{2,3},{3,0},{4,5},{5,6},{6,7},{7,4},{8,9},{9,10},{10,1... | collective-permute-start | bytes 737288 | tf_op jit(solution)/shard_map/ppermute | solution.py:111
  50.2 149.4 %reduce-scatter.8.cloned.1.call-start = ((), (), s32[]{:S(2)}) async-start(), calls=%async_computation.5 | async-start | bytes 1146880 | tf_op jit(solution)/shard_map/reduce_scatter | solution.py:132
  69.5 6.4 %collective-permute-start.40 = (bf16[128,512]{1,0:T(8,128)(2,1)S(1)}, bf16[128,512]{1,0:T(8,128)(2,1)S(1)}, u32[]{:S(2)}, u32[]{:S(2)}) collective-permute-start(bf16[128,512]{1,0:T(8,128)(2,1)S(1)} %collective-permute-done.39), channel_id=1, source_target_pairs={{0,8},{4,12},{8,0},{12,4},{16,24},{20,28},{24,16},{28,20},{1,9},{5... | collective-permute-start | bytes 393224 | tf_op jit(solution)/shard_map/ppermute | solution.py:67
  69.5 8.0 %collective-permute-start.41 = (bf16[128,512]{1,0:T(8,128)(2,1)S(1)}, bf16[128,512]{1,0:T(8,128)(2,1)S(1)}, u32[]{:S(2)}, u32[]{:S(2)}) collective-permute-start(bf16[128,512]{1,0:T(8,128)(2,1)S(1)} %collective-permute-done.39), channel_id=1, source_target_pairs={{0,16},{4,20},{8,24},{12,28},{16,0},{20,4},{24,8},{28,12},{1,17},{... | collective-permute-start | bytes 393224 | tf_op jit(solution)/shard_map/ppermute | solution.py:67
  69.5 8.0 %collective-permute-start.42 = (bf16[128,512]{1,0:T(8,128)(2,1)S(1)}, bf16[128,512]{1,0:T(8,128)(2,1)S(1)}, u32[]{:S(2)}, u32[]{:S(2)}) collective-permute-start(bf16[128,512]{1,0:T(8,128)(2,1)S(1)} %collective-permute-done.39), channel_id=1, source_target_pairs={{0,24},{4,28},{8,16},{12,20},{16,8},{20,12},{24,0},{28,4},{1,25},{... | collective-permute-start | bytes 393224 | tf_op jit(solution)/shard_map/ppermute | solution.py:67
  73.2 11.2 %collective-permute-start.12 = (bf16[64,1920]{1,0:T(8,128)(2,1)S(1)}, bf16[64,1920]{1,0:T(8,128)(2,1)S(1)}, u32[]{:S(2)}, u32[]{:S(2)}) collective-permute-start(bf16[64,1920]{1,0:T(8,128)(2,1)S(1)} %fusion.57), channel_id=1, source_target_pairs={{0,1},{1,2},{2,3},{3,0},{4,5},{5,6},{6,7},{7,4},{8,9},{9,10},{10,1... | collective-permute-start | bytes 737288 | tf_op jit(solution)/shard_map/ppermute | solution.py:111
  77.6 7.3 %collective-permute-start.43 = (bf16[512,512]{1,0:T(8,128)(2,1)S(1)}, bf16[512,512]{1,0:T(8,128)(2,1)S(1)}, u32[]{:S(2)}, u32[]{:S(2)}) collective-permute-start(bf16[512,512]{1,0:T(8,128)(2,1)S(1)} %bitcast.230), channel_id=1, source_target_pairs={{0,4},{4,0},{8,12},{12,8},{16,20},{20,16},{24,28},{28,24},{1,5},{5... | collective-permute-start | bytes 1572872 | tf_op jit(solution)/shard_map/ppermute | solution.py:64
  84.9 10.2 %collective-permute-start.13 = (bf16[64,1792]{1,0:T(8,128)(2,1)S(1)}, bf16[64,1792]{1,0:T(8,128)(2,1)S(1)}, u32[]{:S(2)}, u32[]{:S(2)}) collective-permute-start(bf16[64,1792]{1,0:T(8,128)(2,1)S(1)} %get-tuple-element.43), channel_id=1, source_target_pairs={{0,1},{1,2},{2,3},{3,0},{4,5},{5,6},{6,7},{7,4},{8,9},{9,10},{10,1... | collective-permute-start | bytes 688136 | tf_op jit(solution)/shard_map/ppermute | solution.py:111
  87.7 12.3 %collective-permute-start.52 = (bf16[64,1792]{1,0:T(8,128)(2,1)S(1)}, bf16[64,1792]{1,0:T(8,128)(2,1)S(1)}, u32[]{:S(2)}, u32[]{:S(2)}) collective-permute-start(bf16[64,1792]{1,0:T(8,128)(2,1)S(1)} %dynamic-slice_bitcast_fusion.2), channel_id=1, source_target_pairs={{0,1},{1,2},{2,3},{3,0},{4,5},{5,6},{6,7},{7,4},{8,9},{9,10},{10,1... | collective-permute-start | bytes 688136 | tf_op jit(solution)/shard_map/ppermute | solution.py:111
  95.1 10.3 %collective-permute-start.14 = (bf16[64,1792]{1,0:T(8,128)(2,1)S(1)}, bf16[64,1792]{1,0:T(8,128)(2,1)S(1)}, u32[]{:S(2)}, u32[]{:S(2)}) collective-permute-start(bf16[64,1792]{1,0:T(8,128)(2,1)S(1)} %collective-permute-done.13), channel_id=1, source_target_pairs={{0,1},{1,2},{2,3},{3,0},{4,5},{5,6},{6,7},{7,4},{8,9},{9,10},{10,1... | collective-permute-start | bytes 688136 | tf_op jit(solution)/shard_map/ppermute | solution.py:111
  100.0 10.3 %collective-permute-start.53 = (bf16[64,1792]{1,0:T(8,128)(2,1)S(1)}, bf16[64,1792]{1,0:T(8,128)(2,1)S(1)}, u32[]{:S(2)}, u32[]{:S(2)}) collective-permute-start(bf16[64,1792]{1,0:T(8,128)(2,1)S(1)} %fusion.65), channel_id=1, source_target_pairs={{0,1},{1,2},{2,3},{3,0},{4,5},{5,6},{6,7},{7,4},{8,9},{9,10},{10,1... | collective-permute-start | bytes 688136 | tf_op jit(solution)/shard_map/ppermute | solution.py:111
  105.3 9.7 %collective-permute-start.15 = (bf16[64,1792]{1,0:T(8,128)(2,1)S(1)}, bf16[64,1792]{1,0:T(8,128)(2,1)S(1)}, u32[]{:S(2)}, u32[]{:S(2)}) collective-permute-start(bf16[64,1792]{1,0:T(8,128)(2,1)S(1)} %collective-permute-done.14), channel_id=1, source_target_pairs={{0,1},{1,2},{2,3},{3,0},{4,5},{5,6},{6,7},{7,4},{8,9},{9,10},{10,1... | collective-permute-start | bytes 688136 | tf_op jit(solution)/shard_map/ppermute | solution.py:111
  110.4 8.1 %collective-permute-start.54 = (bf16[64,1792]{1,0:T(8,128)(2,1)S(1)}, bf16[64,1792]{1,0:T(8,128)(2,1)S(1)}, u32[]{:S(2)}, u32[]{:S(2)}) collective-permute-start(bf16[64,1792]{1,0:T(8,128)(2,1)S(1)} %fusion.64), channel_id=1, source_target_pairs={{0,1},{1,2},{2,3},{3,0},{4,5},{5,6},{6,7},{7,4},{8,9},{9,10},{10,1... | collective-permute-start | bytes 688136 | tf_op jit(solution)/shard_map/ppermute | solution.py:111
  118.5 7.9 %collective-permute-start.55 = (bf16[64,1792]{1,0:T(8,128)(2,1)S(1)}, bf16[64,1792]{1,0:T(8,128)(2,1)S(1)}, u32[]{:S(2)}, u32[]{:S(2)}) collective-permute-start(bf16[64,1792]{1,0:T(8,128)(2,1)S(1)} %get-tuple-element.29), channel_id=1, source_target_pairs={{0,1},{1,2},{2,3},{3,0},{4,5},{5,6},{6,7},{7,4},{8,9},{9,10},{10,1... | collective-permute-start | bytes 688136 | tf_op jit(solution)/shard_map/ppermute | solution.py:111
  118.8 7.7 %collective-permute-start.17 = (bf16[64,512]{1,0:T(8,128)(2,1)S(1)}, bf16[64,512]{1,0:T(8,128)(2,1)S(1)}, u32[]{:S(2)}, u32[]{:S(2)}) collective-permute-start(bf16[64,512]{1,0:T(8,128)(2,1)S(1)} %get-tuple-element.66), channel_id=1, source_target_pairs={{0,8},{4,12},{8,0},{12,4},{16,24},{20,28},{24,16},{28,20},{1,9},{5... | collective-permute-start | bytes 196616 | tf_op jit(solution)/shard_map/ppermute | solution.py:67
  118.8 7.6 %collective-permute-start.18 = (bf16[64,512]{1,0:T(8,128)(2,1)S(1)}, bf16[64,512]{1,0:T(8,128)(2,1)S(1)}, u32[]{:S(2)}, u32[]{:S(2)}) collective-permute-start(bf16[64,512]{1,0:T(8,128)(2,1)S(1)} %get-tuple-element.68), channel_id=1, source_target_pairs={{0,16},{4,20},{8,24},{12,28},{16,0},{20,4},{24,8},{28,12},{1,17},{... | collective-permute-start | bytes 196616 | tf_op jit(solution)/shard_map/ppermute | solution.py:67
  120.9 5.6 %collective-permute-start.19 = (bf16[64,512]{1,0:T(8,128)(2,1)S(1)}, bf16[64,512]{1,0:T(8,128)(2,1)S(1)}, u32[]{:S(2)}, u32[]{:S(2)}) collective-permute-start(bf16[64,512]{1,0:T(8,128)(2,1)S(1)} %get-tuple-element.67), channel_id=1, source_target_pairs={{0,24},{4,28},{8,16},{12,20},{16,8},{20,12},{24,0},{28,4},{1,25},{... | collective-permute-start | bytes 196616 | tf_op jit(solution)/shard_map/ppermute | solution.py:67
  124.5 156.8 %reduce-scatter.6.cloned.1.call-start = ((), (), s32[]{:S(2)}) async-start(), calls=%async_computation.4 | async-start | bytes 1228800 | tf_op jit(solution)/shard_map/reduce_scatter | solution.py:132
  126.4 7.9 %collective-permute-start.56 = (bf16[64,1792]{1,0:T(8,128)(2,1)S(1)}, bf16[64,1792]{1,0:T(8,128)(2,1)}, u32[]{:S(2)}, u32[]{:S(2)}) collective-permute-start(bf16[64,1792]{1,0:T(8,128)(2,1)S(1)} %collective-permute-done.55), channel_id=1, source_target_pairs={{0,1},{1,2},{2,3},{3,0},{4,5},{5,6},{6,7},{7,4},{8,9},{9,10},{10,1... | collective-permute-start | bytes 688136 | tf_op jit(solution)/shard_map/ppermute | solution.py:111
  134.1 40.5 %collective-permute-start.27 = (bf16[256,512]{1,0:T(8,128)(2,1)S(1)}, bf16[256,512]{1,0:T(8,128)(2,1)S(1)}, u32[]{:S(2)}, u32[]{:S(2)}) collective-permute-start(bf16[256,512]{1,0:T(8,128)(2,1)S(1)} %bitcast.238), channel_id=1, source_target_pairs={{0,4},{4,0},{8,12},{12,8},{16,20},{20,16},{24,28},{28,24},{1,5},{5... | collective-permute-start | bytes 786440 | tf_op jit(solution)/shard_map/ppermute | solution.py:64
  134.3 49.0 %collective-permute-start.57 = (bf16[64,1792]{1,0:T(8,128)(2,1)}, bf16[64,1792]{1,0:T(8,128)(2,1)}, u32[]{:S(2)}, u32[]{:S(2)}) collective-permute-start(bf16[64,1792]{1,0:T(8,128)(2,1)} %collective-permute-done.56), channel_id=1, source_target_pairs={{0,1},{1,2},{2,3},{3,0},{4,5},{5,6},{6,7},{7,4},{8,9},{9,10},{10,1... | collective-permute-start | bytes 688136 | tf_op jit(solution)/shard_map/ppermute | solution.py:111
  178.7 12.0 %collective-permute-start.28 = (bf16[64,1920]{1,0:T(8,128)(2,1)S(1)}, bf16[64,1920]{1,0:T(8,128)(2,1)S(1)}, u32[]{:S(2)}, u32[]{:S(2)}) collective-permute-start(bf16[64,1920]{1,0:T(8,128)(2,1)S(1)} %dynamic-slice_bitcast_fusion), channel_id=1, source_target_pairs={{0,1},{1,2},{2,3},{3,0},{4,5},{5,6},{6,7},{7,4},{8,9},{9,10},{10,1... | collective-permute-start | bytes 737288 | tf_op jit(solution)/shard_map/ppermute | solution.py:111
  181.9 5.2 %collective-permute-start.9 = (bf16[64,512]{1,0:T(8,128)(2,1)S(1)}, bf16[64,512]{1,0:T(8,128)(2,1)S(1)}, u32[]{:S(2)}, u32[]{:S(2)}) collective-permute-start(bf16[64,512]{1,0:T(8,128)(2,1)S(1)} %get-tuple-element.64), channel_id=1, source_target_pairs={{0,24},{4,28},{8,16},{12,20},{16,8},{20,12},{24,0},{28,4},{1,25},{... | collective-permute-start | bytes 196616 | tf_op jit(solution)/shard_map/ppermute | solution.py:67
  187.1 5.3 %collective-permute-start.20 = (bf16[64,512]{1,0:T(8,128)(2,1)S(1)}, bf16[64,512]{1,0:T(8,128)(2,1)S(1)}, u32[]{:S(2)}, u32[]{:S(2)}) collective-permute-start(bf16[64,512]{1,0:T(8,128)(2,1)S(1)} %get-tuple-element.37), channel_id=1, source_target_pairs={{0,8},{4,12},{8,0},{12,4},{16,24},{20,28},{24,16},{28,20},{1,9},{5... | collective-permute-start | bytes 196616 | tf_op jit(solution)/shard_map/ppermute | solution.py:67
  189.4 5.2 %collective-permute-start.22 = (bf16[64,512]{1,0:T(8,128)(2,1)S(1)}, bf16[64,512]{1,0:T(8,128)(2,1)S(1)}, u32[]{:S(2)}, u32[]{:S(2)}) collective-permute-start(bf16[64,512]{1,0:T(8,128)(2,1)S(1)} %get-tuple-element.37), channel_id=1, source_target_pairs={{0,24},{4,28},{8,16},{12,20},{16,8},{20,12},{24,0},{28,4},{1,25},{... | collective-permute-start | bytes 196616 | tf_op jit(solution)/shard_map/ppermute | solution.py:67
  190.7 8.1 %collective-permute-start.29 = (bf16[64,1920]{1,0:T(8,128)(2,1)S(1)}, bf16[64,1920]{1,0:T(8,128)(2,1)S(1)}, u32[]{:S(2)}, u32[]{:S(2)}) collective-permute-start(bf16[64,1920]{1,0:T(8,128)(2,1)S(1)} %fusion.56), channel_id=1, source_target_pairs={{0,1},{1,2},{2,3},{3,0},{4,5},{5,6},{6,7},{7,4},{8,9},{9,10},{10,1... | collective-permute-start | bytes 737288 | tf_op jit(solution)/shard_map/ppermute | solution.py:111
  194.6 28.4 %collective-permute-start.23 = (bf16[256,512]{1,0:T(8,128)(2,1)S(1)}, bf16[256,512]{1,0:T(8,128)(2,1)}, u32[]{:S(2)}, u32[]{:S(2)}) collective-permute-start(bf16[256,512]{1,0:T(8,128)(2,1)S(1)} %bitcast.236), channel_id=1, source_target_pairs={{0,4},{4,0},{8,12},{12,8},{16,20},{20,16},{24,28},{28,24},{1,5},{5... | collective-permute-start | bytes 786440 | tf_op jit(solution)/shard_map/ppermute | solution.py:64
  199.6 31.3 %collective-permute-start.30 = (bf16[64,1920]{1,0:T(8,128)(2,1)}, bf16[64,1920]{1,0:T(8,128)(2,1)}, u32[]{:S(2)}, u32[]{:S(2)}) collective-permute-start(bf16[64,1920]{1,0:T(8,128)(2,1)} %fusion.55), channel_id=1, source_target_pairs={{0,1},{1,2},{2,3},{3,0},{4,5},{5,6},{6,7},{7,4},{8,9},{9,10},{10,1... | collective-permute-start | bytes 737288 | tf_op jit(solution)/shard_map/ppermute | solution.py:111
  232.5 9.2 %collective-permute-start.31 = (bf16[64,1920]{1,0:T(8,128)(2,1)S(1)}, bf16[64,1920]{1,0:T(8,128)(2,1)S(1)}, u32[]{:S(2)}, u32[]{:S(2)}) collective-permute-start(bf16[64,1920]{1,0:T(8,128)(2,1)S(1)} %concatenate.130), channel_id=1, source_target_pairs={{0,1},{1,2},{2,3},{3,0},{4,5},{5,6},{6,7},{7,4},{8,9},{9,10},{10,1... | collective-permute-start | bytes 737288 | tf_op jit(solution)/shard_map/ppermute | solution.py:111
  241.7 14.4 %collective-permute-start.32 = (bf16[64,1920]{1,0:T(8,128)(2,1)S(1)}, bf16[64,1920]{1,0:T(8,128)(2,1)S(1)}, u32[]{:S(2)}, u32[]{:S(2)}) collective-permute-start(bf16[64,1920]{1,0:T(8,128)(2,1)S(1)} %collective-permute-done.31), channel_id=1, source_target_pairs={{0,1},{1,2},{2,3},{3,0},{4,5},{5,6},{6,7},{7,4},{8,9},{9,10},{10,1... | collective-permute-start | bytes 737288 | tf_op jit(solution)/shard_map/ppermute | solution.py:111
  256.1 10.8 %collective-permute-start.33 = (bf16[64,1920]{1,0:T(8,128)(2,1)S(1)}, bf16[64,1920]{1,0:T(8,128)(2,1)S(1)}, u32[]{:S(2)}, u32[]{:S(2)}) collective-permute-start(bf16[64,1920]{1,0:T(8,128)(2,1)S(1)} %collective-permute-done.32), channel_id=1, source_target_pairs={{0,1},{1,2},{2,3},{3,0},{4,5},{5,6},{6,7},{7,4},{8,9},{9,10},{10,1... | collective-permute-start | bytes 737288 | tf_op jit(solution)/shard_map/ppermute | solution.py:111
  272.5 5.4 %collective-permute-start.59 = (bf16[64,640]{1,0:T(8,128)(2,1)S(1)}, bf16[64,640]{1,0:T(8,128)(2,1)S(1)}, u32[]{:S(2)}, u32[]{:S(2)}) collective-permute-start(bf16[64,640]{1,0:T(8,128)(2,1)S(1)} %get-tuple-element.57), channel_id=1, source_target_pairs={{0,8},{4,12},{8,0},{12,4},{16,24},{20,28},{24,16},{28,20},{1,9},{5... | collective-permute-start | bytes 245768 | tf_op jit(solution)/shard_map/ppermute | solution.py:67
  275.2 5.9 %collective-permute-start.60 = (bf16[64,640]{1,0:T(8,128)(2,1)S(1)}, bf16[64,640]{1,0:T(8,128)(2,1)S(1)}, u32[]{:S(2)}, u32[]{:S(2)}) collective-permute-start(bf16[64,640]{1,0:T(8,128)(2,1)S(1)} %get-tuple-element.59), channel_id=1, source_target_pairs={{0,16},{4,20},{8,24},{12,28},{16,0},{20,4},{24,8},{28,12},{1,17},{... | collective-permute-start | bytes 245768 | tf_op jit(solution)/shard_map/ppermute | solution.py:67
  275.2 5.9 %collective-permute-start.61 = (bf16[64,640]{1,0:T(8,128)(2,1)S(1)}, bf16[64,640]{1,0:T(8,128)(2,1)S(1)}, u32[]{:S(2)}, u32[]{:S(2)}) collective-permute-start(bf16[64,640]{1,0:T(8,128)(2,1)S(1)} %get-tuple-element.58), channel_id=1, source_target_pairs={{0,24},{4,28},{8,16},{12,20},{16,8},{20,12},{24,0},{28,4},{1,25},{... | collective-permute-start | bytes 245768 | tf_op jit(solution)/shard_map/ppermute | solution.py:67
  309.4 14.2 %collective-permute-start.34 = (bf16[512,512]{1,0:T(8,128)(2,1)S(1)}, bf16[512,512]{1,0:T(8,128)(2,1)S(1)}, u32[]{:S(2)}, u32[]{:S(2)}) collective-permute-start(bf16[512,512]{1,0:T(8,128)(2,1)S(1)} %broadcast_select_fusion), channel_id=1, source_target_pairs={{0,4},{4,0},{8,12},{12,8},{16,20},{20,16},{24,28},{28,24},{1,5},{5... | collective-permute-start | bytes 1572872 | tf_op jit(solution)/shard_map/ppermute | solution.py:64
  310.4 5.5 %collective-permute-start.46 = (bf16[64,640]{1,0:T(8,128)(2,1)S(1)}, bf16[64,640]{1,0:T(8,128)(2,1)S(1)}, u32[]{:S(2)}, u32[]{:S(2)}) collective-permute-start(bf16[64,640]{1,0:T(8,128)(2,1)S(1)} %get-tuple-element.62), channel_id=1, source_target_pairs={{0,16},{4,20},{8,24},{12,28},{16,0},{20,4},{24,8},{28,12},{1,17},{... | collective-permute-start | bytes 245768 | tf_op jit(solution)/shard_map/ppermute | solution.py:67
  312.1 5.3 %collective-permute-start.47 = (bf16[64,640]{1,0:T(8,128)(2,1)S(1)}, bf16[64,640]{1,0:T(8,128)(2,1)S(1)}, u32[]{:S(2)}, u32[]{:S(2)}) collective-permute-start(bf16[64,640]{1,0:T(8,128)(2,1)S(1)} %get-tuple-element.61), channel_id=1, source_target_pairs={{0,24},{4,28},{8,16},{12,20},{16,8},{20,12},{24,0},{28,4},{1,25},{... | collective-permute-start | bytes 245768 | tf_op jit(solution)/shard_map/ppermute | solution.py:67
  320.3 7.2 %collective-permute-start.50 = (bf16[64,512]{1,0:T(8,128)(2,1)S(1)}, bf16[64,512]{1,0:T(8,128)(2,1)S(1)}, u32[]{:S(2)}, u32[]{:S(2)}) collective-permute-start(bf16[64,512]{1,0:T(8,128)(2,1)S(1)} %get-tuple-element.31), channel_id=1, source_target_pairs={{0,24},{4,28},{8,16},{12,20},{16,8},{20,12},{24,0},{28,4},{1,25},{... | collective-permute-start | bytes 196616 | tf_op jit(solution)/shard_map/ppermute | solution.py:67
  325.9 6.1 %collective-permute-start.37 = (bf16[128,512]{1,0:T(8,128)(2,1)S(1)}, bf16[128,512]{1,0:T(8,128)(2,1)S(1)}, u32[]{:S(2)}, u32[]{:S(2)}) collective-permute-start(bf16[128,512]{1,0:T(8,128)(2,1)S(1)} %bitcast.262), channel_id=1, source_target_pairs={{0,24},{4,28},{8,16},{12,20},{16,8},{20,12},{24,0},{28,4},{1,25},{... | collective-permute-start | bytes 393224 | tf_op jit(solution)/shard_map/ppermute | solution.py:67
  327.5 14.8 %collective-permute-start.51 = (bf16[256,512]{1,0:T(8,128)(2,1)S(1)}, bf16[256,512]{1,0:T(8,128)(2,1)S(1)}, u32[]{:S(2)}, u32[]{:S(2)}) collective-permute-start(bf16[256,512]{1,0:T(8,128)(2,1)S(1)} %bitcast.244), channel_id=1, source_target_pairs={{0,4},{4,0},{8,12},{12,8},{16,20},{20,16},{24,28},{28,24},{1,5},{5... | collective-permute-start | bytes 786440 | tf_op jit(solution)/shard_map/ppermute | solution.py:64
  339.8 14.3 %collective-permute-start.38 = (bf16[128,512]{1,0:T(8,128)(2,1)S(1)}, bf16[128,512]{1,0:T(8,128)(2,1)S(1)}, u32[]{:S(2)}, u32[]{:S(2)}) collective-permute-start(bf16[128,512]{1,0:T(8,128)(2,1)S(1)} %fusion.69), channel_id=1, source_target_pairs={{0,0},{1,8},{2,16},{3,24},{4,4},{5,12},{6,20},{7,28},{8,1},{9,9},{... | collective-permute-start | bytes 393224 | tf_op jit(solution)/shard_map/ppermute | solution.py:61
  (41 other events, 300.9 us)
Sparse Core Ops, SparseCore 0:
  50.3 32.7 reduce-scatter.3
  124.6 38.0 reduce-scatter.7
  231.1 35.0 reduce-scatter.5

commit v6 on v4

v6 whole, which is shorter than its diff:
```python
import jax
import jax.numpy as jnp
from jax import lax
from jax.sharding import PartitionSpec as P

LANES = 128
PAD = 16
CHUNKS = 1
epsilon = 1e-05
F32 = jnp.float32
BF16 = jnp.bfloat16


def dequant_rows(quanta, scales):
    blocks = scales.shape[0]
    widened = quanta.astype(F32).reshape(blocks, quanta.shape[0] // blocks, quanta.shape[1])
    return (widened * scales.astype(F32)[:, None, :]).reshape(quanta.shape).astype(BF16)


def dequant_cols(quanta, scales):
    blocks = scales.shape[1]
    widened = quanta.astype(F32).reshape(quanta.shape[0], blocks, quanta.shape[1] // blocks)
    return (widened * scales.astype(F32)[:, :, None]).reshape(quanta.shape).astype(BF16)


def dot(left, right, dims):
    return lax.dot_general(left, right, (dims, ((), ())), preferred_element_type=F32)


def split_pair(column):
    high = column.astype(BF16)
    low = (column - high.astype(F32)).astype(BF16)
    shape = (column.shape[0], LANES // 2)
    return [jnp.broadcast_to(high, shape), jnp.broadcast_to(low, shape)]


def join_pair(lanes):
    lanes = lanes.astype(F32)
    return lanes[:, :1] + lanes[:, -1:]


def body(n_node, n_local, tokens, cotangent, gain, up_q, up_scale, down_q, down_scale):
    rows, cols = tokens.shape
    part = rows // CHUNKS
    hidden_units = up_q.shape[1]
    halves = n_node // n_local
    chips = n_local
    features = cols * n_node
    z = lax.axis_index("local")
    node = lax.axis_index("node")
    chip, core = node // halves, node % halves

    swap = [
        ((halves * c + j) * n_local + l, (halves * l + j) * n_local + c)
        for c in range(n_local)
        for j in range(halves)
        for l in range(n_local)
    ]

    def exchange(block):
        return lax.ppermute(block, ("node", "local"), swap)

    def core_swap(block):
        return lax.ppermute(block, "node", [(n, n ^ 1) for n in range(n_node)])

    def chip_swap(block, shift):
        return lax.ppermute(block, "node", [(n, n ^ (2 * shift)) for n in range(n_node)])

    def after(value, *others):
        return lax.optimization_barrier((value,) + others)[0]

    def take(array, index):
        width = array.shape[1]
        array = array.reshape(-1, n_local, part, width)
        return lax.dynamic_slice_in_dim(array, index, 1, 1).reshape(-1, width)

    def put(array, block, index):
        width = array.shape[1]
        stacked = array.reshape(-1, n_local, part, width)
        block = block.reshape(-1, 1, part, width)
        return lax.dynamic_update_slice_in_dim(stacked, block, index, 1).reshape(array.shape)

    def order(own, other):
        return jnp.where(
            core == 0,
            jnp.concatenate([own, other], axis=1),
            jnp.concatenate([other, own], axis=1),
        )

    def gather_chips(block):
        mine = jnp.zeros((block.shape[0] * chips, block.shape[1]), block.dtype)
        mine = put(mine, block, chip)
        for shift in range(1, chips):
            mine = put(mine, chip_swap(block, shift), chip ^ shift)
        return mine

    def gather_core(mine):
        return order(mine, core_swap(mine))

    def gather_node(block):
        return gather_core(gather_chips(block))

    def scatter_core(partial, tail=()):
        first, second = partial[:, :cols], partial[:, cols:]
        keep = jnp.where(core == 0, first, second)
        send = jnp.where(core == 0, second, first)
        if tail:
            keep = jnp.concatenate([keep, *tail], axis=1)
            send = jnp.concatenate([send, *tail], axis=1)
        return (keep.astype(F32) + core_swap(send).astype(F32)).astype(BF16)

    def scatter_chips(both):
        total = take(both, chip).astype(F32)
        for shift in range(1, chips):
            total = total + chip_swap(take(both, chip ^ shift), shift).astype(F32)
        return total

    def scatter_node(partial):
        return scatter_chips(scatter_core(partial))

    def ring(block):
        return lax.ppermute(block, "local", [(s, (s + 1) % n_local) for s in range(n_local)])

    def reduce_local(partial):
        return lax.psum_scatter(partial, "local", scatter_dimension=0, tiled=True).astype(F32)

    def gather_local(block):
        return lax.all_gather(block, "local", axis=0, tiled=True)

    def up_partial(values):
        widened = values.astype(F32)
        squares = jnp.sum((widened * widened).reshape(values.shape[0], -1, LANES), axis=1)
        product = dot((widened * gains).astype(BF16), up_weight, ((1,), (0,)))
        return jnp.concatenate([product.astype(BF16), squares.astype(BF16)], axis=1)

    def finish_pre(total):
        mean = jnp.sum(total[:, hidden_units:], axis=-1, keepdims=True) / features
        factor = lax.rsqrt(mean + epsilon)
        return total[:, :hidden_units] * factor, factor

    first = exchange(
        jnp.concatenate([tokens, cotangent, jnp.broadcast_to(gain, (PAD, cols))], axis=0)
    )
    up_weight = dequant_rows(up_q, up_scale)
    down_weight = dequant_cols(down_q, down_scale)
    first, up_weight, down_weight = lax.optimization_barrier((first, up_weight, down_weight))
    x_home, g_home, gain_rows = first[:rows], first[rows : 2 * rows], first[2 * rows :]
    gains = order(gain_rows, core_swap(gain_rows))[:1].astype(F32)
    gains_home = gain_rows[:1].astype(F32)

    x_mine = gather_chips(x_home)
    g_mine = gather_chips(after(g_home, x_mine))
    partial = after(up_partial(gather_core(x_mine)), g_mine)
    total = reduce_local(partial)
    g = gather_core(after(g_mine, partial))
    slope_part = dot(g, down_weight, ((1,), (1,))).astype(BF16)
    moving = take(slope_part, (z - 1) % n_local)
    moving = ring(moving).astype(F32) + take(slope_part, (z - 2) % n_local).astype(F32)
    moving = moving.astype(BF16)
    total = after(total, moving)
    hidden_own = jax.nn.silu(finish_pre(total)[0]).astype(BF16)

    hidden_1 = gather_local(hidden_own)
    moving = after(moving, hidden_own)
    for step in range(3, n_local + 1):
        moving = ring(moving).astype(F32) + take(slope_part, (z - step) % n_local).astype(F32)
        moving = moving.astype(BF16)
    slope = put(jnp.zeros((rows * n_local, hidden_units), BF16), moving, z)
    hidden_1 = after(hidden_1, moving)
    update = scatter_node(dot(hidden_1, down_weight, ((1,), (0,))).astype(BF16))
    x1_home = (x_home.astype(F32) + update).astype(BF16)
    moving = ring(moving)
    slope = put(slope, moving, (z - 1) % n_local)

    x = after(gather_node(x1_home), moving)
    partial = up_partial(x)
    total = reduce_local(partial)
    moving = after(moving, partial)
    for step in range(2, n_local):
        moving = ring(moving)
        slope = put(slope, moving, (z - step) % n_local)
    total = after(total, moving)
    pre, factor = finish_pre(total)
    packed = gather_local(jnp.concatenate([pre.astype(BF16)] + split_pair(factor), axis=1))

    pre = packed[:, :hidden_units].astype(F32)
    sigma = jax.nn.sigmoid(pre)
    hidden_2 = (pre * sigma).astype(BF16)
    update = dot(hidden_2, down_weight, ((1,), (0,))).astype(BF16)
    slope = after(slope, update).astype(F32)
    pre_grad = slope * sigma * (1.0 + pre * (1.0 - sigma))
    inner = jnp.sum(pre_grad * pre, axis=-1, keepdims=True)
    normed_grad = dot(pre_grad.astype(BF16), up_weight, ((1,), (1,))).astype(BF16)
    update = scatter_core(update)
    both = after(scatter_core(normed_grad, split_pair(inner)), update)
    x2_home = (x1_home.astype(F32) + scatter_chips(update)).astype(BF16)
    result = exchange(x2_home)
    total = scatter_chips(both)
    factor = join_pair(take(packed[:, hidden_units:], chip))
    inner = join_pair(total[:, cols:]) / (features * factor)
    back = factor * (total[:, :cols] * gains_home) - x1_home.astype(F32) * (factor**3 * inner)
    grad_home = (g_home.astype(F32) + back).astype(BF16)
    mine = gather_chips(after(grad_home, x2_home))
    below = gather_core(after(mine, result))
    grad_down = dot(
        jnp.concatenate([hidden_1, hidden_2], axis=0),
        jnp.concatenate([below, g], axis=0),
        ((0,), (0,)),
    ).astype(BF16)
    return (result, grad_down)


def solution(mesh):
    n_node, n_local = mesh.shape["node"], mesh.shape["local"]

    def per_device(*arrays):
        return body(n_node, n_local, *arrays)

    in_specs = (
        P("local", "node"),
        P("local", "node"),
        P(None, "node"),
        P("local", "node"),
        P("local", "node"),
        P("node", "local"),
        P("node", "local"),
    )
    out_specs = (P("local", "node"), P("node", "local"))
    return jax.shard_map(
        per_device, mesh=mesh, in_specs=in_specs, out_specs=out_specs, check_vma=False
    )
```

time: 369 us -> 373 us (1.011)
  waiting for transfers between devices: 255 us -> 263 us
  starting transfers between devices: 39.8 us -> 33.2 us
    ppermute x12 -> x6, waiting for transfers between devices: 198 us -> 96.9 us  [ring(): lax.ppermute(block, 'local', [(s, (s + 1) % n_local) for s in range(n_loc...]
    reduce_scatter x1 -> x2, waiting for transfers between devices: 0.02 us -> 55.4 us  [reduce_local(): lax.psum_scatter(partial, 'local', scatter_dimension=0, tiled=True)]
    all_gather x1 -> x2, waiting for transfers between devices: 0.02 us -> 51.2 us  [gather_local(): return lax.all_gather(block, 'local', axis=0, tiled=True)]
    ppermute x3 -> x2, waiting for transfers between devices: 23.7 us -> 16.2 us  [exchange(): return lax.ppermute(block, ('node', 'local'), swap)]
    ppermute x8, waiting for transfers between devices: 4.79 us -> 10.1 us  [core_swap(): return lax.ppermute(block, 'node', [(n, n ^ 1) for n in range(n_node)])]
    ppermute x21, waiting for transfers between devices: 28.6 us -> 32.8 us  [chip_swap(): lax.ppermute(block, 'node', [(n, n ^ 2 * shift) for n in range(n_node)])]
    ppermute x3 -> x2, starting transfers between devices: 8.01 us -> 5.52 us  [exchange(): return lax.ppermute(block, ('node', 'local'), swap)]
  transfers between devices with their start and end apart: 46 -> 41, of which waited for: 29 -> 33; matrix products, arithmetic and copies ran while one was open for 9% -> 7% of each run, Pallas kernels for 0% -> 0%
where the time goes in v6:
time: 373 us; the launch traced here: 372 us
  waiting for transfers between devices  263 us (71%)
  starting transfers between devices  33.2 us (9%)
  matrix products  28.7 us (8%)
  other arithmetic  24.5 us (7%)
  between operations  14.6 us (4%)
  local copies, waits for them, and re-layouts  8.59 us (2%)
    ppermute x6, waiting for transfers between devices, ring(): lax.ppermute(block, 'local', [(s, (s + 1) % n_local) for s in range(n_loc...  96.9 us
    reduce_scatter x2, waiting for transfers between devices, reduce_local(): lax.psum_scatter(partial, 'local', scatter_dimension=0, tiled=True)  55.4 us
    all_gather x2, waiting for transfers between devices, gather_local(): return lax.all_gather(block, 'local', axis=0, tiled=True)  51.2 us
    ppermute x21, waiting for transfers between devices, chip_swap(): lax.ppermute(block, 'node', [(n, n ^ 2 * shift) for n in range(n_node)])  32.8 us
    dot_general x7, matrix products, dot(): lax.dot_general(left, right, (dims, ((), ())), preferred_element_type=F32)  28.7 us
    ppermute x21, starting transfers between devices, chip_swap(): lax.ppermute(block, 'node', [(n, n ^ 2 * shift) for n in range(n_node)])  23.9 us
    ppermute x2, waiting for transfers between devices, exchange(): return lax.ppermute(block, ('node', 'local'), swap)  16.2 us
    ppermute x8, waiting for transfers between devices, core_swap(): return lax.ppermute(block, 'node', [(n, n ^ 1) for n in range(n_node)])  10.1 us
  transfers between devices with their start and end apart: 41, of which 33 were waited for; matrix products, arithmetic and copies ran while one was open for 7% of the time, Pallas kernels for 0%

profile of v6, /device:TPU:2, one launch (start us, length us, event | category | flops | bytes accessed | tf_op | source)
XLA Modules:
  0.0 372.2 jit_solution(2376273594044650125)
XLA Ops:
  8.9 3.5 collective-permute-start
  13.3 2.0 mul.125
  15.4 3.7 %fusion = bf16[1792,1024]{1,0:T(8,128)(2,1)} fusion(f32[224,8,8,128]{3,2,1,0:T(8,128)S(1)} %bitcast.118, bf16[1792,1024]{1,0:T(8,128)(2,1)S(1)} %copy-done), kind=kLoop, calls=%fused_computation.1 | loop fusion | flops 5505024 | bytes 14680064 | tf_op jit(solution)/shard_map/convert_element_type | solution.py:23
  19.2 4.5 %fusion.1 = bf16[1024,1792]{1,0:T(8,128)(2,1)} fusion(bf16[1024,1792]{1,0:T(8,128)(2,1)} %param.10, f32[8,1792]{1,0:T(8,128)S(1)} %convert_element_type.274), kind=kLoop, calls=%fused_computation.3 | loop fusion | flops 5505024 | bytes 7397376 | tf_op jit(solution)/shard_map/convert_element_type | solution.py:17
  23.7 8.3 %collective-permute-done = bf16[272,512]{1,0:T(8,128)(2,1)S(1)} collective-permute-done((bf16[272,512]{1,0:T(8,128)(2,1)S(1)}, bf16[272,512]{1,0:T(8,128)(2,1)S(1)}, u32[]{:S(2)}, u32[]{:S(2)}) %collective-permute-start) | collective-permute-done | bytes 278560 | tf_op jit(solution)/shard_map/ppermute | solution.py:61
  32.2 3.4 collective-permute-start.3
  39.7 1.7 collective-permute-start.6
  43.4 2.5 collective-permute-done.6
  45.8 4.0 %collective-permute-done.7 = bf16[128,512]{1,0:T(8,128)(2,1)S(1)} collective-permute-done((bf16[128,512]{1,0:T(8,128)(2,1)S(1)}, bf16[128,512]{1,0:T(8,128)(2,1)S(1)}, u32[]{:S(2)}, u32[]{:S(2)}) %collective-permute-start.7) | collective-permute-done | bytes 131104 | tf_op jit(solution)/shard_map/ppermute | solution.py:67
  51.5 4.1 %convolution_convert_fusion.3 = bf16[512,1792]{1,0:T(8,128)(2,1)S(1)} fusion(bf16[1024,1792]{1,0:T(8,128)(2,1)} %fusion.1, bf16[512,512]{1,0:T(8,128)(2,1)S(1)} %collective-permute-done.4, bf16[512,512]{1,0:T(8,128)(2,1)S(1)} %bitcast.134, f32[1024]{0:T(1024)S(1)} %bitcast.141, pred[]{:T(512)S(6)} %eq.11), kind=kOutput, calls=%fused_computation.21 | convolution fusion | flops 1886257152 | bytes 6557697 | tf_op jit(solution)/shard_map/dot_general | solution.py:27
  57.2 1.9 collective-permute-done.9
  59.4 4.5 %convolution_convert_fusion.2 = bf16[512,1792]{1,0:T(8,128)(2,1)S(1)} fusion(bf16[512,1024]{1,0:T(8,128)(2,1)S(1)} %maximum_select_fusion.3, bf16[1792,1024]{1,0:T(8,128)(2,1)} %fusion), kind=kOutput, calls=%fused_computation.20 | convolution fusion | flops 1879965696 | bytes 6553600 | tf_op jit(solution)/shard_map/dot_general | solution.py:27
  64.1 24.7 %collective-permute-done.10 = bf16[128,1792]{1,0:T(8,128)(2,1)S(1)} collective-permute-done((bf16[128,1792]{1,0:T(8,128)(2,1)S(1)}, bf16[128,1792]{1,0:T(8,128)(2,1)S(1)}, u32[]{:S(2)}, u32[]{:S(2)}) %collective-permute-start.10) | collective-permute-done | bytes 458784 | tf_op jit(solution)/shard_map/ppermute | solution.py:122
  88.9 20.0 %reduce-scatter.3.cloned.1.call-done = bf16[128,1920]{1,0:T(8,128)(2,1)} async-done(((bf16[512,1920]{1,0:T(8,128)(2,1)}), bf16[128,1920]{1,0:T(8,128)(2,1)}) %reduce-scatter.3.cloned.1.call-update) | async-done | bytes 491536 | tf_op jit(solution)/shard_map/reduce_scatter | solution.py:125
  112.0 16.8 %collective-permute-done.11 = bf16[128,1792]{1,0:T(8,128)(2,1)S(1)} collective-permute-done((bf16[128,1792]{1,0:T(8,128)(2,1)S(1)}, bf16[128,1792]{1,0:T(8,128)(2,1)S(1)}, u32[]{:S(2)}, u32[]{:S(2)}) %collective-permute-start.11) | collective-permute-done | bytes 458784 | tf_op jit(solution)/shard_map/ppermute | solution.py:122
  129.0 1.7 collective-permute-start.12
  130.7 21.9 %collective-permute-done.12 = bf16[128,1792]{1,0:T(8,128)(2,1)S(1)} collective-permute-done((bf16[128,1792]{1,0:T(8,128)(2,1)S(1)}, bf16[128,1792]{1,0:T(8,128)(2,1)S(1)}, u32[]{:S(2)}, u32[]{:S(2)}) %collective-permute-start.12) | collective-permute-done | bytes 458784 | tf_op jit(solution)/shard_map/ppermute | solution.py:122
  153.8 11.3 %all-gather.3.cloned.1.call-done = bf16[512,1792]{1,0:T(8,128)(2,1)} async-done(((bf16[128,1792]{1,0:T(8,128)(2,1)}), bf16[512,1792]{1,0:T(8,128)(2,1)}) %all-gather.3.cloned.1.call-update) | async-done | bytes 1835024 | tf_op jit(solution)/shard_map/all_gather | solution.py:128
  165.1 4.7 %convolution_convert_fusion.5 = bf16[512,1024]{1,0:T(8,128)(2,1)S(1)} fusion(bf16[512,1792]{1,0:T(8,128)(2,1)} %all-gather.3.cloned.1.call-done, bf16[1792,1024]{1,0:T(8,128)(2,1)} %fusion), kind=kOutput, calls=%fused_computation.38 | convolution fusion | flops 1879572480 | bytes 6553600 | tf_op jit(solution)/shard_map/dot_general | solution.py:27
  170.0 1.9 collective-permute-done.13
  172.1 1.5 collective-permute-start.16
  175.6 3.8 %collective-permute-done.16 = bf16[128,512]{1,0:T(8,128)(2,1)S(1)} collective-permute-done((bf16[128,512]{1,0:T(8,128)(2,1)S(1)}, bf16[128,512]{1,0:T(8,128)(2,1)S(1)}, u32[]{:S(2)}, u32[]{:S(2)}) %collective-permute-start.16) | collective-permute-done | bytes 131104 | tf_op jit(solution)/shard_map/ppermute | solution.py:67
  179.4 2.0 collective-permute-done.15
  183.7 1.5 collective-permute-start.19
  185.2 2.9 collective-permute-done.17
  188.0 2.1 collective-permute-done.18
  190.3 1.8 collective-permute-done.20
  192.5 12.5 %collective-permute-done.21 = bf16[128,1792]{1,0:T(8,128)(2,1)S(1)} collective-permute-done((bf16[128,1792]{1,0:T(8,128)(2,1)S(1)}, bf16[128,1792]{1,0:T(8,128)(2,1)S(1)}, u32[]{:S(2)}, u32[]{:S(2)}) %collective-permute-start.21) | collective-permute-done | bytes 458784 | tf_op jit(solution)/shard_map/ppermute | solution.py:122
  205.3 2.1 convolution_convert_fusion.1
  210.0 21.0 %collective-permute-done.22 = bf16[128,1792]{1,0:T(8,128)(2,1)S(1)} collective-permute-done((bf16[128,1792]{1,0:T(8,128)(2,1)S(1)}, bf16[128,1792]{1,0:T(8,128)(2,1)S(1)}, u32[]{:S(2)}, u32[]{:S(2)}) %collective-permute-start.22) | collective-permute-done | bytes 458784 | tf_op jit(solution)/shard_map/ppermute | solution.py:122
  231.0 35.4 %reduce-scatter.5.cloned.1.call-done = bf16[128,1920]{1,0:T(8,128)(2,1)} async-done(((bf16[512,1920]{1,0:T(8,128)(2,1)}), bf16[128,1920]{1,0:T(8,128)(2,1)}) %reduce-scatter.5.cloned.1.call-update) | async-done | bytes 491536 | tf_op jit(solution)/shard_map/reduce_scatter | solution.py:125
  271.0 39.9 %all-gather.5.cloned.1.call-done = bf16[512,1920]{1,0:T(8,128)(2,1)} async-done(((bf16[128,1920]{1,0:T(8,128)(2,1)}), bf16[512,1920]{1,0:T(8,128)(2,1)}) %all-gather.5.cloned.1.call-update) | async-done | bytes 1966096 | tf_op jit(solution)/shard_map/all_gather | solution.py:128
  310.9 4.8 %convolution_convert_fusion.4 = bf16[512,1024]{1,0:T(8,128)(2,1)S(1)} fusion(bf16[1792,1024]{1,0:T(8,128)(2,1)} %fusion, bf16[512,1920]{1,0:T(8,128)(2,1)} %all-gather.5.cloned.1.call-done), kind=kOutput, calls=%fused_computation.37 | convolution fusion | flops 1885077504 | bytes 6553600 | tf_op jit(solution)/shard_map/dot_general | solution.py:27
  315.8 2.9 fusion.19
  318.9 2.1 fusion.8
  322.1 1.5 collective-permute-done.29
  323.9 1.5 collective-permute-start.32
  327.6 1.5 collective-permute-start.27
  329.6 2.3 collective-permute-done.32
  332.5 3.0 collective-permute-done.31
  335.8 2.5 collective-permute-done.27
  338.3 2.2 collective-permute-done.26
  342.8 1.5 collective-permute-start.35
  344.3 2.1 collective-permute-start.28
  347.2 2.0 collective-permute-done.34
  349.3 7.9 %collective-permute-done.28 = bf16[128,512]{1,0:T(8,128)(2,1)S(1)} collective-permute-done((bf16[128,512]{1,0:T(8,128)(2,1)S(1)}, bf16[128,512]{1,0:T(8,128)(2,1)S(1)}, u32[]{:S(2)}, u32[]{:S(2)}) %collective-permute-start.28) | collective-permute-done | bytes 131104 | tf_op jit(solution)/shard_map/ppermute | solution.py:61
  357.2 1.9 collective-permute-done.36
  359.5 5.5 %convolution_convert_fusion = bf16[1792,1024]{1,0:T(8,128)(2,1)} fusion(bf16[512,1792]{1,0:T(8,128)(2,1)S(1)} %get-tuple-element.45, bf16[512,1792]{1,0:T(8,128)(2,1)S(1)} %copy-done.9, bf16[512,1024]{1,0:T(8,128)(2,1)S(1)} %copy-done.6, bf16[512,1024]{1,0:T(8,128)(2,1)S(1)} %maximum_select_fusion.5), kind=kOutput, calls=%fused_computation.8 | convolution fusion | flops 3771465728 | bytes 9437184 | tf_op jit(solution)/shard_map/dot_general | solution.py:27
  (149 shorter events, 38.7 us)
Async XLA Ops:
  7.2 101.7 %reduce-scatter.3.cloned.1.call-start = ((), (), s32[]{:S(2)}) async-start(), calls=%async_computation.2 | async-start | bytes 2457600 | tf_op jit(solution)/shard_map/reduce_scatter | solution.py:125
  8.9 23.1 %collective-permute-start = (bf16[272,512]{1,0:T(8,128)(2,1)S(1)}, bf16[272,512]{1,0:T(8,128)(2,1)S(1)}, u32[]{:S(2)}, u32[]{:S(2)}) collective-permute-start(bf16[272,512]{1,0:T(8,128)(2,1)S(1)} %pad_maximum_fusion.6), channel_id=1, source_target_pairs={{0,0},{1,8},{2,16},{3,24},{4,4},{5,12},{6,20},{7,28},{8,1},{9,9},{... | collective-permute-start | bytes 835592 | tf_op jit(solution)/shard_map/ppermute | solution.py:61
  32.1 5.9 %collective-permute-start.1 = (bf16[128,512]{1,0:T(8,128)(2,1)S(1)}, bf16[128,512]{1,0:T(8,128)(2,1)S(1)}, u32[]{:S(2)}, u32[]{:S(2)}) collective-permute-start(bf16[128,512]{1,0:T(8,128)(2,1)S(1)} %get-tuple-element.58), channel_id=1, source_target_pairs={{0,8},{4,12},{8,0},{12,4},{16,24},{20,28},{24,16},{28,20},{1,9},{5... | collective-permute-start | bytes 393224 | tf_op jit(solution)/shard_map/ppermute | solution.py:67
  32.1 7.3 %collective-permute-start.2 = (bf16[128,512]{1,0:T(8,128)(2,1)S(1)}, bf16[128,512]{1,0:T(8,128)(2,1)S(1)}, u32[]{:S(2)}, u32[]{:S(2)}) collective-permute-start(bf16[128,512]{1,0:T(8,128)(2,1)S(1)} %get-tuple-element.58), channel_id=1, source_target_pairs={{0,16},{4,20},{8,24},{12,28},{16,0},{20,4},{24,8},{28,12},{1,17},{... | collective-permute-start | bytes 393224 | tf_op jit(solution)/shard_map/ppermute | solution.py:67
  32.2 7.3 %collective-permute-start.3 = (bf16[128,512]{1,0:T(8,128)(2,1)S(1)}, bf16[128,512]{1,0:T(8,128)(2,1)S(1)}, u32[]{:S(2)}, u32[]{:S(2)}) collective-permute-start(bf16[128,512]{1,0:T(8,128)(2,1)S(1)} %get-tuple-element.58), channel_id=1, source_target_pairs={{0,24},{4,28},{8,16},{12,20},{16,8},{20,12},{24,0},{28,4},{1,25},{... | collective-permute-start | bytes 393224 | tf_op jit(solution)/shard_map/ppermute | solution.py:67
  35.6 1.2 collective-permute-start.5
  39.7 10.2 %collective-permute-start.4 = (bf16[512,512]{1,0:T(8,128)(2,1)S(1)}, bf16[512,512]{1,0:T(8,128)(2,1)S(1)}, u32[]{:S(2)}, u32[]{:S(2)}) collective-permute-start(bf16[512,512]{1,0:T(8,128)(2,1)S(1)} %bitcast.133), channel_id=1, source_target_pairs={{0,4},{4,0},{8,12},{12,8},{16,20},{20,16},{24,28},{28,24},{1,5},{5... | collective-permute-start | bytes 1572872 | tf_op jit(solution)/shard_map/ppermute | solution.py:64
  39.7 6.1 %collective-permute-start.6 = (bf16[128,512]{1,0:T(8,128)(2,1)S(1)}, bf16[128,512]{1,0:T(8,128)(2,1)S(1)}, u32[]{:S(2)}, u32[]{:S(2)}) collective-permute-start(bf16[128,512]{1,0:T(8,128)(2,1)S(1)} %get-tuple-element.20), channel_id=1, source_target_pairs={{0,8},{4,12},{8,0},{12,4},{16,24},{20,28},{24,16},{28,20},{1,9},{5... | collective-permute-start | bytes 393224 | tf_op jit(solution)/shard_map/ppermute | solution.py:67
  41.5 8.4 %collective-permute-start.7 = (bf16[128,512]{1,0:T(8,128)(2,1)S(1)}, bf16[128,512]{1,0:T(8,128)(2,1)S(1)}, u32[]{:S(2)}, u32[]{:S(2)}) collective-permute-start(bf16[128,512]{1,0:T(8,128)(2,1)S(1)} %get-tuple-element.20), channel_id=1, source_target_pairs={{0,16},{4,20},{8,24},{12,28},{16,0},{20,4},{24,8},{28,12},{1,17},{... | collective-permute-start | bytes 393224 | tf_op jit(solution)/shard_map/ppermute | solution.py:67
  42.3 7.5 %collective-permute-start.8 = (bf16[128,512]{1,0:T(8,128)(2,1)S(1)}, bf16[128,512]{1,0:T(8,128)(2,1)S(1)}, u32[]{:S(2)}, u32[]{:S(2)}) collective-permute-start(bf16[128,512]{1,0:T(8,128)(2,1)S(1)} %get-tuple-element.20), channel_id=1, source_target_pairs={{0,24},{4,28},{8,16},{12,20},{16,8},{20,12},{24,0},{28,4},{1,25},{... | collective-permute-start | bytes 393224 | tf_op jit(solution)/shard_map/ppermute | solution.py:67
  57.1 108.1 %all-gather.3.cloned.1.call-start = ((), (), s32[]{:S(2)}) async-start(), calls=%async_computation.3 | async-start | bytes 2293760 | tf_op jit(solution)/shard_map/all_gather | solution.py:128
  57.1 2.0 collective-permute-start.9
  64.0 64.9 %copy-start.4 = (bf16[512,1792]{1,0:T(8,128)(2,1)}, bf16[512,1792]{1,0:T(8,128)(2,1)S(1)}, u32[]{:S(2)}) copy-start(bf16[512,1792]{1,0:T(8,128)(2,1)S(1)} %convolution_convert_fusion.2) | copy-start | bytes 5505028
  64.0 24.8 %collective-permute-start.10 = (bf16[128,1792]{1,0:T(8,128)(2,1)S(1)}, bf16[128,1792]{1,0:T(8,128)(2,1)S(1)}, u32[]{:S(2)}, u32[]{:S(2)}) collective-permute-start(bf16[128,1792]{1,0:T(8,128)(2,1)S(1)} %dynamic-slice_bitcast_fusion), channel_id=1, source_target_pairs={{0,1},{1,2},{2,3},{3,0},{4,5},{5,6},{6,7},{7,4},{8,9},{9,10},{10,1... | collective-permute-start | bytes 1376264 | tf_op jit(solution)/shard_map/ppermute | solution.py:122
  111.2 155.1 %reduce-scatter.5.cloned.1.call-start = ((), (), s32[]{:S(2)}) async-start(), calls=%async_computation.4 | async-start | bytes 2457600 | tf_op jit(solution)/shard_map/reduce_scatter | solution.py:125
  111.3 17.6 %collective-permute-start.11 = (bf16[128,1792]{1,0:T(8,128)(2,1)S(1)}, bf16[128,1792]{1,0:T(8,128)(2,1)S(1)}, u32[]{:S(2)}, u32[]{:S(2)}) collective-permute-start(bf16[128,1792]{1,0:T(8,128)(2,1)S(1)} %fusion.33), channel_id=1, source_target_pairs={{0,1},{1,2},{2,3},{3,0},{4,5},{5,6},{6,7},{7,4},{8,9},{9,10},{10,1... | collective-permute-start | bytes 1376264 | tf_op jit(solution)/shard_map/ppermute | solution.py:122
  129.0 23.6 %collective-permute-start.12 = (bf16[128,1792]{1,0:T(8,128)(2,1)S(1)}, bf16[128,1792]{1,0:T(8,128)(2,1)S(1)}, u32[]{:S(2)}, u32[]{:S(2)}) collective-permute-start(bf16[128,1792]{1,0:T(8,128)(2,1)S(1)} %fusion.32), channel_id=1, source_target_pairs={{0,1},{1,2},{2,3},{3,0},{4,5},{5,6},{6,7},{7,4},{8,9},{9,10},{10,1... | collective-permute-start | bytes 1376264 | tf_op jit(solution)/shard_map/ppermute | solution.py:122
  169.9 2.0 collective-permute-start.13
  172.1 7.3 %collective-permute-start.16 = (bf16[128,512]{1,0:T(8,128)(2,1)S(1)}, bf16[128,512]{1,0:T(8,128)(2,1)S(1)}, u32[]{:S(2)}, u32[]{:S(2)}) collective-permute-start(bf16[128,512]{1,0:T(8,128)(2,1)S(1)} %get-tuple-element.55), channel_id=1, source_target_pairs={{0,24},{4,28},{8,16},{12,20},{16,8},{20,12},{24,0},{28,4},{1,25},{... | collective-permute-start | bytes 393224 | tf_op jit(solution)/shard_map/ppermute | solution.py:67
  173.6 7.8 %collective-permute-start.15 = (bf16[128,512]{1,0:T(8,128)(2,1)S(1)}, bf16[128,512]{1,0:T(8,128)(2,1)S(1)}, u32[]{:S(2)}, u32[]{:S(2)}) collective-permute-start(bf16[128,512]{1,0:T(8,128)(2,1)S(1)} %get-tuple-element.56), channel_id=1, source_target_pairs={{0,16},{4,20},{8,24},{12,28},{16,0},{20,4},{24,8},{28,12},{1,17},{... | collective-permute-start | bytes 393224 | tf_op jit(solution)/shard_map/ppermute | solution.py:67
  174.2 7.3 %collective-permute-start.14 = (bf16[128,512]{1,0:T(8,128)(2,1)S(1)}, bf16[128,512]{1,0:T(8,128)(2,1)S(1)}, u32[]{:S(2)}, u32[]{:S(2)}) collective-permute-start(bf16[128,512]{1,0:T(8,128)(2,1)S(1)} %get-tuple-element.54), channel_id=1, source_target_pairs={{0,8},{4,12},{8,0},{12,4},{16,24},{20,28},{24,16},{28,20},{1,9},{5... | collective-permute-start | bytes 393224 | tf_op jit(solution)/shard_map/ppermute | solution.py:67
  181.6 6.4 %collective-permute-start.17 = (bf16[128,512]{1,0:T(8,128)(2,1)S(1)}, bf16[128,512]{1,0:T(8,128)(2,1)S(1)}, u32[]{:S(2)}, u32[]{:S(2)}) collective-permute-start(bf16[128,512]{1,0:T(8,128)(2,1)S(1)} %get-tuple-element.43), channel_id=1, source_target_pairs={{0,8},{4,12},{8,0},{12,4},{16,24},{20,28},{24,16},{28,20},{1,9},{5... | collective-permute-start | bytes 393224 | tf_op jit(solution)/shard_map/ppermute | solution.py:67
  182.2 7.9 %collective-permute-start.18 = (bf16[128,512]{1,0:T(8,128)(2,1)S(1)}, bf16[128,512]{1,0:T(8,128)(2,1)S(1)}, u32[]{:S(2)}, u32[]{:S(2)}) collective-permute-start(bf16[128,512]{1,0:T(8,128)(2,1)S(1)} %get-tuple-element.43), channel_id=1, source_target_pairs={{0,16},{4,20},{8,24},{12,28},{16,0},{20,4},{24,8},{28,12},{1,17},{... | collective-permute-start | bytes 393224 | tf_op jit(solution)/shard_map/ppermute | solution.py:67
  183.7 6.5 %collective-permute-start.19 = (bf16[128,512]{1,0:T(8,128)(2,1)S(1)}, bf16[128,512]{1,0:T(8,128)(2,1)S(1)}, u32[]{:S(2)}, u32[]{:S(2)}) collective-permute-start(bf16[128,512]{1,0:T(8,128)(2,1)S(1)} %get-tuple-element.43), channel_id=1, source_target_pairs={{0,24},{4,28},{8,16},{12,20},{16,8},{20,12},{24,0},{28,4},{1,25},{... | collective-permute-start | bytes 393224 | tf_op jit(solution)/shard_map/ppermute | solution.py:67
  190.2 2.0 collective-permute-start.20
  190.3 14.7 %collective-permute-start.21 = (bf16[128,1792]{1,0:T(8,128)(2,1)S(1)}, bf16[128,1792]{1,0:T(8,128)(2,1)S(1)}, u32[]{:S(2)}, u32[]{:S(2)}) collective-permute-start(bf16[128,1792]{1,0:T(8,128)(2,1)S(1)} %get-tuple-element.39), channel_id=1, source_target_pairs={{0,1},{1,2},{2,3},{3,0},{4,5},{5,6},{6,7},{7,4},{8,9},{9,10},{10,1... | collective-permute-start | bytes 1376264 | tf_op jit(solution)/shard_map/ppermute | solution.py:122
  192.2 13.1 %copy-start.1 = (bf16[1024,1792]{1,0:T(8,128)(2,1)S(1)}, bf16[1024,1792]{1,0:T(8,128)(2,1)}, u32[]{:S(2)}) copy-start(bf16[1024,1792]{1,0:T(8,128)(2,1)} %fusion.1) | copy-start | bytes 11010052
  209.8 101.0 %all-gather.5.cloned.1.call-start = ((), (), s32[]{:S(2)}) async-start(), calls=%async_computation.5 | async-start | bytes 2457600 | tf_op jit(solution)/shard_map/all_gather | solution.py:128
  209.9 21.1 %collective-permute-start.22 = (bf16[128,1792]{1,0:T(8,128)(2,1)S(1)}, bf16[128,1792]{1,0:T(8,128)(2,1)S(1)}, u32[]{:S(2)}, u32[]{:S(2)}) collective-permute-start(bf16[128,1792]{1,0:T(8,128)(2,1)S(1)} %collective-permute-done.21), channel_id=1, source_target_pairs={{0,1},{1,2},{2,3},{3,0},{4,5},{5,6},{6,7},{7,4},{8,9},{9,10},{10,1... | collective-permute-start | bytes 1376264 | tf_op jit(solution)/shard_map/ppermute | solution.py:122
  231.0 36.6 %copy-start.7 = (bf16[128,1792]{1,0:T(8,128)(2,1)}, bf16[128,1792]{1,0:T(8,128)(2,1)S(1)}, u32[]{:S(2)}) copy-start(bf16[128,1792]{1,0:T(8,128)(2,1)S(1)} %collective-permute-done.22) | copy-start | bytes 1376260
  231.0 36.5 %collective-permute-start.23 = (bf16[128,1792]{1,0:T(8,128)(2,1)S(1)}, bf16[128,1792]{1,0:T(8,128)(2,1)}, u32[]{:S(2)}, u32[]{:S(2)}) collective-permute-start(bf16[128,1792]{1,0:T(8,128)(2,1)S(1)} %collective-permute-done.22), channel_id=1, source_target_pairs={{0,1},{1,2},{2,3},{3,0},{4,5},{5,6},{6,7},{7,4},{8,9},{9,10},{10,1... | collective-permute-start | bytes 1376264 | tf_op jit(solution)/shard_map/ppermute | solution.py:122
  310.9 4.9 %copy-start.3 = (bf16[512,1920]{1,0:T(8,128)(2,1)S(1)}, bf16[512,1920]{1,0:T(8,128)(2,1)}, u32[]{:S(2)}) copy-start(bf16[512,1920]{1,0:T(8,128)(2,1)} %all-gather.5.cloned.1.call-done) | copy-start | bytes 5898244
  318.8 3.1 collective-permute-start.24
  321.4 2.3 collective-permute-start.29
  321.9 5.6 %slice-start = ((bf16[512,1920]{1,0:T(8,128)(2,1)}), bf16[512,128]{1,0:T(8,128)(2,1)S(1)}, s32[]{:S(2)}) async-start(bf16[512,1920]{1,0:T(8,128)(2,1)} %all-gather.5.cloned.1.call-done), calls=%async_computation.6 | async-start | bytes 262144 | tf_op jit(solution)/shard_map/slice | solution.py:199
  323.9 8.0 %collective-permute-start.32 = (bf16[128,640]{1,0:T(8,128)(2,1)S(1)}, bf16[128,640]{1,0:T(8,128)(2,1)S(1)}, u32[]{:S(2)}, u32[]{:S(2)}) collective-permute-start(bf16[128,640]{1,0:T(8,128)(2,1)S(1)} %get-tuple-element.49), channel_id=1, source_target_pairs={{0,24},{4,28},{8,16},{12,20},{16,8},{20,12},{24,0},{28,4},{1,25},{... | collective-permute-start | bytes 491528 | tf_op jit(solution)/shard_map/ppermute | solution.py:67
  325.5 10.1 %collective-permute-start.31 = (bf16[128,640]{1,0:T(8,128)(2,1)S(1)}, bf16[128,640]{1,0:T(8,128)(2,1)S(1)}, u32[]{:S(2)}, u32[]{:S(2)}) collective-permute-start(bf16[128,640]{1,0:T(8,128)(2,1)S(1)} %get-tuple-element.50), channel_id=1, source_target_pairs={{0,16},{4,20},{8,24},{12,28},{16,0},{20,4},{24,8},{28,12},{1,17},{... | collective-permute-start | bytes 491528 | tf_op jit(solution)/shard_map/ppermute | solution.py:67
  326.0 9.5 %collective-permute-start.30 = (bf16[128,640]{1,0:T(8,128)(2,1)S(1)}, bf16[128,640]{1,0:T(8,128)(2,1)S(1)}, u32[]{:S(2)}, u32[]{:S(2)}) collective-permute-start(bf16[128,640]{1,0:T(8,128)(2,1)S(1)} %get-tuple-element.48), channel_id=1, source_target_pairs={{0,8},{4,12},{8,0},{12,4},{16,24},{20,28},{24,16},{28,20},{1,9},{5... | collective-permute-start | bytes 491528 | tf_op jit(solution)/shard_map/ppermute | solution.py:67
  327.6 10.8 %collective-permute-start.27 = (bf16[128,512]{1,0:T(8,128)(2,1)S(1)}, bf16[128,512]{1,0:T(8,128)(2,1)S(1)}, u32[]{:S(2)}, u32[]{:S(2)}) collective-permute-start(bf16[128,512]{1,0:T(8,128)(2,1)S(1)} %get-tuple-element.52), channel_id=1, source_target_pairs={{0,24},{4,28},{8,16},{12,20},{16,8},{20,12},{24,0},{28,4},{1,25},{... | collective-permute-start | bytes 393224 | tf_op jit(solution)/shard_map/ppermute | solution.py:67
  329.1 11.4 %collective-permute-start.26 = (bf16[128,512]{1,0:T(8,128)(2,1)S(1)}, bf16[128,512]{1,0:T(8,128)(2,1)S(1)}, u32[]{:S(2)}, u32[]{:S(2)}) collective-permute-start(bf16[128,512]{1,0:T(8,128)(2,1)S(1)} %get-tuple-element.53), channel_id=1, source_target_pairs={{0,16},{4,20},{8,24},{12,28},{16,0},{20,4},{24,8},{28,12},{1,17},{... | collective-permute-start | bytes 393224 | tf_op jit(solution)/shard_map/ppermute | solution.py:67
  332.0 8.6 %collective-permute-start.25 = (bf16[128,512]{1,0:T(8,128)(2,1)S(1)}, bf16[128,512]{1,0:T(8,128)(2,1)S(1)}, u32[]{:S(2)}, u32[]{:S(2)}) collective-permute-start(bf16[128,512]{1,0:T(8,128)(2,1)S(1)} %get-tuple-element.51), channel_id=1, source_target_pairs={{0,8},{4,12},{8,0},{12,4},{16,24},{20,28},{24,16},{28,20},{1,9},{5... | collective-permute-start | bytes 393224 | tf_op jit(solution)/shard_map/ppermute | solution.py:67
  340.8 18.7 %copy-start.6 = (bf16[512,1024]{1,0:T(8,128)(2,1)S(1)}, bf16[512,1024]{1,0:T(8,128)(2,1)}, u32[]{:S(2)}) copy-start(bf16[512,1024]{1,0:T(8,128)(2,1)} %copy-done.5) | copy-start | bytes 3145732
  340.8 18.7 %copy-start.9 = (bf16[512,1792]{1,0:T(8,128)(2,1)S(1)}, bf16[512,1792]{1,0:T(8,128)(2,1)}, u32[]{:S(2)}) copy-start(bf16[512,1792]{1,0:T(8,128)(2,1)} %all-gather.3.cloned.1.call-done) | copy-start | bytes 5505028
  340.8 6.4 %collective-permute-start.33 = (bf16[128,512]{1,0:T(8,128)(2,1)S(1)}, bf16[128,512]{1,0:T(8,128)(2,1)S(1)}, u32[]{:S(2)}, u32[]{:S(2)}) collective-permute-start(bf16[128,512]{1,0:T(8,128)(2,1)S(1)} %get-tuple-element.32), channel_id=1, source_target_pairs={{0,8},{4,12},{8,0},{12,4},{16,24},{20,28},{24,16},{28,20},{1,9},{5... | collective-permute-start | bytes 393224 | tf_op jit(solution)/shard_map/ppermute | solution.py:67
  341.4 7.9 %collective-permute-start.34 = (bf16[128,512]{1,0:T(8,128)(2,1)S(1)}, bf16[128,512]{1,0:T(8,128)(2,1)S(1)}, u32[]{:S(2)}, u32[]{:S(2)}) collective-permute-start(bf16[128,512]{1,0:T(8,128)(2,1)S(1)} %get-tuple-element.32), channel_id=1, source_target_pairs={{0,16},{4,20},{8,24},{12,28},{16,0},{20,4},{24,8},{28,12},{1,17},{... | collective-permute-start | bytes 393224 | tf_op jit(solution)/shard_map/ppermute | solution.py:67
  342.8 6.5 %collective-permute-start.35 = (bf16[128,512]{1,0:T(8,128)(2,1)S(1)}, bf16[128,512]{1,0:T(8,128)(2,1)S(1)}, u32[]{:S(2)}, u32[]{:S(2)}) collective-permute-start(bf16[128,512]{1,0:T(8,128)(2,1)S(1)} %get-tuple-element.32), channel_id=1, source_target_pairs={{0,24},{4,28},{8,16},{12,20},{16,8},{20,12},{24,0},{28,4},{1,25},{... | collective-permute-start | bytes 393224 | tf_op jit(solution)/shard_map/ppermute | solution.py:67
  344.3 12.9 %collective-permute-start.28 = (bf16[128,512]{1,0:T(8,128)(2,1)S(1)}, bf16[128,512]{1,0:T(8,128)(2,1)S(1)}, u32[]{:S(2)}, u32[]{:S(2)}) collective-permute-start(bf16[128,512]{1,0:T(8,128)(2,1)S(1)} %get-tuple-element.60), channel_id=1, source_target_pairs={{0,0},{1,8},{2,16},{3,24},{4,4},{5,12},{6,20},{7,28},{8,1},{9,9},{... | collective-permute-start | bytes 393224 | tf_op jit(solution)/shard_map/ppermute | solution.py:61
  357.2 1.9 collective-permute-start.36
  (4 other events, 15.3 us)
Sparse Core Ops, SparseCore 0:
  57.2 51.6 reduce-scatter.2
  111.4 53.7 all-gather.2
  210.0 56.3 reduce-scatter.4
  268.9 41.8 all-gather.4
